TPU v7x, 512 devices: a whole 4x4x16 slice. The times are simulated.
512 devices in a mesh: layer: 16 (over y_hi, x, core), tensor: 32 (over y_lo, z).
Axes of the slice: x: 4, y: 4 (y_hi: 2, y_lo: 2; y = y_hi * 2 + y_lo), z: 16, core: 2. Of those that a mesh axis runs over, the one named last changes fastest.
Arguments:
- factor_rows: bfloat16 [57344, 3584], P(('layer', 'tensor')), parts along dimension 0, may hold values from -0.07 to 4.6
- basis: bfloat16 [57344, 1024], P(('layer', 'tensor')), parts along dimension 0, may hold values from -6 to 6
Outputs:
- new_basis: bfloat16 [57344, 1024], P(('layer', 'tensor')), parts along dimension 0
There are 16 independent parts, one for each index of `layer`. A program takes and returns all parts, laid end to end along the dimension named above; each array names one. Nothing has to cross between parts.
All inputs are finite; a program needn't handle non-finite values.
Results may differ from a plain program's by a relative error of at most 0.0057.
Values may be sent and summed in bfloat16 or wider, within the bound.
No kernel may reach another device: no remote copies, remote signals or barrier semaphores. Data moves between devices by JAX's collectives and lax.ppermute only.
A program may use at most 64 MiB of HBM per device.

v0:
```python
import math

import jax
import jax.numpy as jnp
from jax import lax
from jax.sharding import PartitionSpec as P


def body(factor_rows, basis):
    order = factor_rows.shape[1]
    columns = basis.shape[1]
    product = jnp.dot(
        factor_rows,
        lax.all_gather(basis, "tensor", axis=0, tiled=True),
        preferred_element_type=jnp.float32,
    )
    power = product.astype(jnp.bfloat16)
    wide = power.astype(jnp.float32)
    total = lax.psum(jnp.sum(wide * wide), "tensor")
    share = lax.psum_scatter(
        jnp.dot(power.T, power, preferred_element_type=jnp.float32),
        "tensor",
        scatter_dimension=0,
        tiled=True,
    )
    gram = lax.all_gather(share, "tensor", axis=0, tiled=True)
    ratio = columns / (3.0 * total)
    scaled = (gram * ratio).astype(jnp.bfloat16)
    first_full = jnp.dot(power, scaled, preferred_element_type=jnp.float32)
    first = first_full.astype(jnp.bfloat16)
    second = jnp.dot(first, scaled, preferred_element_type=jnp.float32)
    mixed = 3.4445 * wide - 4.775 * first_full + 2.0315 * second
    return (math.sqrt(order) * jnp.sqrt(ratio) * mixed).astype(jnp.bfloat16)


def solution(mesh):
    placed = (P(("layer", "tensor"), None), P(("layer", "tensor"), None))
    return jax.shard_map(
        body, mesh=mesh, in_specs=placed, out_specs=P(("layer", "tensor"), None), check_vma=False
    )
```

profile of v0, /device:TPU:6, one launch (start us, length us, event | category | flops | bytes accessed | tf_op | source)
XLA Modules:
  0.0 448.1 jit_solution(10136700760659152953)
XLA Ops:
  6.5 0.0 copy-start
  6.5 0.0 all-gather.3.cloned.1.call-start
  6.5 0.7 all-gather.3.cloned.1.call-update
  7.3 0.0 reduce-scatter.2.cloned.1.call-start
  7.3 151.9 %all-gather.3.cloned.1.call-done = bf16[3584,1024]{1,0:T(8,128)(2,1)} async-done(((bf16[112,1024]{1,0:T(8,128)(2,1)}), bf16[3584,1024]{1,0:T(8,128)(2,1)}) %all-gather.3.cloned.1.call-update) | async-done | bytes 7340048 | tf_op jit(solution)/shard_map/all_gather | solution.py:14
  159.2 0.0 copy-done
  159.2 4.8 %fusion.4 = (f32[]{:T(128)}, bf16[112,1024]{1,0:T(8,128)(2,1)S(1)}) fusion(bf16[112,3584]{1,0:T(8,128)(2,1)S(1)} %copy-done, bf16[3584,1024]{1,0:T(8,128)(2,1)} %all-gather.3.cloned.1.call-done), kind=kOutput, calls=%fused_computation.9 | convolution fusion | flops 822542336 | bytes 8372228 | tf_op jit(solution)/shard_map/dot_general | solution.py:12
  164.1 2.7 fusion.7
  166.8 0.0 reduce-scatter.2.cloned.1.call-update
  166.8 0.0 all-gather.5.cloned.1.call-start
  166.8 138.0 %reduce-scatter.2.cloned.1.call-done = f32[32,1024]{1,0:T(8,128)} async-done(((f32[1024,1024]{1,0:T(8,128)}), f32[32,1024]{1,0:T(8,128)}) %reduce-scatter.2.cloned.1.call-update) | async-done | bytes 131088 | tf_op jit(solution)/shard_map/reduce_scatter | solution.py:20
  304.8 0.0 all-gather.5.cloned.1.call-update
  304.9 62.0 %psum.7 = f32[]{:T(128)} all-reduce(f32[]{:T(128)} %get-tuple-element.5), channel_id=1, replica_groups=mesh['layer'=16,'tensor'=32] {'tensor'}, use_global_device_ids=true, to_apply=%region_1.0 | all-reduce | flops 1 | bytes 8 | tf_op jit(solution)/shard_map/psum | solution.py:19
  367.6 69.2 %all-gather.5.cloned.1.call-done = f32[1024,1024]{1,0:T(8,128)} async-done(((f32[32,1024]{1,0:T(8,128)}), f32[1024,1024]{1,0:T(8,128)}) %all-gather.5.cloned.1.call-update) | async-done | bytes 4194320 | tf_op jit(solution)/shard_map/all_gather | solution.py:26
  436.8 0.0 copy-start.1
  436.8 2.8 fusion.3
  439.6 0.7 copy-done.1
  440.3 1.3 fusion.2
Async XLA Ops:
  6.5 152.7 %copy-start = (bf16[112,3584]{1,0:T(8,128)(2,1)S(1)}, bf16[112,3584]{1,0:T(8,128)(2,1)}, u32[]{:S(2)}) copy-start(bf16[112,3584]{1,0:T(8,128)(2,1)} %param.2) | copy-start | bytes 2408452
  6.5 152.7 %all-gather.3.cloned.1.call-start = ((), (), s32[]{:S(2)}) async-start(), calls=%async_computation.1 | async-start | bytes 7569408 | tf_op jit(solution)/shard_map/all_gather | solution.py:14
  7.3 297.6 %reduce-scatter.2.cloned.1.call-start = ((), (), s32[]{:S(2)}) async-start(), calls=%async_computation.2 | async-start | bytes 4325376 | tf_op jit(solution)/shard_map/reduce_scatter | solution.py:20
  166.8 270.0 %all-gather.5.cloned.1.call-start = ((), (), s32[]{:S(2)}) async-start(), calls=%async_computation.3 | async-start | bytes 4325376 | tf_op jit(solution)/shard_map/all_gather | solution.py:26
  436.8 3.4 copy-start.1
Sparse Core Ops, SparseCore 0:
  9.4 149.7 all-gather.2
  166.9 137.8 reduce-scatter.1
  306.9 129.8 all-gather.4
where the time goes:
time: 448 us
  waiting for transfers between devices  360 us (80%)
  blocking collectives  62 us (14%)
  between operations  13.9 us (3%)
  matrix products  11.6 us (3%)
    all_gather x1, waiting for transfers between devices, body(): lax.all_gather(basis, 'tensor', axis=0, tiled=True)  152 us
    reduce_scatter x1, waiting for transfers between devices, body(): lax.psum_scatter(jnp.dot(power.T, power, preferred_element_type=jnp.float...  138 us
    all_gather x1, waiting for transfers between devices, body(): gram = lax.all_gather(share, 'tensor', axis=0, tiled=True)  69.2 us
    psum x1, blocking collectives, body(): total = lax.psum(jnp.sum(wide * wide), 'tensor')  62 us
  transfers between devices with their start and end apart: 3, of which 3 were waited for; matrix products, arithmetic and copies ran while one was open for 0% of the time, Pallas kernels for 0%

commit v1 on v0

v1 whole, which is shorter than its diff:
```python
import math

import jax
import jax.numpy as jnp
from jax import lax
from jax.sharding import PartitionSpec as P

AXIS = "tensor"
Y = 2
Z = 16
CUBE = 4

ACROSS = [(y * Z + z, (1 - y) * Z + z) for y in range(Y) for z in range(Z)]
PAIRS = [[z, Z + z] for z in range(Z)]
NEAR = [[y * Z + c * CUBE + i for i in range(CUBE)] for y in range(Y) for c in range(Z // CUBE)]
FAR = [[y * Z + c * CUBE + i for c in range(Z // CUBE)] for y in range(Y) for i in range(CUBE)]


def shift(step):
    return [(y * Z + z, y * Z + (z + step) % Z) for y in range(Y) for z in range(Z)]


def ring(block):
    up, down = [], []
    a = b = block
    for step in range(Z // 2):
        a = lax.ppermute(a, AXIS, shift(1))
        up.append(a)
        if step < Z // 2 - 1:
            b = lax.ppermute(b, AXIS, shift(-1))
            down.append(b)
    return up, down


def place(full, block, z):
    return lax.dynamic_update_slice(full, block[:, None], (0, z % Z, 0, 0))


def body(factor_rows, basis):
    rows, order = factor_rows.shape
    columns = basis.shape[1]
    half = columns // 2
    chunk = columns // 4
    position = lax.axis_index(AXIS)
    y, z = position // Z, position % Z

    halves = basis.reshape(rows, 2, half)
    mine = lax.dynamic_index_in_dim(halves, y, 1, keepdims=False)
    other = lax.dynamic_index_in_dim(halves, 1 - y, 1, keepdims=False)
    other = lax.ppermute(other, AXIS, ACROSS)
    first_row = y == 0
    block = jnp.stack([jnp.where(first_row, mine, other), jnp.where(first_row, other, mine)])
    far_rows = lax.ppermute(factor_rows, AXIS, ACROSS)

    up, down = ring(block)
    full = jnp.zeros((2, Z, rows, half), basis.dtype)
    full = place(full, block, z)
    for step, part in enumerate(up):
        full = place(full, part, z - step - 1 + Z)
    for step, part in enumerate(down):
        full = place(full, part, z + step + 1)
    full = full.reshape(order, half)

    near = jnp.dot(factor_rows, full, preferred_element_type=jnp.float32).astype(jnp.bfloat16)
    far = jnp.dot(far_rows, full, preferred_element_type=jnp.float32).astype(jnp.bfloat16)
    tile = jnp.concatenate([jnp.where(first_row, near, far), jnp.where(first_row, far, near)], 0)
    both = lax.all_gather(tile, AXIS, axis=0, axis_index_groups=PAIRS)
    plane = jnp.concatenate([both[0], both[1]], 1)
    power = lax.dynamic_slice_in_dim(plane, y * rows, rows, 0)

    def cross(a, b):
        return lax.dot_general(a, b, (((0,), (0,)), ((), ())), preferred_element_type=jnp.float32)

    square = cross(tile, tile).astype(jnp.bfloat16)
    strip = cross(both[1], lax.dynamic_slice_in_dim(both[0], y * chunk, chunk, 1)).astype(jnp.bfloat16)
    blocks = jnp.concatenate(
        [square[:chunk, :chunk], square[:chunk, chunk:], square[chunk:, chunk:], strip], 0
    )
    parts = lax.all_to_all(
        blocks.reshape(CUBE, -1, chunk), AXIS, 0, 0, axis_index_groups=NEAR
    )
    part = jnp.sum(parts.astype(jnp.float32), 0).astype(jnp.bfloat16)
    parts = lax.all_gather(part, AXIS, axis=0, axis_index_groups=FAR)
    part = jnp.sum(parts.astype(jnp.float32), 0).astype(jnp.bfloat16)
    other_part = lax.ppermute(part, AXIS, ACROSS)
    own_blocks = lax.all_gather(part, AXIS, axis=0, axis_index_groups=NEAR).reshape(5, chunk, chunk)
    other_blocks = lax.all_gather(other_part, AXIS, axis=0, axis_index_groups=NEAR).reshape(5, chunk, chunk)
    low = jnp.where(first_row, own_blocks, other_blocks)
    high = jnp.where(first_row, other_blocks, own_blocks)

    gram = jnp.block(
        [
            [low[0], low[1], low[3].T, low[4].T],
            [low[1].T, low[2], high[3].T, high[4].T],
            [low[3], high[3], high[0], high[1]],
            [low[4], high[4], high[1].T, high[2]],
        ]
    )
    eye = jnp.eye(chunk, dtype=jnp.bool_)
    diagonal = sum(jnp.where(eye, d.astype(jnp.float32), 0.0) for d in (low[0], low[2], high[0], high[2]))
    ratio = columns / (3.0 * jnp.sum(diagonal))
    first_full = jnp.dot(power, gram, preferred_element_type=jnp.float32) * ratio
    first = first_full.astype(jnp.bfloat16)
    second = jnp.dot(first, gram, preferred_element_type=jnp.float32) * ratio
    mixed = 3.4445 * power.astype(jnp.float32) - 4.775 * first_full + 2.0315 * second
    return (math.sqrt(order) * jnp.sqrt(ratio) * mixed).astype(jnp.bfloat16)


def solution(mesh):
    placed = (P(("layer", "tensor"), None), P(("layer", "tensor"), None))
    return jax.shard_map(
        body, mesh=mesh, in_specs=placed, out_specs=P(("layer", "tensor"), None), check_vma=False
    )
```

time: 448 us -> 213 us (0.48)
  waiting for transfers between devices: 360 us -> 44.7 us
  starting transfers between devices: 0.08 us -> 70.6 us
  other arithmetic: 0 us -> 20.6 us
  between operations: 13.9 us -> 1.65 us
  matrix products: 11.6 us -> 4.31 us
    all_gather x2 -> x0, waiting for transfers between devices: 221 us -> none  [the longest x1 152 us: body(): lax.all_gather(basis, 'tensor', axis=0, tiled=True)]
    reduce_scatter x1 -> x0, waiting for transfers between devices: 138 us -> none  [body(): lax.psum_scatter(jnp.dot(power.T, power, preferred_element_type=jnp.float...]
    ppermute x0 -> x18, starting transfers between devices: none -> 67.1 us  [the longest x7 41 us: ring(): b = lax.ppermute(b, AXIS, shift(-1))]
    all_gather x0 -> x4, blocking collectives: none -> 66.2 us  [the longest x1 28.2 us: body(): parts = lax.all_gather(part, AXIS, axis=0, axis_index_groups=FAR)]
    psum x1 -> x0, blocking collectives: 62 us -> none  [body(): total = lax.psum(jnp.sum(wide * wide), 'tensor')]
    ppermute x0 -> x18, waiting for transfers between devices: none -> 26 us  [the longest x8 22.6 us: ring(): a = lax.ppermute(a, AXIS, shift(1))]
    concatenate x0 -> x4, other arithmetic: none -> 19.3 us  [the longest x2 18.4 us: body(): jnp.block([[low[0], low[1], low[3].T, low[4].T], [low[1].T, low[2], high[...]
    all_to_all x0 -> x1, waiting for transfers between devices: none -> 18.7 us  [body(): lax.all_to_all(blocks.reshape(CUBE, -1, chunk), AXIS, 0, 0, axis_index_gr...]
  transfers between devices with their start and end apart: 3 -> 19, of which waited for: 3 -> 10; matrix products, arithmetic and copies ran while one was open for 0% -> 0% of each run, Pallas kernels for 0% -> 0%
where the time goes in v1:
time: 213 us; the launch traced here: 212 us
  starting transfers between devices  70.6 us (33%)
  blocking collectives  66.2 us (31%)
  waiting for transfers between devices  44.7 us (21%)
  other arithmetic  20.6 us (10%)
  matrix products  4.31 us (2%)
  local copies, waits for them, and re-layouts  3.59 us (2%)
    ppermute x7, starting transfers between devices, ring(): b = lax.ppermute(b, AXIS, shift(-1))  41 us
    all_gather x1, blocking collectives, body(): parts = lax.all_gather(part, AXIS, axis=0, axis_index_groups=FAR)  28.2 us
    ppermute x8, waiting for transfers between devices, ring(): a = lax.ppermute(a, AXIS, shift(1))  22.6 us
    all_to_all x1, waiting for transfers between devices, body(): lax.all_to_all(blocks.reshape(CUBE, -1, chunk), AXIS, 0, 0, axis_index_gr...  18.7 us
    concatenate x2, other arithmetic, body(): jnp.block([[low[0], low[1], low[3].T, low[4].T], [low[1].T, low[2], high[...  18.4 us
    ppermute x8, starting transfers between devices, ring(): a = lax.ppermute(a, AXIS, shift(1))  17.2 us
    all_gather x1, blocking collectives, body(): lax.all_gather(part, AXIS, axis=0, axis_index_groups=NEAR)  16 us
    all_gather x1, blocking collectives, body(): lax.all_gather(other_part, AXIS, axis=0, axis_index_groups=NEAR)  15.3 us
  transfers between devices with their start and end apart: 19, of which 10 were waited for; matrix products, arithmetic and copies ran while one was open for 0% of the time, Pallas kernels for 0%

profile of v1, /device:TPU:6, one launch (start us, length us, event | category | flops | bytes accessed | tf_op | source)
XLA Modules:
  0.0 211.7 jit_solution(357767960563718753)
XLA Ops:
  0.0 1.1 reshape.16
  1.1 0.5 constant_dynamic-slice_fusion.1
  1.6 3.5 %collective-permute-start = (bf16[112,512]{1,0:T(8,128)(2,1)S(1)}, bf16[112,512]{1,0:T(8,128)(2,1)S(1)}, u32[]{:S(2)}, u32[]{:S(2)}) collective-permute-start(bf16[112,512]{1,0:T(8,128)(2,1)S(1)} %bitcast.107), channel_id=1, source_target_pairs={{0,16},{1,17},{2,18},{3,19},{4,20},{5,21},{6,22},{7,23},{8,24},{9,... | collective-permute-start | bytes 344072 | tf_op jit(solution)/shard_map/ppermute | solution.py:50
  5.1 3.3 %collective-permute-done = bf16[112,512]{1,0:T(8,128)(2,1)S(1)} collective-permute-done((bf16[112,512]{1,0:T(8,128)(2,1)S(1)}, bf16[112,512]{1,0:T(8,128)(2,1)S(1)}, u32[]{:S(2)}, u32[]{:S(2)}) %collective-permute-start) | collective-permute-done | bytes 114720 | tf_op jit(solution)/shard_map/ppermute | solution.py:50
  8.5 3.8 %collective-permute-start.1 = (bf16[2,112,512]{2,1,0:T(8,128)(2,1)S(1)}, bf16[2,112,512]{2,1,0:T(8,128)(2,1)S(1)}, u32[]{:S(2)}, u32[]{:S(2)}) collective-permute-start(bf16[2,112,512]{2,1,0:T(8,128)(2,1)S(1)} %pad_maximum_fusion.2), channel_id=1, source_target_pairs={{0,1},{1,2},{2,3},{3,4},{4,5},{5,6},{6,7},{7,8},{8,9},{9,10},{10,1... | collective-permute-start | bytes 688136 | tf_op jit(solution)/shard_map/ppermute | solution.py:27
  12.3 9.5 %collective-permute-start.9 = (bf16[2,112,512]{2,1,0:T(8,128)(2,1)S(1)}, bf16[2,112,512]{2,1,0:T(8,128)(2,1)S(1)}, u32[]{:S(2)}, u32[]{:S(2)}) collective-permute-start(bf16[2,112,512]{2,1,0:T(8,128)(2,1)S(1)} %pad_maximum_fusion.2), channel_id=1, source_target_pairs={{0,15},{1,0},{2,1},{3,2},{4,3},{5,4},{6,5},{7,6},{8,7},{9,8},{10,9... | collective-permute-start | bytes 688136 | tf_op jit(solution)/shard_map/ppermute | solution.py:30
  21.8 3.5 %collective-permute-start.16 = (bf16[112,3584]{1,0:T(8,128)(2,1)}, bf16[112,3584]{1,0:T(8,128)(2,1)S(1)}, u32[]{:S(2)}, u32[]{:S(2)}) collective-permute-start(bf16[112,3584]{1,0:T(8,128)(2,1)} %param.2), channel_id=1, source_target_pairs={{0,16},{1,17},{2,18},{3,19},{4,20},{5,21},{6,22},{7,23},{8,24},{9,... | collective-permute-start | bytes 2408456 | tf_op jit(solution)/shard_map/ppermute | solution.py:53
  25.7 0.4 broadcast_in_dim.58
  26.1 0.0 collective-permute-done.1
  26.1 1.9 collective-permute-start.2
  28.0 0.0 collective-permute-done.9
  28.1 5.1 %collective-permute-start.10 = (bf16[2,112,512]{2,1,0:T(8,128)(2,1)S(1)}, bf16[2,112,512]{2,1,0:T(8,128)(2,1)S(1)}, u32[]{:S(2)}, u32[]{:S(2)}) collective-permute-start(bf16[2,112,512]{2,1,0:T(8,128)(2,1)S(1)} %collective-permute-done.9), channel_id=1, source_target_pairs={{0,15},{1,0},{2,1},{3,2},{4,3},{5,4},{6,5},{7,6},{8,7},{9,8},{10,9... | collective-permute-start | bytes 688136 | tf_op jit(solution)/shard_map/ppermute | solution.py:30
  33.2 2.0 collective-permute-done.2
  35.2 1.9 collective-permute-start.3
  37.2 5.1 %collective-permute-start.11 = (bf16[2,112,512]{2,1,0:T(8,128)(2,1)S(1)}, bf16[2,112,512]{2,1,0:T(8,128)(2,1)S(1)}, u32[]{:S(2)}, u32[]{:S(2)}) collective-permute-start(bf16[2,112,512]{2,1,0:T(8,128)(2,1)S(1)} %collective-permute-done.10), channel_id=1, source_target_pairs={{0,15},{1,0},{2,1},{3,2},{4,3},{5,4},{6,5},{7,6},{8,7},{9,8},{10,9... | collective-permute-start | bytes 688136 | tf_op jit(solution)/shard_map/ppermute | solution.py:30
  42.3 2.0 collective-permute-done.3
  44.4 1.9 collective-permute-start.4
  46.3 0.0 collective-permute-done.11
  46.3 5.1 %collective-permute-start.12 = (bf16[2,112,512]{2,1,0:T(8,128)(2,1)S(1)}, bf16[2,112,512]{2,1,0:T(8,128)(2,1)S(1)}, u32[]{:S(2)}, u32[]{:S(2)}) collective-permute-start(bf16[2,112,512]{2,1,0:T(8,128)(2,1)S(1)} %collective-permute-done.11), channel_id=1, source_target_pairs={{0,15},{1,0},{2,1},{3,2},{4,3},{5,4},{6,5},{7,6},{8,7},{9,8},{10,9... | collective-permute-start | bytes 688136 | tf_op jit(solution)/shard_map/ppermute | solution.py:30
  51.5 2.0 collective-permute-done.4
  53.5 1.9 collective-permute-start.5
  55.4 0.0 collective-permute-done.12
  55.4 5.1 %collective-permute-start.13 = (bf16[2,112,512]{2,1,0:T(8,128)(2,1)S(1)}, bf16[2,112,512]{2,1,0:T(8,128)(2,1)S(1)}, u32[]{:S(2)}, u32[]{:S(2)}) collective-permute-start(bf16[2,112,512]{2,1,0:T(8,128)(2,1)S(1)} %collective-permute-done.12), channel_id=1, source_target_pairs={{0,15},{1,0},{2,1},{3,2},{4,3},{5,4},{6,5},{7,6},{8,7},{9,8},{10,9... | collective-permute-start | bytes 688136 | tf_op jit(solution)/shard_map/ppermute | solution.py:30
  60.6 2.5 %collective-permute-done.5 = bf16[2,112,512]{2,1,0:T(8,128)(2,1)S(1)} collective-permute-done((bf16[2,112,512]{2,1,0:T(8,128)(2,1)S(1)}, bf16[2,112,512]{2,1,0:T(8,128)(2,1)S(1)}, u32[]{:S(2)}, u32[]{:S(2)}) %collective-permute-start.5) | collective-permute-done | bytes 229408 | tf_op jit(solution)/shard_map/ppermute | solution.py:27
  63.0 1.9 collective-permute-start.6
  65.0 5.4 %collective-permute-start.14 = (bf16[2,112,512]{2,1,0:T(8,128)(2,1)S(1)}, bf16[2,112,512]{2,1,0:T(8,128)(2,1)S(1)}, u32[]{:S(2)}, u32[]{:S(2)}) collective-permute-start(bf16[2,112,512]{2,1,0:T(8,128)(2,1)S(1)} %collective-permute-done.13), channel_id=1, source_target_pairs={{0,15},{1,0},{2,1},{3,2},{4,3},{5,4},{6,5},{7,6},{8,7},{9,8},{10,9... | collective-permute-start | bytes 688136 | tf_op jit(solution)/shard_map/ppermute | solution.py:30
  70.4 3.3 %collective-permute-done.6 = bf16[2,112,512]{2,1,0:T(8,128)(2,1)S(1)} collective-permute-done((bf16[2,112,512]{2,1,0:T(8,128)(2,1)S(1)}, bf16[2,112,512]{2,1,0:T(8,128)(2,1)S(1)}, u32[]{:S(2)}, u32[]{:S(2)}) %collective-permute-start.6) | collective-permute-done | bytes 229408 | tf_op jit(solution)/shard_map/ppermute | solution.py:27
  73.7 1.9 collective-permute-start.7
  75.7 0.2 collective-permute-done.14
  75.8 5.6 %collective-permute-start.15 = (bf16[2,112,512]{2,1,0:T(8,128)(2,1)S(1)}, bf16[2,112,512]{2,1,0:T(8,128)(2,1)S(1)}, u32[]{:S(2)}, u32[]{:S(2)}) collective-permute-start(bf16[2,112,512]{2,1,0:T(8,128)(2,1)S(1)} %collective-permute-done.14), channel_id=1, source_target_pairs={{0,15},{1,0},{2,1},{3,2},{4,3},{5,4},{6,5},{7,6},{8,7},{9,8},{10,9... | collective-permute-start | bytes 688136 | tf_op jit(solution)/shard_map/ppermute | solution.py:30
  81.4 3.6 %collective-permute-done.7 = bf16[2,112,512]{2,1,0:T(8,128)(2,1)S(1)} collective-permute-done((bf16[2,112,512]{2,1,0:T(8,128)(2,1)S(1)}, bf16[2,112,512]{2,1,0:T(8,128)(2,1)S(1)}, u32[]{:S(2)}, u32[]{:S(2)}) %collective-permute-start.7) | collective-permute-done | bytes 229408 | tf_op jit(solution)/shard_map/ppermute | solution.py:27
  85.0 1.9 collective-permute-start.8
  87.0 7.2 %collective-permute-done.8 = bf16[2,112,512]{2,1,0:T(8,128)(2,1)S(1)} collective-permute-done((bf16[2,112,512]{2,1,0:T(8,128)(2,1)S(1)}, bf16[2,112,512]{2,1,0:T(8,128)(2,1)S(1)}, u32[]{:S(2)}, u32[]{:S(2)}) %collective-permute-start.8) | collective-permute-done | bytes 229408 | tf_op jit(solution)/shard_map/ppermute | solution.py:27
  94.2 0.0 copy-start
  94.4 0.7 convolution_convert_fusion.2
  95.1 0.2 copy-done
  95.3 0.7 select_bitcast_fusion.1
  96.0 0.3 convolution_convert_fusion
  96.4 6.7 %all-gather = bf16[448,512]{1,0:T(8,128)(2,1)S(1)} all-gather(bf16[224,512]{1,0:T(8,128)(2,1)S(1)} %pad_maximum_fusion.3), channel_id=2, replica_groups={{0,16},{1,17},{2,18},{3,19},{4,20},{5,21},{6,22},{7,23},{8,24},{9,25},{..., dimensions={0}, use_global_device_ids=true | all-gather | bytes 688128 | tf_op jit(solution)/shard_map/all_gather | solution.py:67
  103.2 0.3 convolution_convert_fusion.1
  103.4 0.9 pad_maximum_fusion
  104.3 3.5 %all-to-all-start = ((bf16[4,320,256]{2,1,0:T(8,128)(2,1)}), bf16[4,320,256]{2,1,0:T(8,128)(2,1)S(1)}, u32[]{:S(2)}, u32[]{:S(2)}) async-start(bf16[4,320,256]{2,1,0:T(8,128)(2,1)} %bitcast.37), calls=%async_computation | async-start | bytes 1310720 | tf_op jit(solution)/shard_map/all_to_all | solution.py:79
  107.8 18.7 %all-to-all-done = bf16[4,320,256]{2,1,0:T(8,128)(2,1)S(1)} async-done(((bf16[4,320,256]{2,1,0:T(8,128)(2,1)}), bf16[4,320,256]{2,1,0:T(8,128)(2,1)S(1)}, u32[]{:S(2)}, u32[]{:S(2)}) %all-to-all-start) | async-done | bytes 655392 | tf_op jit(solution)/shard_map/all_to_all | solution.py:79
  126.5 0.1 reduce_sum.33
  126.6 28.2 %all-gather.1 = bf16[1280,256]{1,0:T(8,128)(2,1)S(1)} all-gather(bf16[320,256]{1,0:T(8,128)(2,1)S(1)} %reduce_sum.33), channel_id=3, replica_groups={{0,4,8,12},{1,5,9,13},{2,6,10,14},{3,7,11,15},{16,20,24,28},{17,21,25,2..., dimensions={0}, use_global_device_ids=true | all-gather | bytes 819200 | tf_op jit(solution)/shard_map/all_gather | solution.py:83
  154.8 0.1 reduce_sum.34
  154.9 1.9 collective-permute-start.17
  156.8 16.0 %all-gather.2 = bf16[1280,256]{1,0:T(8,128)(2,1)S(1)} all-gather(bf16[320,256]{1,0:T(8,128)(2,1)S(1)} %reduce_sum.34), channel_id=4, replica_groups={{0,1,2,3},{4,5,6,7},{8,9,10,11},{12,13,14,15},{16,17,18,19},{20,21,22,2..., dimensions={0}, use_global_device_ids=true | all-gather | bytes 819200 | tf_op jit(solution)/shard_map/all_gather | solution.py:86
  172.8 15.3 %all-gather.3 = bf16[1280,256]{1,0:T(8,128)(2,1)S(1)} all-gather(bf16[320,256]{1,0:T(8,128)(2,1)S(1)} %collective-permute-done.17), channel_id=5, replica_groups={{0,1,2,3},{4,5,6,7},{8,9,10,11},{12,13,14,15},{16,17,18,19},{20,21,22,2..., dimensions={0}, use_global_device_ids=true | all-gather | bytes 819200 | tf_op jit(solution)/shard_map/all_gather | solution.py:87
  188.1 0.1 broadcast_select_fusion.1
  188.2 0.3 slice_convert_fusion
  188.5 0.1 copy.68
  188.7 0.1 copy.79
  188.8 0.1 copy.80
  188.9 0.1 copy.81
  189.0 0.1 pad_maximum_fusion.1
  189.1 0.2 copy.75
  189.3 0.1 copy.72
  189.4 0.1 copy.74
  189.5 0.1 copy.82
  189.6 0.7 add_reduce_fusion
  191.0 18.3 %maximum_maximum_fusion = bf16[1024,1024]{0,1:T(8,128)(2,1)S(1)} fusion(bf16[256,256]{0,1:T(8,128)(2,1)S(1)} %copy.81, bf16[256,256]{0,1:T(8,128)(2,1)S(1)} %get-tuple-element.10, bf16[256,256]{0,1:T(8,128)(2,1)S(1)} %copy.74, bf16[256,256]{0,1:T(8,128)(2,1)S(1)} %copy.82, bf16[256,1024]{0,1:T(8,128)(2,1)S(1)} %copy.75, ...), kind=kLoop, calls=%fused_computation | loop fusion | flops 27262976 | bytes 4194304 | tf_op jit(solution)/shard_map/jit(block)/concatenate | solution.py:91
  209.3 0.8 convolution_multiply_fusion.1
  210.1 1.5 fusion.3
  (28 shorter events, 0.5 us)
Async XLA Ops:
  1.6 6.8 %collective-permute-start = (bf16[112,512]{1,0:T(8,128)(2,1)S(1)}, bf16[112,512]{1,0:T(8,128)(2,1)S(1)}, u32[]{:S(2)}, u32[]{:S(2)}) collective-permute-start(bf16[112,512]{1,0:T(8,128)(2,1)S(1)} %bitcast.107), channel_id=1, source_target_pairs={{0,16},{1,17},{2,18},{3,19},{4,20},{5,21},{6,22},{7,23},{8,24},{9,... | collective-permute-start | bytes 344072 | tf_op jit(solution)/shard_map/ppermute | solution.py:50
  8.5 17.6 %collective-permute-start.1 = (bf16[2,112,512]{2,1,0:T(8,128)(2,1)S(1)}, bf16[2,112,512]{2,1,0:T(8,128)(2,1)S(1)}, u32[]{:S(2)}, u32[]{:S(2)}) collective-permute-start(bf16[2,112,512]{2,1,0:T(8,128)(2,1)S(1)} %pad_maximum_fusion.2), channel_id=1, source_target_pairs={{0,1},{1,2},{2,3},{3,4},{4,5},{5,6},{6,7},{7,8},{8,9},{9,10},{10,1... | collective-permute-start | bytes 688136 | tf_op jit(solution)/shard_map/ppermute | solution.py:27
  12.3 15.7 %collective-permute-start.9 = (bf16[2,112,512]{2,1,0:T(8,128)(2,1)S(1)}, bf16[2,112,512]{2,1,0:T(8,128)(2,1)S(1)}, u32[]{:S(2)}, u32[]{:S(2)}) collective-permute-start(bf16[2,112,512]{2,1,0:T(8,128)(2,1)S(1)} %pad_maximum_fusion.2), channel_id=1, source_target_pairs={{0,15},{1,0},{2,1},{3,2},{4,3},{5,4},{6,5},{7,6},{8,7},{9,8},{10,9... | collective-permute-start | bytes 688136 | tf_op jit(solution)/shard_map/ppermute | solution.py:30
  21.8 72.6 %collective-permute-start.16 = (bf16[112,3584]{1,0:T(8,128)(2,1)}, bf16[112,3584]{1,0:T(8,128)(2,1)S(1)}, u32[]{:S(2)}, u32[]{:S(2)}) collective-permute-start(bf16[112,3584]{1,0:T(8,128)(2,1)} %param.2), channel_id=1, source_target_pairs={{0,16},{1,17},{2,18},{3,19},{4,20},{5,21},{6,22},{7,23},{8,24},{9,... | collective-permute-start | bytes 2408456 | tf_op jit(solution)/shard_map/ppermute | solution.py:53
  26.1 9.1 %collective-permute-start.2 = (bf16[2,112,512]{2,1,0:T(8,128)(2,1)S(1)}, bf16[2,112,512]{2,1,0:T(8,128)(2,1)S(1)}, u32[]{:S(2)}, u32[]{:S(2)}) collective-permute-start(bf16[2,112,512]{2,1,0:T(8,128)(2,1)S(1)} %collective-permute-done.1), channel_id=1, source_target_pairs={{0,1},{1,2},{2,3},{3,4},{4,5},{5,6},{6,7},{7,8},{8,9},{9,10},{10,1... | collective-permute-start | bytes 688136 | tf_op jit(solution)/shard_map/ppermute | solution.py:27
  28.1 9.1 %collective-permute-start.10 = (bf16[2,112,512]{2,1,0:T(8,128)(2,1)S(1)}, bf16[2,112,512]{2,1,0:T(8,128)(2,1)S(1)}, u32[]{:S(2)}, u32[]{:S(2)}) collective-permute-start(bf16[2,112,512]{2,1,0:T(8,128)(2,1)S(1)} %collective-permute-done.9), channel_id=1, source_target_pairs={{0,15},{1,0},{2,1},{3,2},{4,3},{5,4},{6,5},{7,6},{8,7},{9,8},{10,9... | collective-permute-start | bytes 688136 | tf_op jit(solution)/shard_map/ppermute | solution.py:30
  35.2 9.1 %collective-permute-start.3 = (bf16[2,112,512]{2,1,0:T(8,128)(2,1)S(1)}, bf16[2,112,512]{2,1,0:T(8,128)(2,1)S(1)}, u32[]{:S(2)}, u32[]{:S(2)}) collective-permute-start(bf16[2,112,512]{2,1,0:T(8,128)(2,1)S(1)} %collective-permute-done.2), channel_id=1, source_target_pairs={{0,1},{1,2},{2,3},{3,4},{4,5},{5,6},{6,7},{7,8},{8,9},{9,10},{10,1... | collective-permute-start | bytes 688136 | tf_op jit(solution)/shard_map/ppermute | solution.py:27
  37.2 9.1 %collective-permute-start.11 = (bf16[2,112,512]{2,1,0:T(8,128)(2,1)S(1)}, bf16[2,112,512]{2,1,0:T(8,128)(2,1)S(1)}, u32[]{:S(2)}, u32[]{:S(2)}) collective-permute-start(bf16[2,112,512]{2,1,0:T(8,128)(2,1)S(1)} %collective-permute-done.10), channel_id=1, source_target_pairs={{0,15},{1,0},{2,1},{3,2},{4,3},{5,4},{6,5},{7,6},{8,7},{9,8},{10,9... | collective-permute-start | bytes 688136 | tf_op jit(solution)/shard_map/ppermute | solution.py:30
  44.4 9.1 %collective-permute-start.4 = (bf16[2,112,512]{2,1,0:T(8,128)(2,1)S(1)}, bf16[2,112,512]{2,1,0:T(8,128)(2,1)S(1)}, u32[]{:S(2)}, u32[]{:S(2)}) collective-permute-start(bf16[2,112,512]{2,1,0:T(8,128)(2,1)S(1)} %collective-permute-done.3), channel_id=1, source_target_pairs={{0,1},{1,2},{2,3},{3,4},{4,5},{5,6},{6,7},{7,8},{8,9},{9,10},{10,1... | collective-permute-start | bytes 688136 | tf_op jit(solution)/shard_map/ppermute | solution.py:27
  46.3 9.1 %collective-permute-start.12 = (bf16[2,112,512]{2,1,0:T(8,128)(2,1)S(1)}, bf16[2,112,512]{2,1,0:T(8,128)(2,1)S(1)}, u32[]{:S(2)}, u32[]{:S(2)}) collective-permute-start(bf16[2,112,512]{2,1,0:T(8,128)(2,1)S(1)} %collective-permute-done.11), channel_id=1, source_target_pairs={{0,15},{1,0},{2,1},{3,2},{4,3},{5,4},{6,5},{7,6},{8,7},{9,8},{10,9... | collective-permute-start | bytes 688136 | tf_op jit(solution)/shard_map/ppermute | solution.py:30
  53.5 9.6 %collective-permute-start.5 = (bf16[2,112,512]{2,1,0:T(8,128)(2,1)S(1)}, bf16[2,112,512]{2,1,0:T(8,128)(2,1)S(1)}, u32[]{:S(2)}, u32[]{:S(2)}) collective-permute-start(bf16[2,112,512]{2,1,0:T(8,128)(2,1)S(1)} %collective-permute-done.4), channel_id=1, source_target_pairs={{0,1},{1,2},{2,3},{3,4},{4,5},{5,6},{6,7},{7,8},{8,9},{9,10},{10,1... | collective-permute-start | bytes 688136 | tf_op jit(solution)/shard_map/ppermute | solution.py:27
  55.4 9.5 %collective-permute-start.13 = (bf16[2,112,512]{2,1,0:T(8,128)(2,1)S(1)}, bf16[2,112,512]{2,1,0:T(8,128)(2,1)S(1)}, u32[]{:S(2)}, u32[]{:S(2)}) collective-permute-start(bf16[2,112,512]{2,1,0:T(8,128)(2,1)S(1)} %collective-permute-done.12), channel_id=1, source_target_pairs={{0,15},{1,0},{2,1},{3,2},{4,3},{5,4},{6,5},{7,6},{8,7},{9,8},{10,9... | collective-permute-start | bytes 688136 | tf_op jit(solution)/shard_map/ppermute | solution.py:30
  63.0 10.7 %collective-permute-start.6 = (bf16[2,112,512]{2,1,0:T(8,128)(2,1)S(1)}, bf16[2,112,512]{2,1,0:T(8,128)(2,1)S(1)}, u32[]{:S(2)}, u32[]{:S(2)}) collective-permute-start(bf16[2,112,512]{2,1,0:T(8,128)(2,1)S(1)} %collective-permute-done.5), channel_id=1, source_target_pairs={{0,1},{1,2},{2,3},{3,4},{4,5},{5,6},{6,7},{7,8},{8,9},{9,10},{10,1... | collective-permute-start | bytes 688136 | tf_op jit(solution)/shard_map/ppermute | solution.py:27
  65.0 10.9 %collective-permute-start.14 = (bf16[2,112,512]{2,1,0:T(8,128)(2,1)S(1)}, bf16[2,112,512]{2,1,0:T(8,128)(2,1)S(1)}, u32[]{:S(2)}, u32[]{:S(2)}) collective-permute-start(bf16[2,112,512]{2,1,0:T(8,128)(2,1)S(1)} %collective-permute-done.13), channel_id=1, source_target_pairs={{0,15},{1,0},{2,1},{3,2},{4,3},{5,4},{6,5},{7,6},{8,7},{9,8},{10,9... | collective-permute-start | bytes 688136 | tf_op jit(solution)/shard_map/ppermute | solution.py:30
  73.7 11.3 %collective-permute-start.7 = (bf16[2,112,512]{2,1,0:T(8,128)(2,1)S(1)}, bf16[2,112,512]{2,1,0:T(8,128)(2,1)S(1)}, u32[]{:S(2)}, u32[]{:S(2)}) collective-permute-start(bf16[2,112,512]{2,1,0:T(8,128)(2,1)S(1)} %collective-permute-done.6), channel_id=1, source_target_pairs={{0,1},{1,2},{2,3},{3,4},{4,5},{5,6},{6,7},{7,8},{8,9},{9,10},{10,1... | collective-permute-start | bytes 688136 | tf_op jit(solution)/shard_map/ppermute | solution.py:27
  75.8 18.5 %collective-permute-start.15 = (bf16[2,112,512]{2,1,0:T(8,128)(2,1)S(1)}, bf16[2,112,512]{2,1,0:T(8,128)(2,1)S(1)}, u32[]{:S(2)}, u32[]{:S(2)}) collective-permute-start(bf16[2,112,512]{2,1,0:T(8,128)(2,1)S(1)} %collective-permute-done.14), channel_id=1, source_target_pairs={{0,15},{1,0},{2,1},{3,2},{4,3},{5,4},{6,5},{7,6},{8,7},{9,8},{10,9... | collective-permute-start | bytes 688136 | tf_op jit(solution)/shard_map/ppermute | solution.py:30
  85.0 9.1 %collective-permute-start.8 = (bf16[2,112,512]{2,1,0:T(8,128)(2,1)S(1)}, bf16[2,112,512]{2,1,0:T(8,128)(2,1)S(1)}, u32[]{:S(2)}, u32[]{:S(2)}) collective-permute-start(bf16[2,112,512]{2,1,0:T(8,128)(2,1)S(1)} %collective-permute-done.7), channel_id=1, source_target_pairs={{0,1},{1,2},{2,3},{3,4},{4,5},{5,6},{6,7},{7,8},{8,9},{9,10},{10,1... | collective-permute-start | bytes 688136 | tf_op jit(solution)/shard_map/ppermute | solution.py:27
  94.2 1.1 copy-start
  104.3 22.2 %all-to-all-start = ((bf16[4,320,256]{2,1,0:T(8,128)(2,1)}), bf16[4,320,256]{2,1,0:T(8,128)(2,1)S(1)}, u32[]{:S(2)}, u32[]{:S(2)}) async-start(bf16[4,320,256]{2,1,0:T(8,128)(2,1)} %bitcast.37), calls=%async_computation | async-start | bytes 1310720 | tf_op jit(solution)/shard_map/all_to_all | solution.py:79
  154.9 17.9 %collective-permute-start.17 = (bf16[320,256]{1,0:T(8,128)(2,1)S(1)}, bf16[320,256]{1,0:T(8,128)(2,1)S(1)}, u32[]{:S(2)}, u32[]{:S(2)}) collective-permute-start(bf16[320,256]{1,0:T(8,128)(2,1)S(1)} %reduce_sum.34), channel_id=1, source_target_pairs={{0,16},{1,17},{2,18},{3,19},{4,20},{5,21},{6,22},{7,23},{8,24},{9,... | collective-permute-start | bytes 491528 | tf_op jit(solution)/shard_map/ppermute | solution.py:85

commit v2 on v1

--- a/solution.py
+++ b/solution.py
@@ -1,8 +1,11 @@
+import functools
 import math
 
 import jax
 import jax.numpy as jnp
 from jax import lax
+from jax.experimental import pallas as pl
+from jax.experimental.pallas import tpu as pltpu
 from jax.sharding import PartitionSpec as P
 
 AXIS = "tensor"
@@ -36,6 +39,55 @@
     return lax.dynamic_update_slice(full, block[:, None], (0, z % Z, 0, 0))
 
 
+def finish_kernel(order, low_ref, high_ref, power_ref, out_ref):
+    held = {
+        (0, 0): (low_ref, 0), (0, 1): (low_ref, 1), (1, 1): (low_ref, 2), (2, 0): (low_ref, 3), (3, 0): (low_ref, 4),
+        (2, 2): (high_ref, 0), (2, 3): (high_ref, 1), (3, 3): (high_ref, 2), (2, 1): (high_ref, 3), (3, 1): (high_ref, 4),
+    }
+    columns = power_ref.shape[1]
+    chunk = columns // 4
+
+    def times_gram(left, c):
+        total = None
+        for d in range(4):
+            ref, i = held[(d, c)] if (d, c) in held else held[(c, d)]
+            contract = 0 if (d, c) in held else 1
+            term = lax.dot_general(
+                left[d], ref[i * chunk:(i + 1) * chunk, :], (((1,), (contract,)), ((), ())),
+                preferred_element_type=jnp.float32,
+            )
+            total = term if total is None else total + term
+        return total
+
+    row = lax.broadcasted_iota(jnp.int32, (chunk, chunk), 0)
+    column = lax.broadcasted_iota(jnp.int32, (chunk, chunk), 1)
+    diagonal = jnp.zeros((chunk, chunk), jnp.float32)
+    for ref, i in (held[(d, d)] for d in range(4)):
+        block = ref[i * chunk:(i + 1) * chunk, :].astype(jnp.float32)
+        diagonal += jnp.where(row == column, block, 0.0)
+    ratio = columns / (3.0 * jnp.sum(diagonal, keepdims=True))
+    scale = math.sqrt(order) * jnp.sqrt(ratio)
+
+    power = [power_ref[:, d * chunk:(d + 1) * chunk] for d in range(4)]
+    first_full = [times_gram(power, c) * ratio for c in range(4)]
+    first = [f.astype(jnp.bfloat16) for f in first_full]
+    for c in range(4):
+        second = times_gram(first, c) * ratio
+        mixed = 3.4445 * power[c].astype(jnp.float32) - 4.775 * first_full[c] + 2.0315 * second
+        out_ref[:, c * chunk:(c + 1) * chunk] = (scale * mixed).astype(jnp.bfloat16)
+
+
+def finish(low, high, power, order):
+    return pl.pallas_call(
+        functools.partial(finish_kernel, order),
+        out_shape=jax.ShapeDtypeStruct(power.shape, jnp.bfloat16),
+        in_specs=[pl.BlockSpec(memory_space=pltpu.VMEM)] * 3,
+        out_specs=pl.BlockSpec(memory_space=pltpu.VMEM),
+        compiler_params=pltpu.CompilerParams(vmem_limit_bytes=32 * 1024 * 1024),
+        name="finish",
+    )(low, high, power)
+
+
 def body(factor_rows, basis):
     rows, order = factor_rows.shape
     columns = basis.shape[1]
@@ -44,9 +96,8 @@
     position = lax.axis_index(AXIS)
     y, z = position // Z, position % Z
 
-    halves = basis.reshape(rows, 2, half)
-    mine = lax.dynamic_index_in_dim(halves, y, 1, keepdims=False)
-    other = lax.dynamic_index_in_dim(halves, 1 - y, 1, keepdims=False)
+    mine = lax.dynamic_slice_in_dim(basis, y * half, half, 1)
+    other = lax.dynamic_slice_in_dim(basis, (1 - y) * half, half, 1)
     other = lax.ppermute(other, AXIS, ACROSS)
     first_row = y == 0
     block = jnp.stack([jnp.where(first_row, mine, other), jnp.where(first_row, other, mine)])
@@ -83,27 +134,11 @@
     parts = lax.all_gather(part, AXIS, axis=0, axis_index_groups=FAR)
     part = jnp.sum(parts.astype(jnp.float32), 0).astype(jnp.bfloat16)
     other_part = lax.ppermute(part, AXIS, ACROSS)
-    own_blocks = lax.all_gather(part, AXIS, axis=0, axis_index_groups=NEAR).reshape(5, chunk, chunk)
-    other_blocks = lax.all_gather(other_part, AXIS, axis=0, axis_index_groups=NEAR).reshape(5, chunk, chunk)
+    own_blocks = lax.all_gather(part, AXIS, axis=0, tiled=True, axis_index_groups=NEAR)
+    other_blocks = lax.all_gather(other_part, AXIS, axis=0, tiled=True, axis_index_groups=NEAR)
     low = jnp.where(first_row, own_blocks, other_blocks)
     high = jnp.where(first_row, other_blocks, own_blocks)
-
-    gram = jnp.block(
-        [
-            [low[0], low[1], low[3].T, low[4].T],
-            [low[1].T, low[2], high[3].T, high[4].T],
-            [low[3], high[3], high[0], high[1]],
-            [low[4], high[4], high[1].T, high[2]],
-        ]
-    )
-    eye = jnp.eye(chunk, dtype=jnp.bool_)
-    diagonal = sum(jnp.where(eye, d.astype(jnp.float32), 0.0) for d in (low[0], low[2], high[0], high[2]))
-    ratio = columns / (3.0 * jnp.sum(diagonal))
-    first_full = jnp.dot(power, gram, preferred_element_type=jnp.float32) * ratio
-    first = first_full.astype(jnp.bfloat16)
-    second = jnp.dot(first, gram, preferred_element_type=jnp.float32) * ratio
-    mixed = 3.4445 * power.astype(jnp.float32) - 4.775 * first_full + 2.0315 * second
-    return (math.sqrt(order) * jnp.sqrt(ratio) * mixed).astype(jnp.bfloat16)
+    return finish(low, high, power, order)
 
 
 def solution(mesh):

time: 213 us -> 191 us (0.90)
  other arithmetic: 20.6 us -> 2.24 us
  matrix products: 4.31 us -> 1.96 us
    concatenate x2 -> x1, other arithmetic: 18.4 us -> 0.02 us  [body(): plane = jnp.concatenate([both[0], both[1]], 1)]
    dot_general x2 -> x0, matrix products: 2.35 us -> none  [the longest x1 1.55 us: body(): second = jnp.dot(first, gram, preferred_element_type=jnp.float32) * ratio]
where the time goes in v2:
time: 191 us; the launch traced here: 190 us
  starting transfers between devices  70.6 us (37%)
  blocking collectives  66 us (35%)
  waiting for transfers between devices  44.7 us (23%)
  other arithmetic  2.24 us (1%)
  matrix products  1.96 us (1%)
  local copies, waits for them, and re-layouts  1.95 us (1%)
    ppermute x7, starting transfers between devices, ring(): b = lax.ppermute(b, AXIS, shift(-1))  41 us
    all_gather x1, blocking collectives, body(): parts = lax.all_gather(part, AXIS, axis=0, axis_index_groups=FAR)  28.2 us
    ppermute x8, waiting for transfers between devices, ring(): a = lax.ppermute(a, AXIS, shift(1))  22.6 us
    all_to_all x1, waiting for transfers between devices, body(): lax.all_to_all(blocks.reshape(CUBE, -1, chunk), AXIS, 0, 0, axis_index_gr...  18.6 us
    ppermute x8, starting transfers between devices, ring(): a = lax.ppermute(a, AXIS, shift(1))  17.2 us
    all_gather x1, blocking collectives, body(): lax.all_gather(part, AXIS, axis=0, tiled=True, axis_index_groups=NEAR)  15.8 us
    all_gather x1, blocking collectives, body(): lax.all_gather(other_part, AXIS, axis=0, tiled=True, axis_index_groups=NEAR)  15.2 us
    all_gather x1, blocking collectives, body(): both = lax.all_gather(tile, AXIS, axis=0, axis_index_groups=PAIRS)  6.7 us
  transfers between devices with their start and end apart: 19, of which 10 were waited for; matrix products, arithmetic and copies ran while one was open for 0% of the time, Pallas kernels for 0%

profile of v2, /device:TPU:6, one launch (start us, length us, event | category | flops | bytes accessed | tf_op | source)
XLA Modules:
  0.0 189.9 jit_solution(9203143088804295185)
XLA Ops:
  0.0 0.9 constant_dynamic-slice_fusion
  0.9 3.5 %collective-permute-start = (bf16[112,512]{1,0:T(8,128)(2,1)S(1)}, bf16[112,512]{1,0:T(8,128)(2,1)S(1)}, u32[]{:S(2)}, u32[]{:S(2)}) collective-permute-start(bf16[112,512]{1,0:T(8,128)(2,1)S(1)} %constant_dynamic-slice_fusion), channel_id=1, source_target_pairs={{0,16},{1,17},{2,18},{3,19},{4,20},{5,21},{6,22},{7,23},{8,24},{9,... | collective-permute-start | bytes 344072 | tf_op jit(solution)/shard_map/ppermute | solution.py:101
  4.4 3.3 %collective-permute-done = bf16[112,512]{1,0:T(8,128)(2,1)S(1)} collective-permute-done((bf16[112,512]{1,0:T(8,128)(2,1)S(1)}, bf16[112,512]{1,0:T(8,128)(2,1)S(1)}, u32[]{:S(2)}, u32[]{:S(2)}) %collective-permute-start) | collective-permute-done | bytes 114720 | tf_op jit(solution)/shard_map/ppermute | solution.py:101
  7.7 0.9 select_bitcast_fusion.3
  8.6 3.8 %collective-permute-start.1 = (bf16[2,112,512]{2,1,0:T(8,128)(2,1)S(1)}, bf16[2,112,512]{2,1,0:T(8,128)(2,1)S(1)}, u32[]{:S(2)}, u32[]{:S(2)}) collective-permute-start(bf16[2,112,512]{2,1,0:T(8,128)(2,1)S(1)} %pad_maximum_fusion.1), channel_id=1, source_target_pairs={{0,1},{1,2},{2,3},{3,4},{4,5},{5,6},{6,7},{7,8},{8,9},{9,10},{10,1... | collective-permute-start | bytes 688136 | tf_op jit(solution)/shard_map/ppermute | solution.py:30
  12.5 9.5 %collective-permute-start.9 = (bf16[2,112,512]{2,1,0:T(8,128)(2,1)S(1)}, bf16[2,112,512]{2,1,0:T(8,128)(2,1)S(1)}, u32[]{:S(2)}, u32[]{:S(2)}) collective-permute-start(bf16[2,112,512]{2,1,0:T(8,128)(2,1)S(1)} %pad_maximum_fusion.1), channel_id=1, source_target_pairs={{0,15},{1,0},{2,1},{3,2},{4,3},{5,4},{6,5},{7,6},{8,7},{9,8},{10,9... | collective-permute-start | bytes 688136 | tf_op jit(solution)/shard_map/ppermute | solution.py:33
  22.0 3.5 %collective-permute-start.16 = (bf16[112,3584]{1,0:T(8,128)(2,1)}, bf16[112,3584]{1,0:T(8,128)(2,1)S(1)}, u32[]{:S(2)}, u32[]{:S(2)}) collective-permute-start(bf16[112,3584]{1,0:T(8,128)(2,1)} %param.2), channel_id=1, source_target_pairs={{0,16},{1,17},{2,18},{3,19},{4,20},{5,21},{6,22},{7,23},{8,24},{9,... | collective-permute-start | bytes 2408456 | tf_op jit(solution)/shard_map/ppermute | solution.py:104
  25.8 0.4 broadcast_in_dim.51
  26.3 0.0 collective-permute-done.1
  26.3 1.9 %collective-permute-start.2 = (bf16[2,112,512]{2,1,0:T(8,128)(2,1)S(1)}, bf16[2,112,512]{2,1,0:T(8,128)(2,1)S(1)}, u32[]{:S(2)}, u32[]{:S(2)}) collective-permute-start(bf16[2,112,512]{2,1,0:T(8,128)(2,1)S(1)} %collective-permute-done.1), channel_id=1, source_target_pairs={{0,1},{1,2},{2,3},{3,4},{4,5},{5,6},{6,7},{7,8},{8,9},{9,10},{10,1... | collective-permute-start | bytes 688136 | tf_op jit(solution)/shard_map/ppermute | solution.py:30
  28.2 0.0 collective-permute-done.9
  28.2 5.1 %collective-permute-start.10 = (bf16[2,112,512]{2,1,0:T(8,128)(2,1)S(1)}, bf16[2,112,512]{2,1,0:T(8,128)(2,1)S(1)}, u32[]{:S(2)}, u32[]{:S(2)}) collective-permute-start(bf16[2,112,512]{2,1,0:T(8,128)(2,1)S(1)} %collective-permute-done.9), channel_id=1, source_target_pairs={{0,15},{1,0},{2,1},{3,2},{4,3},{5,4},{6,5},{7,6},{8,7},{9,8},{10,9... | collective-permute-start | bytes 688136 | tf_op jit(solution)/shard_map/ppermute | solution.py:33
  33.4 2.0 %collective-permute-done.2 = bf16[2,112,512]{2,1,0:T(8,128)(2,1)S(1)} collective-permute-done((bf16[2,112,512]{2,1,0:T(8,128)(2,1)S(1)}, bf16[2,112,512]{2,1,0:T(8,128)(2,1)S(1)}, u32[]{:S(2)}, u32[]{:S(2)}) %collective-permute-start.2) | collective-permute-done | bytes 229408 | tf_op jit(solution)/shard_map/ppermute | solution.py:30
  35.4 1.9 %collective-permute-start.3 = (bf16[2,112,512]{2,1,0:T(8,128)(2,1)S(1)}, bf16[2,112,512]{2,1,0:T(8,128)(2,1)S(1)}, u32[]{:S(2)}, u32[]{:S(2)}) collective-permute-start(bf16[2,112,512]{2,1,0:T(8,128)(2,1)S(1)} %collective-permute-done.2), channel_id=1, source_target_pairs={{0,1},{1,2},{2,3},{3,4},{4,5},{5,6},{6,7},{7,8},{8,9},{9,10},{10,1... | collective-permute-start | bytes 688136 | tf_op jit(solution)/shard_map/ppermute | solution.py:30
  37.3 0.0 collective-permute-done.10
  37.3 5.1 %collective-permute-start.11 = (bf16[2,112,512]{2,1,0:T(8,128)(2,1)S(1)}, bf16[2,112,512]{2,1,0:T(8,128)(2,1)S(1)}, u32[]{:S(2)}, u32[]{:S(2)}) collective-permute-start(bf16[2,112,512]{2,1,0:T(8,128)(2,1)S(1)} %collective-permute-done.10), channel_id=1, source_target_pairs={{0,15},{1,0},{2,1},{3,2},{4,3},{5,4},{6,5},{7,6},{8,7},{9,8},{10,9... | collective-permute-start | bytes 688136 | tf_op jit(solution)/shard_map/ppermute | solution.py:33
  42.5 2.0 %collective-permute-done.3 = bf16[2,112,512]{2,1,0:T(8,128)(2,1)S(1)} collective-permute-done((bf16[2,112,512]{2,1,0:T(8,128)(2,1)S(1)}, bf16[2,112,512]{2,1,0:T(8,128)(2,1)S(1)}, u32[]{:S(2)}, u32[]{:S(2)}) %collective-permute-start.3) | collective-permute-done | bytes 229408 | tf_op jit(solution)/shard_map/ppermute | solution.py:30
  44.5 1.9 %collective-permute-start.4 = (bf16[2,112,512]{2,1,0:T(8,128)(2,1)S(1)}, bf16[2,112,512]{2,1,0:T(8,128)(2,1)S(1)}, u32[]{:S(2)}, u32[]{:S(2)}) collective-permute-start(bf16[2,112,512]{2,1,0:T(8,128)(2,1)S(1)} %collective-permute-done.3), channel_id=1, source_target_pairs={{0,1},{1,2},{2,3},{3,4},{4,5},{5,6},{6,7},{7,8},{8,9},{9,10},{10,1... | collective-permute-start | bytes 688136 | tf_op jit(solution)/shard_map/ppermute | solution.py:30
  46.4 0.0 collective-permute-done.11
  46.5 5.1 %collective-permute-start.12 = (bf16[2,112,512]{2,1,0:T(8,128)(2,1)S(1)}, bf16[2,112,512]{2,1,0:T(8,128)(2,1)S(1)}, u32[]{:S(2)}, u32[]{:S(2)}) collective-permute-start(bf16[2,112,512]{2,1,0:T(8,128)(2,1)S(1)} %collective-permute-done.11), channel_id=1, source_target_pairs={{0,15},{1,0},{2,1},{3,2},{4,3},{5,4},{6,5},{7,6},{8,7},{9,8},{10,9... | collective-permute-start | bytes 688136 | tf_op jit(solution)/shard_map/ppermute | solution.py:33
  51.6 2.0 %collective-permute-done.4 = bf16[2,112,512]{2,1,0:T(8,128)(2,1)S(1)} collective-permute-done((bf16[2,112,512]{2,1,0:T(8,128)(2,1)S(1)}, bf16[2,112,512]{2,1,0:T(8,128)(2,1)S(1)}, u32[]{:S(2)}, u32[]{:S(2)}) %collective-permute-start.4) | collective-permute-done | bytes 229408 | tf_op jit(solution)/shard_map/ppermute | solution.py:30
  53.6 1.9 %collective-permute-start.5 = (bf16[2,112,512]{2,1,0:T(8,128)(2,1)S(1)}, bf16[2,112,512]{2,1,0:T(8,128)(2,1)S(1)}, u32[]{:S(2)}, u32[]{:S(2)}) collective-permute-start(bf16[2,112,512]{2,1,0:T(8,128)(2,1)S(1)} %collective-permute-done.4), channel_id=1, source_target_pairs={{0,1},{1,2},{2,3},{3,4},{4,5},{5,6},{6,7},{7,8},{8,9},{9,10},{10,1... | collective-permute-start | bytes 688136 | tf_op jit(solution)/shard_map/ppermute | solution.py:30
  55.6 0.0 collective-permute-done.12
  55.6 5.1 %collective-permute-start.13 = (bf16[2,112,512]{2,1,0:T(8,128)(2,1)S(1)}, bf16[2,112,512]{2,1,0:T(8,128)(2,1)S(1)}, u32[]{:S(2)}, u32[]{:S(2)}) collective-permute-start(bf16[2,112,512]{2,1,0:T(8,128)(2,1)S(1)} %collective-permute-done.12), channel_id=1, source_target_pairs={{0,15},{1,0},{2,1},{3,2},{4,3},{5,4},{6,5},{7,6},{8,7},{9,8},{10,9... | collective-permute-start | bytes 688136 | tf_op jit(solution)/shard_map/ppermute | solution.py:33
  60.7 2.5 %collective-permute-done.5 = bf16[2,112,512]{2,1,0:T(8,128)(2,1)S(1)} collective-permute-done((bf16[2,112,512]{2,1,0:T(8,128)(2,1)S(1)}, bf16[2,112,512]{2,1,0:T(8,128)(2,1)S(1)}, u32[]{:S(2)}, u32[]{:S(2)}) %collective-permute-start.5) | collective-permute-done | bytes 229408 | tf_op jit(solution)/shard_map/ppermute | solution.py:30
  63.2 1.9 %collective-permute-start.6 = (bf16[2,112,512]{2,1,0:T(8,128)(2,1)S(1)}, bf16[2,112,512]{2,1,0:T(8,128)(2,1)S(1)}, u32[]{:S(2)}, u32[]{:S(2)}) collective-permute-start(bf16[2,112,512]{2,1,0:T(8,128)(2,1)S(1)} %collective-permute-done.5), channel_id=1, source_target_pairs={{0,1},{1,2},{2,3},{3,4},{4,5},{5,6},{6,7},{7,8},{8,9},{9,10},{10,1... | collective-permute-start | bytes 688136 | tf_op jit(solution)/shard_map/ppermute | solution.py:30
  65.1 0.0 collective-permute-done.13
  65.1 5.4 %collective-permute-start.14 = (bf16[2,112,512]{2,1,0:T(8,128)(2,1)S(1)}, bf16[2,112,512]{2,1,0:T(8,128)(2,1)S(1)}, u32[]{:S(2)}, u32[]{:S(2)}) collective-permute-start(bf16[2,112,512]{2,1,0:T(8,128)(2,1)S(1)} %collective-permute-done.13), channel_id=1, source_target_pairs={{0,15},{1,0},{2,1},{3,2},{4,3},{5,4},{6,5},{7,6},{8,7},{9,8},{10,9... | collective-permute-start | bytes 688136 | tf_op jit(solution)/shard_map/ppermute | solution.py:33
  70.6 3.3 %collective-permute-done.6 = bf16[2,112,512]{2,1,0:T(8,128)(2,1)S(1)} collective-permute-done((bf16[2,112,512]{2,1,0:T(8,128)(2,1)S(1)}, bf16[2,112,512]{2,1,0:T(8,128)(2,1)S(1)}, u32[]{:S(2)}, u32[]{:S(2)}) %collective-permute-start.6) | collective-permute-done | bytes 229408 | tf_op jit(solution)/shard_map/ppermute | solution.py:30
  73.9 1.9 %collective-permute-start.7 = (bf16[2,112,512]{2,1,0:T(8,128)(2,1)S(1)}, bf16[2,112,512]{2,1,0:T(8,128)(2,1)S(1)}, u32[]{:S(2)}, u32[]{:S(2)}) collective-permute-start(bf16[2,112,512]{2,1,0:T(8,128)(2,1)S(1)} %collective-permute-done.6), channel_id=1, source_target_pairs={{0,1},{1,2},{2,3},{3,4},{4,5},{5,6},{6,7},{7,8},{8,9},{9,10},{10,1... | collective-permute-start | bytes 688136 | tf_op jit(solution)/shard_map/ppermute | solution.py:30
  75.8 0.2 collective-permute-done.14
  76.0 5.6 %collective-permute-start.15 = (bf16[2,112,512]{2,1,0:T(8,128)(2,1)S(1)}, bf16[2,112,512]{2,1,0:T(8,128)(2,1)S(1)}, u32[]{:S(2)}, u32[]{:S(2)}) collective-permute-start(bf16[2,112,512]{2,1,0:T(8,128)(2,1)S(1)} %collective-permute-done.14), channel_id=1, source_target_pairs={{0,15},{1,0},{2,1},{3,2},{4,3},{5,4},{6,5},{7,6},{8,7},{9,8},{10,9... | collective-permute-start | bytes 688136 | tf_op jit(solution)/shard_map/ppermute | solution.py:33
  81.6 3.6 %collective-permute-done.7 = bf16[2,112,512]{2,1,0:T(8,128)(2,1)S(1)} collective-permute-done((bf16[2,112,512]{2,1,0:T(8,128)(2,1)S(1)}, bf16[2,112,512]{2,1,0:T(8,128)(2,1)S(1)}, u32[]{:S(2)}, u32[]{:S(2)}) %collective-permute-start.7) | collective-permute-done | bytes 229408 | tf_op jit(solution)/shard_map/ppermute | solution.py:30
  85.2 1.9 %collective-permute-start.8 = (bf16[2,112,512]{2,1,0:T(8,128)(2,1)S(1)}, bf16[2,112,512]{2,1,0:T(8,128)(2,1)S(1)}, u32[]{:S(2)}, u32[]{:S(2)}) collective-permute-start(bf16[2,112,512]{2,1,0:T(8,128)(2,1)S(1)} %collective-permute-done.7), channel_id=1, source_target_pairs={{0,1},{1,2},{2,3},{3,4},{4,5},{5,6},{6,7},{7,8},{8,9},{9,10},{10,1... | collective-permute-start | bytes 688136 | tf_op jit(solution)/shard_map/ppermute | solution.py:30
  87.1 7.2 %collective-permute-done.8 = bf16[2,112,512]{2,1,0:T(8,128)(2,1)S(1)} collective-permute-done((bf16[2,112,512]{2,1,0:T(8,128)(2,1)S(1)}, bf16[2,112,512]{2,1,0:T(8,128)(2,1)S(1)}, u32[]{:S(2)}, u32[]{:S(2)}) %collective-permute-start.8) | collective-permute-done | bytes 229408 | tf_op jit(solution)/shard_map/ppermute | solution.py:30
  94.4 0.0 copy-start
  94.5 0.0 collective-permute-done.15
  94.6 0.0 collective-permute-done.16
  94.6 0.7 convolution_convert_fusion.2
  95.3 0.2 copy-done
  95.5 0.7 select_bitcast_fusion.1
  96.2 0.3 convolution_convert_fusion
  96.6 6.7 %all-gather = bf16[448,512]{1,0:T(8,128)(2,1)S(1)} all-gather(bf16[224,512]{1,0:T(8,128)(2,1)S(1)} %pad_maximum_fusion.2), channel_id=2, replica_groups={{0,16},{1,17},{2,18},{3,19},{4,20},{5,21},{6,22},{7,23},{8,24},{9,25},{..., dimensions={0}, use_global_device_ids=true | all-gather | bytes 688128 | tf_op jit(solution)/shard_map/all_gather | solution.py:118
  103.3 0.3 convolution_convert_fusion.1
  103.6 0.9 pad_maximum_fusion
  104.5 3.5 %all-to-all-start = ((bf16[4,320,256]{2,1,0:T(8,128)(2,1)}), bf16[4,320,256]{2,1,0:T(8,128)(2,1)S(1)}, u32[]{:S(2)}, u32[]{:S(2)}) async-start(bf16[4,320,256]{2,1,0:T(8,128)(2,1)} %bitcast.36), calls=%async_computation | async-start | bytes 1310720 | tf_op jit(solution)/shard_map/all_to_all | solution.py:130
  108.0 18.6 %all-to-all-done = bf16[4,320,256]{2,1,0:T(8,128)(2,1)S(1)} async-done(((bf16[4,320,256]{2,1,0:T(8,128)(2,1)}), bf16[4,320,256]{2,1,0:T(8,128)(2,1)S(1)}, u32[]{:S(2)}, u32[]{:S(2)}) %all-to-all-start) | async-done | bytes 655392 | tf_op jit(solution)/shard_map/all_to_all | solution.py:130
  126.7 0.1 reduce_sum.24
  126.8 28.2 %all-gather.1 = bf16[1280,256]{1,0:T(8,128)(2,1)S(1)} all-gather(bf16[320,256]{1,0:T(8,128)(2,1)S(1)} %reduce_sum.24), channel_id=3, replica_groups={{0,4,8,12},{1,5,9,13},{2,6,10,14},{3,7,11,15},{16,20,24,28},{17,21,25,2..., dimensions={0}, use_global_device_ids=true | all-gather | bytes 819200 | tf_op jit(solution)/shard_map/all_gather | solution.py:134
  155.0 0.1 reduce_sum.25
  155.1 1.9 %collective-permute-start.17 = (bf16[320,256]{1,0:T(8,128)(2,1)S(1)}, bf16[320,256]{1,0:T(8,128)(2,1)S(1)}, u32[]{:S(2)}, u32[]{:S(2)}) collective-permute-start(bf16[320,256]{1,0:T(8,128)(2,1)S(1)} %reduce_sum.25), channel_id=1, source_target_pairs={{0,16},{1,17},{2,18},{3,19},{4,20},{5,21},{6,22},{7,23},{8,24},{9,... | collective-permute-start | bytes 491528 | tf_op jit(solution)/shard_map/ppermute | solution.py:136
  157.0 15.8 %all_gather.22 = bf16[1280,256]{1,0:T(8,128)(2,1)S(1)} all-gather(bf16[320,256]{1,0:T(8,128)(2,1)S(1)} %reduce_sum.25), channel_id=1, replica_groups={{0,1,2,3},{4,5,6,7},{8,9,10,11},{12,13,14,15},{16,17,18,19},{20,21,22,2..., dimensions={0}, use_global_device_ids=true | all-gather | bytes 819200 | tf_op jit(solution)/shard_map/all_gather | solution.py:137
  172.8 0.0 collective-permute-done.17
  172.9 15.2 %all_gather.23 = bf16[1280,256]{1,0:T(8,128)(2,1)S(1)} all-gather(bf16[320,256]{1,0:T(8,128)(2,1)S(1)} %collective-permute-done.17), channel_id=1, replica_groups={{0,1,2,3},{4,5,6,7},{8,9,10,11},{12,13,14,15},{16,17,18,19},{20,21,22,2..., dimensions={0}, use_global_device_ids=true | all-gather | bytes 819200 | tf_op jit(solution)/shard_map/all_gather | solution.py:138
  188.1 0.1 broadcast_select_fusion
  188.2 1.7 finish.1
  (22 shorter events, 0.5 us)
Async XLA Ops:
  0.9 6.8 %collective-permute-start = (bf16[112,512]{1,0:T(8,128)(2,1)S(1)}, bf16[112,512]{1,0:T(8,128)(2,1)S(1)}, u32[]{:S(2)}, u32[]{:S(2)}) collective-permute-start(bf16[112,512]{1,0:T(8,128)(2,1)S(1)} %constant_dynamic-slice_fusion), channel_id=1, source_target_pairs={{0,16},{1,17},{2,18},{3,19},{4,20},{5,21},{6,22},{7,23},{8,24},{9,... | collective-permute-start | bytes 344072 | tf_op jit(solution)/shard_map/ppermute | solution.py:101
  8.6 17.6 %collective-permute-start.1 = (bf16[2,112,512]{2,1,0:T(8,128)(2,1)S(1)}, bf16[2,112,512]{2,1,0:T(8,128)(2,1)S(1)}, u32[]{:S(2)}, u32[]{:S(2)}) collective-permute-start(bf16[2,112,512]{2,1,0:T(8,128)(2,1)S(1)} %pad_maximum_fusion.1), channel_id=1, source_target_pairs={{0,1},{1,2},{2,3},{3,4},{4,5},{5,6},{6,7},{7,8},{8,9},{9,10},{10,1... | collective-permute-start | bytes 688136 | tf_op jit(solution)/shard_map/ppermute | solution.py:30
  12.5 15.7 %collective-permute-start.9 = (bf16[2,112,512]{2,1,0:T(8,128)(2,1)S(1)}, bf16[2,112,512]{2,1,0:T(8,128)(2,1)S(1)}, u32[]{:S(2)}, u32[]{:S(2)}) collective-permute-start(bf16[2,112,512]{2,1,0:T(8,128)(2,1)S(1)} %pad_maximum_fusion.1), channel_id=1, source_target_pairs={{0,15},{1,0},{2,1},{3,2},{4,3},{5,4},{6,5},{7,6},{8,7},{9,8},{10,9... | collective-permute-start | bytes 688136 | tf_op jit(solution)/shard_map/ppermute | solution.py:33
  22.0 72.6 %collective-permute-start.16 = (bf16[112,3584]{1,0:T(8,128)(2,1)}, bf16[112,3584]{1,0:T(8,128)(2,1)S(1)}, u32[]{:S(2)}, u32[]{:S(2)}) collective-permute-start(bf16[112,3584]{1,0:T(8,128)(2,1)} %param.2), channel_id=1, source_target_pairs={{0,16},{1,17},{2,18},{3,19},{4,20},{5,21},{6,22},{7,23},{8,24},{9,... | collective-permute-start | bytes 2408456 | tf_op jit(solution)/shard_map/ppermute | solution.py:104
  26.3 9.1 %collective-permute-start.2 = (bf16[2,112,512]{2,1,0:T(8,128)(2,1)S(1)}, bf16[2,112,512]{2,1,0:T(8,128)(2,1)S(1)}, u32[]{:S(2)}, u32[]{:S(2)}) collective-permute-start(bf16[2,112,512]{2,1,0:T(8,128)(2,1)S(1)} %collective-permute-done.1), channel_id=1, source_target_pairs={{0,1},{1,2},{2,3},{3,4},{4,5},{5,6},{6,7},{7,8},{8,9},{9,10},{10,1... | collective-permute-start | bytes 688136 | tf_op jit(solution)/shard_map/ppermute | solution.py:30
  28.2 9.1 %collective-permute-start.10 = (bf16[2,112,512]{2,1,0:T(8,128)(2,1)S(1)}, bf16[2,112,512]{2,1,0:T(8,128)(2,1)S(1)}, u32[]{:S(2)}, u32[]{:S(2)}) collective-permute-start(bf16[2,112,512]{2,1,0:T(8,128)(2,1)S(1)} %collective-permute-done.9), channel_id=1, source_target_pairs={{0,15},{1,0},{2,1},{3,2},{4,3},{5,4},{6,5},{7,6},{8,7},{9,8},{10,9... | collective-permute-start | bytes 688136 | tf_op jit(solution)/shard_map/ppermute | solution.py:33
  35.4 9.1 %collective-permute-start.3 = (bf16[2,112,512]{2,1,0:T(8,128)(2,1)S(1)}, bf16[2,112,512]{2,1,0:T(8,128)(2,1)S(1)}, u32[]{:S(2)}, u32[]{:S(2)}) collective-permute-start(bf16[2,112,512]{2,1,0:T(8,128)(2,1)S(1)} %collective-permute-done.2), channel_id=1, source_target_pairs={{0,1},{1,2},{2,3},{3,4},{4,5},{5,6},{6,7},{7,8},{8,9},{9,10},{10,1... | collective-permute-start | bytes 688136 | tf_op jit(solution)/shard_map/ppermute | solution.py:30
  37.3 9.1 %collective-permute-start.11 = (bf16[2,112,512]{2,1,0:T(8,128)(2,1)S(1)}, bf16[2,112,512]{2,1,0:T(8,128)(2,1)S(1)}, u32[]{:S(2)}, u32[]{:S(2)}) collective-permute-start(bf16[2,112,512]{2,1,0:T(8,128)(2,1)S(1)} %collective-permute-done.10), channel_id=1, source_target_pairs={{0,15},{1,0},{2,1},{3,2},{4,3},{5,4},{6,5},{7,6},{8,7},{9,8},{10,9... | collective-permute-start | bytes 688136 | tf_op jit(solution)/shard_map/ppermute | solution.py:33
  44.5 9.1 %collective-permute-start.4 = (bf16[2,112,512]{2,1,0:T(8,128)(2,1)S(1)}, bf16[2,112,512]{2,1,0:T(8,128)(2,1)S(1)}, u32[]{:S(2)}, u32[]{:S(2)}) collective-permute-start(bf16[2,112,512]{2,1,0:T(8,128)(2,1)S(1)} %collective-permute-done.3), channel_id=1, source_target_pairs={{0,1},{1,2},{2,3},{3,4},{4,5},{5,6},{6,7},{7,8},{8,9},{9,10},{10,1... | collective-permute-start | bytes 688136 | tf_op jit(solution)/shard_map/ppermute | solution.py:30
  46.5 9.1 %collective-permute-start.12 = (bf16[2,112,512]{2,1,0:T(8,128)(2,1)S(1)}, bf16[2,112,512]{2,1,0:T(8,128)(2,1)S(1)}, u32[]{:S(2)}, u32[]{:S(2)}) collective-permute-start(bf16[2,112,512]{2,1,0:T(8,128)(2,1)S(1)} %collective-permute-done.11), channel_id=1, source_target_pairs={{0,15},{1,0},{2,1},{3,2},{4,3},{5,4},{6,5},{7,6},{8,7},{9,8},{10,9... | collective-permute-start | bytes 688136 | tf_op jit(solution)/shard_map/ppermute | solution.py:33
  53.6 9.6 %collective-permute-start.5 = (bf16[2,112,512]{2,1,0:T(8,128)(2,1)S(1)}, bf16[2,112,512]{2,1,0:T(8,128)(2,1)S(1)}, u32[]{:S(2)}, u32[]{:S(2)}) collective-permute-start(bf16[2,112,512]{2,1,0:T(8,128)(2,1)S(1)} %collective-permute-done.4), channel_id=1, source_target_pairs={{0,1},{1,2},{2,3},{3,4},{4,5},{5,6},{6,7},{7,8},{8,9},{9,10},{10,1... | collective-permute-start | bytes 688136 | tf_op jit(solution)/shard_map/ppermute | solution.py:30
  55.6 9.5 %collective-permute-start.13 = (bf16[2,112,512]{2,1,0:T(8,128)(2,1)S(1)}, bf16[2,112,512]{2,1,0:T(8,128)(2,1)S(1)}, u32[]{:S(2)}, u32[]{:S(2)}) collective-permute-start(bf16[2,112,512]{2,1,0:T(8,128)(2,1)S(1)} %collective-permute-done.12), channel_id=1, source_target_pairs={{0,15},{1,0},{2,1},{3,2},{4,3},{5,4},{6,5},{7,6},{8,7},{9,8},{10,9... | collective-permute-start | bytes 688136 | tf_op jit(solution)/shard_map/ppermute | solution.py:33
  63.2 10.7 %collective-permute-start.6 = (bf16[2,112,512]{2,1,0:T(8,128)(2,1)S(1)}, bf16[2,112,512]{2,1,0:T(8,128)(2,1)S(1)}, u32[]{:S(2)}, u32[]{:S(2)}) collective-permute-start(bf16[2,112,512]{2,1,0:T(8,128)(2,1)S(1)} %collective-permute-done.5), channel_id=1, source_target_pairs={{0,1},{1,2},{2,3},{3,4},{4,5},{5,6},{6,7},{7,8},{8,9},{9,10},{10,1... | collective-permute-start | bytes 688136 | tf_op jit(solution)/shard_map/ppermute | solution.py:30
  65.1 10.9 %collective-permute-start.14 = (bf16[2,112,512]{2,1,0:T(8,128)(2,1)S(1)}, bf16[2,112,512]{2,1,0:T(8,128)(2,1)S(1)}, u32[]{:S(2)}, u32[]{:S(2)}) collective-permute-start(bf16[2,112,512]{2,1,0:T(8,128)(2,1)S(1)} %collective-permute-done.13), channel_id=1, source_target_pairs={{0,15},{1,0},{2,1},{3,2},{4,3},{5,4},{6,5},{7,6},{8,7},{9,8},{10,9... | collective-permute-start | bytes 688136 | tf_op jit(solution)/shard_map/ppermute | solution.py:33
  73.9 11.3 %collective-permute-start.7 = (bf16[2,112,512]{2,1,0:T(8,128)(2,1)S(1)}, bf16[2,112,512]{2,1,0:T(8,128)(2,1)S(1)}, u32[]{:S(2)}, u32[]{:S(2)}) collective-permute-start(bf16[2,112,512]{2,1,0:T(8,128)(2,1)S(1)} %collective-permute-done.6), channel_id=1, source_target_pairs={{0,1},{1,2},{2,3},{3,4},{4,5},{5,6},{6,7},{7,8},{8,9},{9,10},{10,1... | collective-permute-start | bytes 688136 | tf_op jit(solution)/shard_map/ppermute | solution.py:30
  76.0 18.5 %collective-permute-start.15 = (bf16[2,112,512]{2,1,0:T(8,128)(2,1)S(1)}, bf16[2,112,512]{2,1,0:T(8,128)(2,1)S(1)}, u32[]{:S(2)}, u32[]{:S(2)}) collective-permute-start(bf16[2,112,512]{2,1,0:T(8,128)(2,1)S(1)} %collective-permute-done.14), channel_id=1, source_target_pairs={{0,15},{1,0},{2,1},{3,2},{4,3},{5,4},{6,5},{7,6},{8,7},{9,8},{10,9... | collective-permute-start | bytes 688136 | tf_op jit(solution)/shard_map/ppermute | solution.py:33
  85.2 9.1 %collective-permute-start.8 = (bf16[2,112,512]{2,1,0:T(8,128)(2,1)S(1)}, bf16[2,112,512]{2,1,0:T(8,128)(2,1)S(1)}, u32[]{:S(2)}, u32[]{:S(2)}) collective-permute-start(bf16[2,112,512]{2,1,0:T(8,128)(2,1)S(1)} %collective-permute-done.7), channel_id=1, source_target_pairs={{0,1},{1,2},{2,3},{3,4},{4,5},{5,6},{6,7},{7,8},{8,9},{9,10},{10,1... | collective-permute-start | bytes 688136 | tf_op jit(solution)/shard_map/ppermute | solution.py:30
  94.4 1.1 copy-start
  104.5 22.2 %all-to-all-start = ((bf16[4,320,256]{2,1,0:T(8,128)(2,1)}), bf16[4,320,256]{2,1,0:T(8,128)(2,1)S(1)}, u32[]{:S(2)}, u32[]{:S(2)}) async-start(bf16[4,320,256]{2,1,0:T(8,128)(2,1)} %bitcast.36), calls=%async_computation | async-start | bytes 1310720 | tf_op jit(solution)/shard_map/all_to_all | solution.py:130
  155.1 17.7 %collective-permute-start.17 = (bf16[320,256]{1,0:T(8,128)(2,1)S(1)}, bf16[320,256]{1,0:T(8,128)(2,1)S(1)}, u32[]{:S(2)}, u32[]{:S(2)}) collective-permute-start(bf16[320,256]{1,0:T(8,128)(2,1)S(1)} %reduce_sum.25), channel_id=1, source_target_pairs={{0,16},{1,17},{2,18},{3,19},{4,20},{5,21},{6,22},{7,23},{8,24},{9,... | collective-permute-start | bytes 491528 | tf_op jit(solution)/shard_map/ppermute | solution.py:136

commit v3 on v2

--- a/solution.py
+++ b/solution.py
@@ -14,6 +14,7 @@
 CUBE = 4
 
 ACROSS = [(y * Z + z, (1 - y) * Z + z) for y in range(Y) for z in range(Z)]
+ALONG = [[y * Z + z for z in range(Z)] for y in range(Y)]
 PAIRS = [[z, Z + z] for z in range(Z)]
 NEAR = [[y * Z + c * CUBE + i for i in range(CUBE)] for y in range(Y) for c in range(Z // CUBE)]
 FAR = [[y * Z + c * CUBE + i for c in range(Z // CUBE)] for y in range(Y) for i in range(CUBE)]
@@ -35,8 +36,8 @@
     return up, down
 
 
-def place(full, block, z):
-    return lax.dynamic_update_slice(full, block[:, None], (0, z % Z, 0, 0))
+def place(full, block, y, z):
+    return lax.dynamic_update_slice(full, block[None, None], (y, z % Z, 0, 0))
 
 
 def finish_kernel(order, low_ref, high_ref, power_ref, out_ref):
@@ -98,18 +99,19 @@
 
     mine = lax.dynamic_slice_in_dim(basis, y * half, half, 1)
     other = lax.dynamic_slice_in_dim(basis, (1 - y) * half, half, 1)
+    own_rows = lax.all_gather(mine, AXIS, axis=0, axis_index_groups=ALONG)
     other = lax.ppermute(other, AXIS, ACROSS)
     first_row = y == 0
-    block = jnp.stack([jnp.where(first_row, mine, other), jnp.where(first_row, other, mine)])
     far_rows = lax.ppermute(factor_rows, AXIS, ACROSS)
 
-    up, down = ring(block)
+    up, down = ring(other)
     full = jnp.zeros((2, Z, rows, half), basis.dtype)
-    full = place(full, block, z)
+    full = place(full, other, 1 - y, z)
     for step, part in enumerate(up):
-        full = place(full, part, z - step - 1 + Z)
+        full = place(full, part, 1 - y, z - step - 1 + Z)
     for step, part in enumerate(down):
-        full = place(full, part, z + step + 1)
+        full = place(full, part, 1 - y, z + step + 1)
+    full = lax.dynamic_update_slice(full, own_rows[None], (y, 0, 0, 0))
     full = full.reshape(order, half)
 
     near = jnp.dot(factor_rows, full, preferred_element_type=jnp.float32).astype(jnp.bfloat16)

time: 191 us -> 207 us (1.084)
  waiting for transfers between devices: 44.7 us -> 29.1 us
  local copies, waits for them, and re-layouts: 1.95 us -> 17.3 us
  between operations: 0.81 us -> 14 us
  matrix products: 1.96 us -> 6.04 us
  blocking collectives: 66 us -> 63.1 us
  starting transfers between devices: 70.6 us -> 72.8 us
    ppermute x8, waiting for transfers between devices: 22.6 us -> 7.16 us  [ring(): a = lax.ppermute(a, AXIS, shift(1))]
    dynamic_update_slice x15 -> x17, local copies, waits for them, and re-layouts: 0.34 us -> 13.4 us  [the longest x16 10.4 us: place(): return lax.dynamic_update_slice(full, block[None, None], (y, z % Z, 0, 0))]
    all_gather x1, blocking collectives: 28.2 us -> 24 us  [body(): parts = lax.all_gather(part, AXIS, axis=0, axis_index_groups=FAR)]
    ppermute x7, waiting for transfers between devices: 0.17 us -> 3.5 us  [ring(): b = lax.ppermute(b, AXIS, shift(-1))]
    ppermute x1, waiting for transfers between devices: 3.28 us -> 0.53 us  [body(): other = lax.ppermute(other, AXIS, ACROSS)]
  transfers between devices with their start and end apart: 19 -> 20, of which waited for: 10 -> 10; matrix products, arithmetic and copies ran while one was open for 0% -> 8% of each run, Pallas kernels for 0% -> 0%
where the time goes in v3:
time: 207 us; the launch traced here: 205 us
  starting transfers between devices  72.8 us (35%)
  blocking collectives  63.1 us (30%)
  waiting for transfers between devices  29.1 us (14%)
  local copies, waits for them, and re-layouts  17.3 us (8%)
  between operations  14 us (7%)
  matrix products  6.04 us (3%)
    ppermute x7, starting transfers between devices, ring(): b = lax.ppermute(b, AXIS, shift(-1))  42.7 us
    all_gather x1, blocking collectives, body(): parts = lax.all_gather(part, AXIS, axis=0, axis_index_groups=FAR)  24 us
    all_to_all x1, waiting for transfers between devices, body(): lax.all_to_all(blocks.reshape(CUBE, -1, chunk), AXIS, 0, 0, axis_index_gr...  17.9 us
    all_gather x1, blocking collectives, body(): lax.all_gather(part, AXIS, axis=0, tiled=True, axis_index_groups=NEAR)  17.2 us
    ppermute x8, starting transfers between devices, ring(): a = lax.ppermute(a, AXIS, shift(1))  17.2 us
    all_gather x1, blocking collectives, body(): lax.all_gather(other_part, AXIS, axis=0, tiled=True, axis_index_groups=NEAR)  15.1 us
    dynamic_update_slice x16, local copies, waits for them, and re-layouts, place(): return lax.dynamic_update_slice(full, block[None, None], (y, z % Z, 0, 0))  10.4 us
    ppermute x8, waiting for transfers between devices, ring(): a = lax.ppermute(a, AXIS, shift(1))  7.16 us
  transfers between devices with their start and end apart: 20, of which 10 were waited for; matrix products, arithmetic and copies ran while one was open for 8% of the time, Pallas kernels for 0%

profile of v3, /device:TPU:6, one launch (start us, length us, event | category | flops | bytes accessed | tf_op | source)
XLA Modules:
  0.0 205.2 jit_solution(9835447592157236329)
XLA Ops:
  6.5 1.6 constant_dynamic-slice_fusion
  8.2 3.5 %collective-permute-start = (bf16[112,512]{1,0:T(8,128)(2,1)S(1)}, bf16[112,512]{1,0:T(8,128)(2,1)S(1)}, u32[]{:S(2)}, u32[]{:S(2)}) collective-permute-start(bf16[112,512]{1,0:T(8,128)(2,1)S(1)} %get-tuple-element.12), channel_id=1, source_target_pairs={{0,16},{1,17},{2,18},{3,19},{4,20},{5,21},{6,22},{7,23},{8,24},{9,... | collective-permute-start | bytes 344072 | tf_op jit(solution)/shard_map/ppermute | solution.py:103
  11.6 0.0 all-gather.5.cloned.1.call-update
  11.7 2.4 %collective-permute-start.16 = (bf16[112,3584]{1,0:T(8,128)(2,1)}, bf16[112,3584]{1,0:T(8,128)(2,1)S(1)}, u32[]{:S(2)}, u32[]{:S(2)}) collective-permute-start(bf16[112,3584]{1,0:T(8,128)(2,1)} %param.2), channel_id=1, source_target_pairs={{0,16},{1,17},{2,18},{3,19},{4,20},{5,21},{6,22},{7,23},{8,24},{9,... | collective-permute-start | bytes 2408456 | tf_op jit(solution)/shard_map/ppermute | solution.py:105
  14.4 0.5 collective-permute-done
  14.9 3.8 %collective-permute-start.1 = (bf16[112,512]{1,0:T(8,128)(2,1)S(1)}, bf16[112,512]{1,0:T(8,128)(2,1)S(1)}, u32[]{:S(2)}, u32[]{:S(2)}) collective-permute-start(bf16[112,512]{1,0:T(8,128)(2,1)S(1)} %collective-permute-done), channel_id=1, source_target_pairs={{0,1},{1,2},{2,3},{3,4},{4,5},{5,6},{6,7},{7,8},{8,9},{9,10},{10,1... | collective-permute-start | bytes 344072 | tf_op jit(solution)/shard_map/ppermute | solution.py:31
  18.7 9.5 %collective-permute-start.9 = (bf16[112,512]{1,0:T(8,128)(2,1)S(1)}, bf16[112,512]{1,0:T(8,128)(2,1)S(1)}, u32[]{:S(2)}, u32[]{:S(2)}) collective-permute-start(bf16[112,512]{1,0:T(8,128)(2,1)S(1)} %collective-permute-done), channel_id=1, source_target_pairs={{0,15},{1,0},{2,1},{3,2},{4,3},{5,4},{6,5},{7,6},{8,7},{9,8},{10,9... | collective-permute-start | bytes 344072 | tf_op jit(solution)/shard_map/ppermute | solution.py:34
  28.2 2.2 %broadcast_in_dim.54 = bf16[2,16,112,512]{3,2,1,0:T(8,128)(2,1)} broadcast(bf16[]{:T(256)} %constant.147.clone.1), dimensions={} | broadcast | bytes 3670018 | tf_op jit(solution)/shard_map/broadcast_in_dim | solution.py:108
  30.5 0.6 bitcast_dynamic-update-slice_fusion.15
  31.1 0.0 collective-permute-done.1
  31.1 1.9 collective-permute-start.2
  33.0 5.1 %collective-permute-start.10 = (bf16[112,512]{1,0:T(8,128)(2,1)S(1)}, bf16[112,512]{1,0:T(8,128)(2,1)S(1)}, u32[]{:S(2)}, u32[]{:S(2)}) collective-permute-start(bf16[112,512]{1,0:T(8,128)(2,1)S(1)} %collective-permute-done.9), channel_id=1, source_target_pairs={{0,15},{1,0},{2,1},{3,2},{4,3},{5,4},{6,5},{7,6},{8,7},{9,8},{10,9... | collective-permute-start | bytes 344072 | tf_op jit(solution)/shard_map/ppermute | solution.py:34
  38.2 0.6 bitcast_dynamic-update-slice_fusion.14
  38.8 0.3 collective-permute-done.2
  39.2 1.9 collective-permute-start.3
  41.1 5.6 %collective-permute-start.11 = (bf16[112,512]{1,0:T(8,128)(2,1)S(1)}, bf16[112,512]{1,0:T(8,128)(2,1)S(1)}, u32[]{:S(2)}, u32[]{:S(2)}) collective-permute-start(bf16[112,512]{1,0:T(8,128)(2,1)S(1)} %collective-permute-done.10), channel_id=1, source_target_pairs={{0,15},{1,0},{2,1},{3,2},{4,3},{5,4},{6,5},{7,6},{8,7},{9,8},{10,9... | collective-permute-start | bytes 344072 | tf_op jit(solution)/shard_map/ppermute | solution.py:34
  46.7 0.7 bitcast_dynamic-update-slice_fusion.13
  47.3 0.1 collective-permute-done.3
  47.4 1.9 collective-permute-start.4
  49.3 0.0 collective-permute-done.11
  49.3 5.6 %collective-permute-start.12 = (bf16[112,512]{1,0:T(8,128)(2,1)S(1)}, bf16[112,512]{1,0:T(8,128)(2,1)S(1)}, u32[]{:S(2)}, u32[]{:S(2)}) collective-permute-start(bf16[112,512]{1,0:T(8,128)(2,1)S(1)} %collective-permute-done.11), channel_id=1, source_target_pairs={{0,15},{1,0},{2,1},{3,2},{4,3},{5,4},{6,5},{7,6},{8,7},{9,8},{10,9... | collective-permute-start | bytes 344072 | tf_op jit(solution)/shard_map/ppermute | solution.py:34
  54.9 0.7 bitcast_dynamic-update-slice_fusion.12
  55.6 1.9 collective-permute-start.5
  57.5 0.4 collective-permute-done.12
  57.9 5.7 %collective-permute-start.13 = (bf16[112,512]{1,0:T(8,128)(2,1)S(1)}, bf16[112,512]{1,0:T(8,128)(2,1)S(1)}, u32[]{:S(2)}, u32[]{:S(2)}) collective-permute-start(bf16[112,512]{1,0:T(8,128)(2,1)S(1)} %collective-permute-done.12), channel_id=1, source_target_pairs={{0,15},{1,0},{2,1},{3,2},{4,3},{5,4},{6,5},{7,6},{8,7},{9,8},{10,9... | collective-permute-start | bytes 344072 | tf_op jit(solution)/shard_map/ppermute | solution.py:34
  63.6 0.6 bitcast_dynamic-update-slice_fusion.11
  64.2 0.5 collective-permute-done.5
  64.7 1.9 collective-permute-start.6
  66.6 1.4 collective-permute-done.13
  68.0 5.6 %collective-permute-start.14 = (bf16[112,512]{1,0:T(8,128)(2,1)S(1)}, bf16[112,512]{1,0:T(8,128)(2,1)S(1)}, u32[]{:S(2)}, u32[]{:S(2)}) collective-permute-start(bf16[112,512]{1,0:T(8,128)(2,1)S(1)} %collective-permute-done.13), channel_id=1, source_target_pairs={{0,15},{1,0},{2,1},{3,2},{4,3},{5,4},{6,5},{7,6},{8,7},{9,8},{10,9... | collective-permute-start | bytes 344072 | tf_op jit(solution)/shard_map/ppermute | solution.py:34
  73.6 0.6 bitcast_dynamic-update-slice_fusion.10
  74.3 1.0 collective-permute-done.6
  75.3 1.9 collective-permute-start.7
  77.2 1.7 collective-permute-done.14
  78.9 5.6 %collective-permute-start.15 = (bf16[112,512]{1,0:T(8,128)(2,1)S(1)}, bf16[112,512]{1,0:T(8,128)(2,1)S(1)}, u32[]{:S(2)}, u32[]{:S(2)}) collective-permute-start(bf16[112,512]{1,0:T(8,128)(2,1)S(1)} %collective-permute-done.14), channel_id=1, source_target_pairs={{0,15},{1,0},{2,1},{3,2},{4,3},{5,4},{6,5},{7,6},{8,7},{9,8},{10,9... | collective-permute-start | bytes 344072 | tf_op jit(solution)/shard_map/ppermute | solution.py:34
  84.5 0.7 bitcast_dynamic-update-slice_fusion.9
  85.1 1.9 collective-permute-start.8
  87.0 0.7 bitcast_dynamic-update-slice_fusion.8
  87.7 5.3 %collective-permute-done.8 = bf16[112,512]{1,0:T(8,128)(2,1)S(1)} collective-permute-done((bf16[112,512]{1,0:T(8,128)(2,1)S(1)}, bf16[112,512]{1,0:T(8,128)(2,1)S(1)}, u32[]{:S(2)}, u32[]{:S(2)}) %collective-permute-start.8) | collective-permute-done | bytes 114720 | tf_op jit(solution)/shard_map/ppermute | solution.py:31
  93.0 0.7 bitcast_dynamic-update-slice_fusion.7
  93.7 0.6 bitcast_dynamic-update-slice_fusion.6
  94.3 0.6 bitcast_dynamic-update-slice_fusion.5
  95.0 0.6 bitcast_dynamic-update-slice_fusion.4
  95.6 0.6 bitcast_dynamic-update-slice_fusion.3
  96.2 0.6 bitcast_dynamic-update-slice_fusion.2
  96.9 0.6 bitcast_dynamic-update-slice_fusion.1
  97.5 0.7 bitcast_dynamic-update-slice_fusion
  98.2 3.0 %constant_dynamic-update-slice_fusion = bf16[2,16,112,512]{3,2,1,0:T(8,128)(2,1)} fusion(bf16[2,16,112,512]{3,2,1,0:T(8,128)(2,1)} %bitcast_dynamic-update-slice_fusion, bf16[1,16,112,512]{3,2,1,0:T(8,128)(2,1)} %bitcast.45, s32[]{:T(128)S(6)} %select_n.225), kind=kLoop, calls=%fused_computation.31 | loop fusion | bytes 3670020 | tf_op jit(solution)/shard_map/dynamic_update_slice | solution.py:114
  101.2 2.7 %convolution_convert_fusion.2 = bf16[512,112]{0,1:T(8,128)(2,1)S(1)} fusion(bf16[112,3584]{1,0:T(8,128)(2,1)S(1)} %collective-permute-done.16, bf16[3584,512]{1,0:T(8,128)(2,1)} %bitcast.17), kind=kOutput, calls=%fused_computation.2 | convolution fusion | flops 411099136 | bytes 4587520 | tf_op jit(solution)/shard_map/dot_general | solution.py:118
  103.9 2.7 %select_bitcast_fusion.1 = (bf16[112,512]{1,0:T(8,128)(2,1)S(1)}, bf16[112,512]{1,0:T(8,128)(2,1)S(1)}) fusion(bf16[512,112]{0,1:T(8,128)(2,1)S(1)} %convolution_convert_fusion.2, pred[]{:T(512)S(6)} %eq.21, bf16[112,3584]{1,0:T(8,128)(2,1)S(1)} %copy-done, bf16[3584,512]{1,0:T(8,128)(2,1)} %bitcast.17), kind=kOutput, calls=%fused_computation.29 | convolution fusion | flops 411213824 | bytes 4816897 | tf_op jit(solution)/shard_map/dot_general | solution.py:117
  106.7 0.3 convolution_convert_fusion
  107.0 6.7 %all-gather.1 = bf16[448,512]{1,0:T(8,128)(2,1)S(1)} all-gather(bf16[224,512]{1,0:T(8,128)(2,1)S(1)} %pad_maximum_fusion.1), channel_id=3, replica_groups={{0,16},{1,17},{2,18},{3,19},{4,20},{5,21},{6,22},{7,23},{8,24},{9,25},{..., dimensions={0}, use_global_device_ids=true | all-gather | bytes 688128 | tf_op jit(solution)/shard_map/all_gather | solution.py:120
  113.8 0.3 convolution_convert_fusion.1
  114.1 0.9 pad_maximum_fusion
  115.0 3.5 %all-to-all-start = ((bf16[4,320,256]{2,1,0:T(8,128)(2,1)}), bf16[4,320,256]{2,1,0:T(8,128)(2,1)S(1)}, u32[]{:S(2)}, u32[]{:S(2)}) async-start(bf16[4,320,256]{2,1,0:T(8,128)(2,1)} %bitcast.20), calls=%async_computation | async-start | bytes 1310720 | tf_op jit(solution)/shard_map/all_to_all | solution.py:132
  118.5 17.9 %all-to-all-done = bf16[4,320,256]{2,1,0:T(8,128)(2,1)S(1)} async-done(((bf16[4,320,256]{2,1,0:T(8,128)(2,1)}), bf16[4,320,256]{2,1,0:T(8,128)(2,1)S(1)}, u32[]{:S(2)}, u32[]{:S(2)}) %all-to-all-start) | async-done | bytes 655392 | tf_op jit(solution)/shard_map/all_to_all | solution.py:132
  136.4 0.1 reduce_sum.24
  136.5 24.0 %all-gather.2 = bf16[1280,256]{1,0:T(8,128)(2,1)S(1)} all-gather(bf16[320,256]{1,0:T(8,128)(2,1)S(1)} %reduce_sum.24), channel_id=4, replica_groups={{0,4,8,12},{1,5,9,13},{2,6,10,14},{3,7,11,15},{16,20,24,28},{17,21,25,2..., dimensions={0}, use_global_device_ids=true | all-gather | bytes 819200 | tf_op jit(solution)/shard_map/all_gather | solution.py:136
  160.5 0.1 reduce_sum.25
  160.6 3.7 %collective-permute-start.17 = (bf16[320,256]{1,0:T(8,128)(2,1)S(1)}, bf16[320,256]{1,0:T(8,128)(2,1)S(1)}, u32[]{:S(2)}, u32[]{:S(2)}) collective-permute-start(bf16[320,256]{1,0:T(8,128)(2,1)S(1)} %reduce_sum.25), channel_id=1, source_target_pairs={{0,16},{1,17},{2,18},{3,19},{4,20},{5,21},{6,22},{7,23},{8,24},{9,... | collective-permute-start | bytes 491528 | tf_op jit(solution)/shard_map/ppermute | solution.py:138
  164.3 17.2 %all_gather.30 = bf16[1280,256]{1,0:T(8,128)(2,1)S(1)} all-gather(bf16[320,256]{1,0:T(8,128)(2,1)S(1)} %reduce_sum.25), channel_id=1, replica_groups={{0,1,2,3},{4,5,6,7},{8,9,10,11},{12,13,14,15},{16,17,18,19},{20,21,22,2..., dimensions={0}, use_global_device_ids=true | all-gather | bytes 819200 | tf_op jit(solution)/shard_map/all_gather | solution.py:139
  181.5 15.1 %all_gather.31 = bf16[1280,256]{1,0:T(8,128)(2,1)S(1)} all-gather(bf16[320,256]{1,0:T(8,128)(2,1)S(1)} %collective-permute-done.17), channel_id=1, replica_groups={{0,1,2,3},{4,5,6,7},{8,9,10,11},{12,13,14,15},{16,17,18,19},{20,21,22,2..., dimensions={0}, use_global_device_ids=true | all-gather | bytes 819200 | tf_op jit(solution)/shard_map/all_gather | solution.py:140
  196.6 0.1 broadcast_select_fusion
  196.7 1.7 finish.1
  (16 shorter events, 0.1 us)
Async XLA Ops:
  6.5 91.7 %all-gather.5.cloned.1.call-start = ((), (), s32[]{:S(2)}) async-start(), calls=%async_computation.1 | async-start | bytes 1949696 | tf_op jit(solution)/shard_map/all_gather | solution.py:102
  8.2 6.8 %collective-permute-start = (bf16[112,512]{1,0:T(8,128)(2,1)S(1)}, bf16[112,512]{1,0:T(8,128)(2,1)S(1)}, u32[]{:S(2)}, u32[]{:S(2)}) collective-permute-start(bf16[112,512]{1,0:T(8,128)(2,1)S(1)} %get-tuple-element.12), channel_id=1, source_target_pairs={{0,16},{1,17},{2,18},{3,19},{4,20},{5,21},{6,22},{7,23},{8,24},{9,... | collective-permute-start | bytes 344072 | tf_op jit(solution)/shard_map/ppermute | solution.py:103
  11.7 89.5 %collective-permute-start.16 = (bf16[112,3584]{1,0:T(8,128)(2,1)}, bf16[112,3584]{1,0:T(8,128)(2,1)S(1)}, u32[]{:S(2)}, u32[]{:S(2)}) collective-permute-start(bf16[112,3584]{1,0:T(8,128)(2,1)} %param.2), channel_id=1, source_target_pairs={{0,16},{1,17},{2,18},{3,19},{4,20},{5,21},{6,22},{7,23},{8,24},{9,... | collective-permute-start | bytes 2408456 | tf_op jit(solution)/shard_map/ppermute | solution.py:105
  14.9 16.2 %collective-permute-start.1 = (bf16[112,512]{1,0:T(8,128)(2,1)S(1)}, bf16[112,512]{1,0:T(8,128)(2,1)S(1)}, u32[]{:S(2)}, u32[]{:S(2)}) collective-permute-start(bf16[112,512]{1,0:T(8,128)(2,1)S(1)} %collective-permute-done), channel_id=1, source_target_pairs={{0,1},{1,2},{2,3},{3,4},{4,5},{5,6},{6,7},{7,8},{8,9},{9,10},{10,1... | collective-permute-start | bytes 344072 | tf_op jit(solution)/shard_map/ppermute | solution.py:31
  18.7 14.3 %collective-permute-start.9 = (bf16[112,512]{1,0:T(8,128)(2,1)S(1)}, bf16[112,512]{1,0:T(8,128)(2,1)S(1)}, u32[]{:S(2)}, u32[]{:S(2)}) collective-permute-start(bf16[112,512]{1,0:T(8,128)(2,1)S(1)} %collective-permute-done), channel_id=1, source_target_pairs={{0,15},{1,0},{2,1},{3,2},{4,3},{5,4},{6,5},{7,6},{8,7},{9,8},{10,9... | collective-permute-start | bytes 344072 | tf_op jit(solution)/shard_map/ppermute | solution.py:34
  31.1 8.1 %collective-permute-start.2 = (bf16[112,512]{1,0:T(8,128)(2,1)S(1)}, bf16[112,512]{1,0:T(8,128)(2,1)S(1)}, u32[]{:S(2)}, u32[]{:S(2)}) collective-permute-start(bf16[112,512]{1,0:T(8,128)(2,1)S(1)} %collective-permute-done.1), channel_id=1, source_target_pairs={{0,1},{1,2},{2,3},{3,4},{4,5},{5,6},{6,7},{7,8},{8,9},{9,10},{10,1... | collective-permute-start | bytes 344072 | tf_op jit(solution)/shard_map/ppermute | solution.py:31
  33.0 8.0 %collective-permute-start.10 = (bf16[112,512]{1,0:T(8,128)(2,1)S(1)}, bf16[112,512]{1,0:T(8,128)(2,1)S(1)}, u32[]{:S(2)}, u32[]{:S(2)}) collective-permute-start(bf16[112,512]{1,0:T(8,128)(2,1)S(1)} %collective-permute-done.9), channel_id=1, source_target_pairs={{0,15},{1,0},{2,1},{3,2},{4,3},{5,4},{6,5},{7,6},{8,7},{9,8},{10,9... | collective-permute-start | bytes 344072 | tf_op jit(solution)/shard_map/ppermute | solution.py:34
  39.2 8.2 %collective-permute-start.3 = (bf16[112,512]{1,0:T(8,128)(2,1)S(1)}, bf16[112,512]{1,0:T(8,128)(2,1)S(1)}, u32[]{:S(2)}, u32[]{:S(2)}) collective-permute-start(bf16[112,512]{1,0:T(8,128)(2,1)S(1)} %collective-permute-done.2), channel_id=1, source_target_pairs={{0,1},{1,2},{2,3},{3,4},{4,5},{5,6},{6,7},{7,8},{8,9},{9,10},{10,1... | collective-permute-start | bytes 344072 | tf_op jit(solution)/shard_map/ppermute | solution.py:31
  41.1 8.2 %collective-permute-start.11 = (bf16[112,512]{1,0:T(8,128)(2,1)S(1)}, bf16[112,512]{1,0:T(8,128)(2,1)S(1)}, u32[]{:S(2)}, u32[]{:S(2)}) collective-permute-start(bf16[112,512]{1,0:T(8,128)(2,1)S(1)} %collective-permute-done.10), channel_id=1, source_target_pairs={{0,15},{1,0},{2,1},{3,2},{4,3},{5,4},{6,5},{7,6},{8,7},{9,8},{10,9... | collective-permute-start | bytes 344072 | tf_op jit(solution)/shard_map/ppermute | solution.py:34
  47.4 8.2 %collective-permute-start.4 = (bf16[112,512]{1,0:T(8,128)(2,1)S(1)}, bf16[112,512]{1,0:T(8,128)(2,1)S(1)}, u32[]{:S(2)}, u32[]{:S(2)}) collective-permute-start(bf16[112,512]{1,0:T(8,128)(2,1)S(1)} %collective-permute-done.3), channel_id=1, source_target_pairs={{0,1},{1,2},{2,3},{3,4},{4,5},{5,6},{6,7},{7,8},{8,9},{9,10},{10,1... | collective-permute-start | bytes 344072 | tf_op jit(solution)/shard_map/ppermute | solution.py:31
  49.3 8.6 %collective-permute-start.12 = (bf16[112,512]{1,0:T(8,128)(2,1)S(1)}, bf16[112,512]{1,0:T(8,128)(2,1)S(1)}, u32[]{:S(2)}, u32[]{:S(2)}) collective-permute-start(bf16[112,512]{1,0:T(8,128)(2,1)S(1)} %collective-permute-done.11), channel_id=1, source_target_pairs={{0,15},{1,0},{2,1},{3,2},{4,3},{5,4},{6,5},{7,6},{8,7},{9,8},{10,9... | collective-permute-start | bytes 344072 | tf_op jit(solution)/shard_map/ppermute | solution.py:34
  55.6 9.1 %collective-permute-start.5 = (bf16[112,512]{1,0:T(8,128)(2,1)S(1)}, bf16[112,512]{1,0:T(8,128)(2,1)S(1)}, u32[]{:S(2)}, u32[]{:S(2)}) collective-permute-start(bf16[112,512]{1,0:T(8,128)(2,1)S(1)} %collective-permute-done.4), channel_id=1, source_target_pairs={{0,1},{1,2},{2,3},{3,4},{4,5},{5,6},{6,7},{7,8},{8,9},{9,10},{10,1... | collective-permute-start | bytes 344072 | tf_op jit(solution)/shard_map/ppermute | solution.py:31
  57.9 10.2 %collective-permute-start.13 = (bf16[112,512]{1,0:T(8,128)(2,1)S(1)}, bf16[112,512]{1,0:T(8,128)(2,1)S(1)}, u32[]{:S(2)}, u32[]{:S(2)}) collective-permute-start(bf16[112,512]{1,0:T(8,128)(2,1)S(1)} %collective-permute-done.12), channel_id=1, source_target_pairs={{0,15},{1,0},{2,1},{3,2},{4,3},{5,4},{6,5},{7,6},{8,7},{9,8},{10,9... | collective-permute-start | bytes 344072 | tf_op jit(solution)/shard_map/ppermute | solution.py:34
  64.7 10.5 %collective-permute-start.6 = (bf16[112,512]{1,0:T(8,128)(2,1)S(1)}, bf16[112,512]{1,0:T(8,128)(2,1)S(1)}, u32[]{:S(2)}, u32[]{:S(2)}) collective-permute-start(bf16[112,512]{1,0:T(8,128)(2,1)S(1)} %collective-permute-done.5), channel_id=1, source_target_pairs={{0,1},{1,2},{2,3},{3,4},{4,5},{5,6},{6,7},{7,8},{8,9},{9,10},{10,1... | collective-permute-start | bytes 344072 | tf_op jit(solution)/shard_map/ppermute | solution.py:31
  68.0 10.8 %collective-permute-start.14 = (bf16[112,512]{1,0:T(8,128)(2,1)S(1)}, bf16[112,512]{1,0:T(8,128)(2,1)S(1)}, u32[]{:S(2)}, u32[]{:S(2)}) collective-permute-start(bf16[112,512]{1,0:T(8,128)(2,1)S(1)} %collective-permute-done.13), channel_id=1, source_target_pairs={{0,15},{1,0},{2,1},{3,2},{4,3},{5,4},{6,5},{7,6},{8,7},{9,8},{10,9... | collective-permute-start | bytes 344072 | tf_op jit(solution)/shard_map/ppermute | solution.py:34
  75.3 9.9 %collective-permute-start.7 = (bf16[112,512]{1,0:T(8,128)(2,1)S(1)}, bf16[112,512]{1,0:T(8,128)(2,1)S(1)}, u32[]{:S(2)}, u32[]{:S(2)}) collective-permute-start(bf16[112,512]{1,0:T(8,128)(2,1)S(1)} %collective-permute-done.6), channel_id=1, source_target_pairs={{0,1},{1,2},{2,3},{3,4},{4,5},{5,6},{6,7},{7,8},{8,9},{9,10},{10,1... | collective-permute-start | bytes 344072 | tf_op jit(solution)/shard_map/ppermute | solution.py:31
  78.9 18.7 %collective-permute-start.15 = (bf16[112,512]{1,0:T(8,128)(2,1)S(1)}, bf16[112,512]{1,0:T(8,128)(2,1)S(1)}, u32[]{:S(2)}, u32[]{:S(2)}) collective-permute-start(bf16[112,512]{1,0:T(8,128)(2,1)S(1)} %collective-permute-done.14), channel_id=1, source_target_pairs={{0,15},{1,0},{2,1},{3,2},{4,3},{5,4},{6,5},{7,6},{8,7},{9,8},{10,9... | collective-permute-start | bytes 344072 | tf_op jit(solution)/shard_map/ppermute | solution.py:34
  85.1 7.9 %collective-permute-start.8 = (bf16[112,512]{1,0:T(8,128)(2,1)S(1)}, bf16[112,512]{1,0:T(8,128)(2,1)S(1)}, u32[]{:S(2)}, u32[]{:S(2)}) collective-permute-start(bf16[112,512]{1,0:T(8,128)(2,1)S(1)} %collective-permute-done.7), channel_id=1, source_target_pairs={{0,1},{1,2},{2,3},{3,4},{4,5},{5,6},{6,7},{7,8},{8,9},{9,10},{10,1... | collective-permute-start | bytes 344072 | tf_op jit(solution)/shard_map/ppermute | solution.py:31
  98.2 5.7 %copy-start = (bf16[112,3584]{1,0:T(8,128)(2,1)S(1)}, bf16[112,3584]{1,0:T(8,128)(2,1)}, u32[]{:S(2)}) copy-start(bf16[112,3584]{1,0:T(8,128)(2,1)} %param.2) | copy-start | bytes 2408452
  115.0 21.4 %all-to-all-start = ((bf16[4,320,256]{2,1,0:T(8,128)(2,1)}), bf16[4,320,256]{2,1,0:T(8,128)(2,1)S(1)}, u32[]{:S(2)}, u32[]{:S(2)}) async-start(bf16[4,320,256]{2,1,0:T(8,128)(2,1)} %bitcast.20), calls=%async_computation | async-start | bytes 1310720 | tf_op jit(solution)/shard_map/all_to_all | solution.py:132
  160.6 20.9 %collective-permute-start.17 = (bf16[320,256]{1,0:T(8,128)(2,1)S(1)}, bf16[320,256]{1,0:T(8,128)(2,1)S(1)}, u32[]{:S(2)}, u32[]{:S(2)}) collective-permute-start(bf16[320,256]{1,0:T(8,128)(2,1)S(1)} %reduce_sum.25), channel_id=1, source_target_pairs={{0,16},{1,17},{2,18},{3,19},{4,20},{5,21},{6,22},{7,23},{8,24},{9,... | collective-permute-start | bytes 491528 | tf_op jit(solution)/shard_map/ppermute | solution.py:138
Sparse Core Ops, SparseCore 0:
  11.8 78.8 all-gather.4

commit v4 on v2

--- a/solution.py
+++ b/solution.py
@@ -127,6 +127,7 @@
     blocks = jnp.concatenate(
         [square[:chunk, :chunk], square[:chunk, chunk:], square[chunk:, chunk:], strip], 0
     )
+    blocks, power = lax.optimization_barrier((blocks, power))
     parts = lax.all_to_all(
         blocks.reshape(CUBE, -1, chunk), AXIS, 0, 0, axis_index_groups=NEAR
     )
@@ -134,8 +135,15 @@
     parts = lax.all_gather(part, AXIS, axis=0, axis_index_groups=FAR)
     part = jnp.sum(parts.astype(jnp.float32), 0).astype(jnp.bfloat16)
     other_part = lax.ppermute(part, AXIS, ACROSS)
-    own_blocks = lax.all_gather(part, AXIS, axis=0, tiled=True, axis_index_groups=NEAR)
-    other_blocks = lax.all_gather(other_part, AXIS, axis=0, tiled=True, axis_index_groups=NEAR)
+    cut = part.shape[0] // 2
+
+    def near(piece):
+        return lax.all_gather(piece, AXIS, axis=0, axis_index_groups=NEAR)
+
+    head = near(part[:cut])
+    tail = near(jnp.concatenate([part[cut:], other_part], 0))
+    own_blocks = jnp.concatenate([head, tail[:, :cut]], 1).reshape(blocks.shape)
+    other_blocks = tail[:, cut:].reshape(blocks.shape)
     low = jnp.where(first_row, own_blocks, other_blocks)
     high = jnp.where(first_row, other_blocks, own_blocks)
     return finish(low, high, power, order)

time: 191 us -> 189 us (0.990)
  blocking collectives: 66 us -> 86.8 us
  waiting for transfers between devices: 44.7 us -> 26 us
  starting transfers between devices: 70.6 us -> 67.6 us
    all_to_all x0 -> x1, blocking collectives: none -> 22.2 us  [body(): lax.all_to_all(blocks.reshape(CUBE, -1, chunk), AXIS, 0, 0, axis_index_gr...]
    all_to_all x1 -> x0, waiting for transfers between devices: 18.6 us -> none  [body(): lax.all_to_all(blocks.reshape(CUBE, -1, chunk), AXIS, 0, 0, axis_index_gr...]
    all_to_all x1 -> x0, starting transfers between devices: 3.48 us -> none  [body(): lax.all_to_all(blocks.reshape(CUBE, -1, chunk), AXIS, 0, 0, axis_index_gr...]
  transfers between devices with their start and end apart: 19 -> 18, of which waited for: 10 -> 9; matrix products, arithmetic and copies ran while one was open for 0% -> 0% of each run, Pallas kernels for 0% -> 0%
where the time goes in v4:
time: 189 us; the launch traced here: 188 us
  blocking collectives  86.8 us (46%)
  starting transfers between devices  67.6 us (36%)
  waiting for transfers between devices  26 us (14%)
  local copies, waits for them, and re-layouts  1.99 us (1%)
  matrix products  1.95 us (1%)
    ppermute x7, starting transfers between devices, ring(): b = lax.ppermute(b, AXIS, shift(-1))  41 us
    all_gather x2, blocking collectives, near(): return lax.all_gather(piece, AXIS, axis=0, axis_index_groups=NEAR)  31.1 us
    all_gather x1, blocking collectives, body(): parts = lax.all_gather(part, AXIS, axis=0, axis_index_groups=FAR)  26.8 us
    ppermute x8, waiting for transfers between devices, ring(): a = lax.ppermute(a, AXIS, shift(1))  22.6 us
    all_to_all x1, blocking collectives, body(): lax.all_to_all(blocks.reshape(CUBE, -1, chunk), AXIS, 0, 0, axis_index_gr...  22.2 us
    ppermute x8, starting transfers between devices, ring(): a = lax.ppermute(a, AXIS, shift(1))  17.2 us
    all_gather x1, blocking collectives, body(): both = lax.all_gather(tile, AXIS, axis=0, axis_index_groups=PAIRS)  6.7 us
  transfers between devices with their start and end apart: 18, of which 9 were waited for; matrix products, arithmetic and copies ran while one was open for 0% of the time, Pallas kernels for 0%

profile of v4, /device:TPU:6, one launch (start us, length us, event | category | flops | bytes accessed | tf_op | source)
XLA Modules:
  0.0 188.4 jit_solution(12391934352543897864)
XLA Ops:
  0.0 0.9 constant_dynamic-slice_fusion
  0.9 3.5 %collective-permute-start = (bf16[112,512]{1,0:T(8,128)(2,1)S(1)}, bf16[112,512]{1,0:T(8,128)(2,1)S(1)}, u32[]{:S(2)}, u32[]{:S(2)}) collective-permute-start(bf16[112,512]{1,0:T(8,128)(2,1)S(1)} %constant_dynamic-slice_fusion), channel_id=1, source_target_pairs={{0,16},{1,17},{2,18},{3,19},{4,20},{5,21},{6,22},{7,23},{8,24},{9,... | collective-permute-start | bytes 344072 | tf_op jit(solution)/shard_map/ppermute | solution.py:101
  4.4 3.3 %collective-permute-done = bf16[112,512]{1,0:T(8,128)(2,1)S(1)} collective-permute-done((bf16[112,512]{1,0:T(8,128)(2,1)S(1)}, bf16[112,512]{1,0:T(8,128)(2,1)S(1)}, u32[]{:S(2)}, u32[]{:S(2)}) %collective-permute-start) | collective-permute-done | bytes 114720 | tf_op jit(solution)/shard_map/ppermute | solution.py:101
  7.7 0.9 select_bitcast_fusion.3
  8.6 3.8 %collective-permute-start.1 = (bf16[2,112,512]{2,1,0:T(8,128)(2,1)S(1)}, bf16[2,112,512]{2,1,0:T(8,128)(2,1)S(1)}, u32[]{:S(2)}, u32[]{:S(2)}) collective-permute-start(bf16[2,112,512]{2,1,0:T(8,128)(2,1)S(1)} %pad_maximum_fusion.3), channel_id=1, source_target_pairs={{0,1},{1,2},{2,3},{3,4},{4,5},{5,6},{6,7},{7,8},{8,9},{9,10},{10,1... | collective-permute-start | bytes 688136 | tf_op jit(solution)/shard_map/ppermute | solution.py:30
  12.5 9.5 %collective-permute-start.9 = (bf16[2,112,512]{2,1,0:T(8,128)(2,1)S(1)}, bf16[2,112,512]{2,1,0:T(8,128)(2,1)S(1)}, u32[]{:S(2)}, u32[]{:S(2)}) collective-permute-start(bf16[2,112,512]{2,1,0:T(8,128)(2,1)S(1)} %pad_maximum_fusion.3), channel_id=1, source_target_pairs={{0,15},{1,0},{2,1},{3,2},{4,3},{5,4},{6,5},{7,6},{8,7},{9,8},{10,9... | collective-permute-start | bytes 688136 | tf_op jit(solution)/shard_map/ppermute | solution.py:33
  22.0 3.5 %collective-permute-start.16 = (bf16[112,3584]{1,0:T(8,128)(2,1)}, bf16[112,3584]{1,0:T(8,128)(2,1)S(1)}, u32[]{:S(2)}, u32[]{:S(2)}) collective-permute-start(bf16[112,3584]{1,0:T(8,128)(2,1)} %param.2), channel_id=1, source_target_pairs={{0,16},{1,17},{2,18},{3,19},{4,20},{5,21},{6,22},{7,23},{8,24},{9,... | collective-permute-start | bytes 2408456 | tf_op jit(solution)/shard_map/ppermute | solution.py:104
  25.8 0.4 broadcast_in_dim.51
  26.3 0.0 collective-permute-done.1
  26.3 1.9 %collective-permute-start.2 = (bf16[2,112,512]{2,1,0:T(8,128)(2,1)S(1)}, bf16[2,112,512]{2,1,0:T(8,128)(2,1)S(1)}, u32[]{:S(2)}, u32[]{:S(2)}) collective-permute-start(bf16[2,112,512]{2,1,0:T(8,128)(2,1)S(1)} %collective-permute-done.1), channel_id=1, source_target_pairs={{0,1},{1,2},{2,3},{3,4},{4,5},{5,6},{6,7},{7,8},{8,9},{9,10},{10,1... | collective-permute-start | bytes 688136 | tf_op jit(solution)/shard_map/ppermute | solution.py:30
  28.2 0.0 collective-permute-done.9
  28.2 5.1 %collective-permute-start.10 = (bf16[2,112,512]{2,1,0:T(8,128)(2,1)S(1)}, bf16[2,112,512]{2,1,0:T(8,128)(2,1)S(1)}, u32[]{:S(2)}, u32[]{:S(2)}) collective-permute-start(bf16[2,112,512]{2,1,0:T(8,128)(2,1)S(1)} %collective-permute-done.9), channel_id=1, source_target_pairs={{0,15},{1,0},{2,1},{3,2},{4,3},{5,4},{6,5},{7,6},{8,7},{9,8},{10,9... | collective-permute-start | bytes 688136 | tf_op jit(solution)/shard_map/ppermute | solution.py:33
  33.4 2.0 %collective-permute-done.2 = bf16[2,112,512]{2,1,0:T(8,128)(2,1)S(1)} collective-permute-done((bf16[2,112,512]{2,1,0:T(8,128)(2,1)S(1)}, bf16[2,112,512]{2,1,0:T(8,128)(2,1)S(1)}, u32[]{:S(2)}, u32[]{:S(2)}) %collective-permute-start.2) | collective-permute-done | bytes 229408 | tf_op jit(solution)/shard_map/ppermute | solution.py:30
  35.4 1.9 %collective-permute-start.3 = (bf16[2,112,512]{2,1,0:T(8,128)(2,1)S(1)}, bf16[2,112,512]{2,1,0:T(8,128)(2,1)S(1)}, u32[]{:S(2)}, u32[]{:S(2)}) collective-permute-start(bf16[2,112,512]{2,1,0:T(8,128)(2,1)S(1)} %collective-permute-done.2), channel_id=1, source_target_pairs={{0,1},{1,2},{2,3},{3,4},{4,5},{5,6},{6,7},{7,8},{8,9},{9,10},{10,1... | collective-permute-start | bytes 688136 | tf_op jit(solution)/shard_map/ppermute | solution.py:30
  37.3 0.0 collective-permute-done.10
  37.3 5.1 %collective-permute-start.11 = (bf16[2,112,512]{2,1,0:T(8,128)(2,1)S(1)}, bf16[2,112,512]{2,1,0:T(8,128)(2,1)S(1)}, u32[]{:S(2)}, u32[]{:S(2)}) collective-permute-start(bf16[2,112,512]{2,1,0:T(8,128)(2,1)S(1)} %collective-permute-done.10), channel_id=1, source_target_pairs={{0,15},{1,0},{2,1},{3,2},{4,3},{5,4},{6,5},{7,6},{8,7},{9,8},{10,9... | collective-permute-start | bytes 688136 | tf_op jit(solution)/shard_map/ppermute | solution.py:33
  42.5 2.0 %collective-permute-done.3 = bf16[2,112,512]{2,1,0:T(8,128)(2,1)S(1)} collective-permute-done((bf16[2,112,512]{2,1,0:T(8,128)(2,1)S(1)}, bf16[2,112,512]{2,1,0:T(8,128)(2,1)S(1)}, u32[]{:S(2)}, u32[]{:S(2)}) %collective-permute-start.3) | collective-permute-done | bytes 229408 | tf_op jit(solution)/shard_map/ppermute | solution.py:30
  44.5 1.9 %collective-permute-start.4 = (bf16[2,112,512]{2,1,0:T(8,128)(2,1)S(1)}, bf16[2,112,512]{2,1,0:T(8,128)(2,1)S(1)}, u32[]{:S(2)}, u32[]{:S(2)}) collective-permute-start(bf16[2,112,512]{2,1,0:T(8,128)(2,1)S(1)} %collective-permute-done.3), channel_id=1, source_target_pairs={{0,1},{1,2},{2,3},{3,4},{4,5},{5,6},{6,7},{7,8},{8,9},{9,10},{10,1... | collective-permute-start | bytes 688136 | tf_op jit(solution)/shard_map/ppermute | solution.py:30
  46.4 0.0 collective-permute-done.11
  46.5 5.1 %collective-permute-start.12 = (bf16[2,112,512]{2,1,0:T(8,128)(2,1)S(1)}, bf16[2,112,512]{2,1,0:T(8,128)(2,1)S(1)}, u32[]{:S(2)}, u32[]{:S(2)}) collective-permute-start(bf16[2,112,512]{2,1,0:T(8,128)(2,1)S(1)} %collective-permute-done.11), channel_id=1, source_target_pairs={{0,15},{1,0},{2,1},{3,2},{4,3},{5,4},{6,5},{7,6},{8,7},{9,8},{10,9... | collective-permute-start | bytes 688136 | tf_op jit(solution)/shard_map/ppermute | solution.py:33
  51.6 2.0 %collective-permute-done.4 = bf16[2,112,512]{2,1,0:T(8,128)(2,1)S(1)} collective-permute-done((bf16[2,112,512]{2,1,0:T(8,128)(2,1)S(1)}, bf16[2,112,512]{2,1,0:T(8,128)(2,1)S(1)}, u32[]{:S(2)}, u32[]{:S(2)}) %collective-permute-start.4) | collective-permute-done | bytes 229408 | tf_op jit(solution)/shard_map/ppermute | solution.py:30
  53.6 1.9 %collective-permute-start.5 = (bf16[2,112,512]{2,1,0:T(8,128)(2,1)S(1)}, bf16[2,112,512]{2,1,0:T(8,128)(2,1)S(1)}, u32[]{:S(2)}, u32[]{:S(2)}) collective-permute-start(bf16[2,112,512]{2,1,0:T(8,128)(2,1)S(1)} %collective-permute-done.4), channel_id=1, source_target_pairs={{0,1},{1,2},{2,3},{3,4},{4,5},{5,6},{6,7},{7,8},{8,9},{9,10},{10,1... | collective-permute-start | bytes 688136 | tf_op jit(solution)/shard_map/ppermute | solution.py:30
  55.6 0.0 collective-permute-done.12
  55.6 5.1 %collective-permute-start.13 = (bf16[2,112,512]{2,1,0:T(8,128)(2,1)S(1)}, bf16[2,112,512]{2,1,0:T(8,128)(2,1)S(1)}, u32[]{:S(2)}, u32[]{:S(2)}) collective-permute-start(bf16[2,112,512]{2,1,0:T(8,128)(2,1)S(1)} %collective-permute-done.12), channel_id=1, source_target_pairs={{0,15},{1,0},{2,1},{3,2},{4,3},{5,4},{6,5},{7,6},{8,7},{9,8},{10,9... | collective-permute-start | bytes 688136 | tf_op jit(solution)/shard_map/ppermute | solution.py:33
  60.7 2.5 %collective-permute-done.5 = bf16[2,112,512]{2,1,0:T(8,128)(2,1)S(1)} collective-permute-done((bf16[2,112,512]{2,1,0:T(8,128)(2,1)S(1)}, bf16[2,112,512]{2,1,0:T(8,128)(2,1)S(1)}, u32[]{:S(2)}, u32[]{:S(2)}) %collective-permute-start.5) | collective-permute-done | bytes 229408 | tf_op jit(solution)/shard_map/ppermute | solution.py:30
  63.2 1.9 %collective-permute-start.6 = (bf16[2,112,512]{2,1,0:T(8,128)(2,1)S(1)}, bf16[2,112,512]{2,1,0:T(8,128)(2,1)S(1)}, u32[]{:S(2)}, u32[]{:S(2)}) collective-permute-start(bf16[2,112,512]{2,1,0:T(8,128)(2,1)S(1)} %collective-permute-done.5), channel_id=1, source_target_pairs={{0,1},{1,2},{2,3},{3,4},{4,5},{5,6},{6,7},{7,8},{8,9},{9,10},{10,1... | collective-permute-start | bytes 688136 | tf_op jit(solution)/shard_map/ppermute | solution.py:30
  65.1 0.0 collective-permute-done.13
  65.1 5.4 %collective-permute-start.14 = (bf16[2,112,512]{2,1,0:T(8,128)(2,1)S(1)}, bf16[2,112,512]{2,1,0:T(8,128)(2,1)S(1)}, u32[]{:S(2)}, u32[]{:S(2)}) collective-permute-start(bf16[2,112,512]{2,1,0:T(8,128)(2,1)S(1)} %collective-permute-done.13), channel_id=1, source_target_pairs={{0,15},{1,0},{2,1},{3,2},{4,3},{5,4},{6,5},{7,6},{8,7},{9,8},{10,9... | collective-permute-start | bytes 688136 | tf_op jit(solution)/shard_map/ppermute | solution.py:33
  70.6 3.3 %collective-permute-done.6 = bf16[2,112,512]{2,1,0:T(8,128)(2,1)S(1)} collective-permute-done((bf16[2,112,512]{2,1,0:T(8,128)(2,1)S(1)}, bf16[2,112,512]{2,1,0:T(8,128)(2,1)S(1)}, u32[]{:S(2)}, u32[]{:S(2)}) %collective-permute-start.6) | collective-permute-done | bytes 229408 | tf_op jit(solution)/shard_map/ppermute | solution.py:30
  73.9 1.9 %collective-permute-start.7 = (bf16[2,112,512]{2,1,0:T(8,128)(2,1)S(1)}, bf16[2,112,512]{2,1,0:T(8,128)(2,1)S(1)}, u32[]{:S(2)}, u32[]{:S(2)}) collective-permute-start(bf16[2,112,512]{2,1,0:T(8,128)(2,1)S(1)} %collective-permute-done.6), channel_id=1, source_target_pairs={{0,1},{1,2},{2,3},{3,4},{4,5},{5,6},{6,7},{7,8},{8,9},{9,10},{10,1... | collective-permute-start | bytes 688136 | tf_op jit(solution)/shard_map/ppermute | solution.py:30
  75.8 0.2 collective-permute-done.14
  76.0 5.6 %collective-permute-start.15 = (bf16[2,112,512]{2,1,0:T(8,128)(2,1)S(1)}, bf16[2,112,512]{2,1,0:T(8,128)(2,1)S(1)}, u32[]{:S(2)}, u32[]{:S(2)}) collective-permute-start(bf16[2,112,512]{2,1,0:T(8,128)(2,1)S(1)} %collective-permute-done.14), channel_id=1, source_target_pairs={{0,15},{1,0},{2,1},{3,2},{4,3},{5,4},{6,5},{7,6},{8,7},{9,8},{10,9... | collective-permute-start | bytes 688136 | tf_op jit(solution)/shard_map/ppermute | solution.py:33
  81.6 3.6 %collective-permute-done.7 = bf16[2,112,512]{2,1,0:T(8,128)(2,1)S(1)} collective-permute-done((bf16[2,112,512]{2,1,0:T(8,128)(2,1)S(1)}, bf16[2,112,512]{2,1,0:T(8,128)(2,1)S(1)}, u32[]{:S(2)}, u32[]{:S(2)}) %collective-permute-start.7) | collective-permute-done | bytes 229408 | tf_op jit(solution)/shard_map/ppermute | solution.py:30
  85.2 1.9 %collective-permute-start.8 = (bf16[2,112,512]{2,1,0:T(8,128)(2,1)S(1)}, bf16[2,112,512]{2,1,0:T(8,128)(2,1)S(1)}, u32[]{:S(2)}, u32[]{:S(2)}) collective-permute-start(bf16[2,112,512]{2,1,0:T(8,128)(2,1)S(1)} %collective-permute-done.7), channel_id=1, source_target_pairs={{0,1},{1,2},{2,3},{3,4},{4,5},{5,6},{6,7},{7,8},{8,9},{9,10},{10,1... | collective-permute-start | bytes 688136 | tf_op jit(solution)/shard_map/ppermute | solution.py:30
  87.1 7.2 %collective-permute-done.8 = bf16[2,112,512]{2,1,0:T(8,128)(2,1)S(1)} collective-permute-done((bf16[2,112,512]{2,1,0:T(8,128)(2,1)S(1)}, bf16[2,112,512]{2,1,0:T(8,128)(2,1)S(1)}, u32[]{:S(2)}, u32[]{:S(2)}) %collective-permute-start.8) | collective-permute-done | bytes 229408 | tf_op jit(solution)/shard_map/ppermute | solution.py:30
  94.4 0.0 copy-start
  94.5 0.0 collective-permute-done.15
  94.6 0.0 collective-permute-done.16
  94.6 0.7 convolution_convert_fusion.2
  95.3 0.2 copy-done
  95.5 0.7 select_bitcast_fusion.1
  96.2 0.3 convolution_convert_fusion
  96.6 6.7 %all-gather = bf16[448,512]{1,0:T(8,128)(2,1)S(1)} all-gather(bf16[224,512]{1,0:T(8,128)(2,1)S(1)} %pad_maximum_fusion.4), channel_id=2, replica_groups={{0,16},{1,17},{2,18},{3,19},{4,20},{5,21},{6,22},{7,23},{8,24},{9,25},{..., dimensions={0}, use_global_device_ids=true | all-gather | bytes 688128 | tf_op jit(solution)/shard_map/all_gather | solution.py:118
  103.3 0.3 convolution_convert_fusion.1
  103.7 22.2 %all_to_all.5 = bf16[4,320,256]{2,1,0:T(8,128)(2,1)S(1)} all-to-all(bf16[4,320,256]{2,1,0:T(8,128)(2,1)S(1)} %bitcast.87), channel_id=1, replica_groups={{0,1,2,3},{4,5,6,7},{8,9,10,11},{12,13,14,15},{16,17,18,19},{20,21,22,2..., dimensions={0} | all-to-all | bytes 1310720 | tf_op jit(solution)/shard_map/all_to_all | solution.py:131
  125.9 0.1 reduce_sum.24
  126.0 26.8 %all-gather.1 = bf16[1280,256]{1,0:T(8,128)(2,1)S(1)} all-gather(bf16[320,256]{1,0:T(8,128)(2,1)S(1)} %reduce_sum.24), channel_id=3, replica_groups={{0,4,8,12},{1,5,9,13},{2,6,10,14},{3,7,11,15},{16,20,24,28},{17,21,25,2..., dimensions={0}, use_global_device_ids=true | all-gather | bytes 819200 | tf_op jit(solution)/shard_map/all_gather | solution.py:135
  152.8 0.1 reduce_sum.25
  153.0 2.4 %collective-permute-start.17 = (bf16[320,256]{1,0:T(8,128)(2,1)S(1)}, bf16[320,256]{1,0:T(8,128)(2,1)S(1)}, u32[]{:S(2)}, u32[]{:S(2)}) collective-permute-start(bf16[320,256]{1,0:T(8,128)(2,1)S(1)} %reduce_sum.25), channel_id=1, source_target_pairs={{0,16},{1,17},{2,18},{3,19},{4,20},{5,21},{6,22},{7,23},{8,24},{9,... | collective-permute-start | bytes 491528 | tf_op jit(solution)/shard_map/ppermute | solution.py:137
  155.4 14.8 %all-gather.2 = bf16[640,256]{1,0:T(8,128)(2,1)S(1)} all-gather(bf16[160,256]{1,0:T(8,128)(2,1)S(1)} %get-tuple-element.17), channel_id=4, replica_groups={{0,1,2,3},{4,5,6,7},{8,9,10,11},{12,13,14,15},{16,17,18,19},{20,21,22,2..., dimensions={0}, use_global_device_ids=true | all-gather | bytes 409600 | tf_op jit(solution)/shard_map/all_gather | solution.py:141
  170.1 0.0 collective-permute-done.17
  170.2 16.3 %all-gather.3 = bf16[1920,256]{1,0:T(8,128)(2,1)S(1)} all-gather(bf16[480,256]{1,0:T(8,128)(2,1)S(1)} %pad_maximum_fusion.2), channel_id=5, replica_groups={{0,1,2,3},{4,5,6,7},{8,9,10,11},{12,13,14,15},{16,17,18,19},{20,21,22,2..., dimensions={0}, use_global_device_ids=true | all-gather | bytes 1228800 | tf_op jit(solution)/shard_map/all_gather | solution.py:141
  186.5 0.3 broadcast_select_fusion
  186.8 1.7 finish.1
  (26 shorter events, 0.6 us)
Async XLA Ops:
  0.9 6.8 %collective-permute-start = (bf16[112,512]{1,0:T(8,128)(2,1)S(1)}, bf16[112,512]{1,0:T(8,128)(2,1)S(1)}, u32[]{:S(2)}, u32[]{:S(2)}) collective-permute-start(bf16[112,512]{1,0:T(8,128)(2,1)S(1)} %constant_dynamic-slice_fusion), channel_id=1, source_target_pairs={{0,16},{1,17},{2,18},{3,19},{4,20},{5,21},{6,22},{7,23},{8,24},{9,... | collective-permute-start | bytes 344072 | tf_op jit(solution)/shard_map/ppermute | solution.py:101
  8.6 17.6 %collective-permute-start.1 = (bf16[2,112,512]{2,1,0:T(8,128)(2,1)S(1)}, bf16[2,112,512]{2,1,0:T(8,128)(2,1)S(1)}, u32[]{:S(2)}, u32[]{:S(2)}) collective-permute-start(bf16[2,112,512]{2,1,0:T(8,128)(2,1)S(1)} %pad_maximum_fusion.3), channel_id=1, source_target_pairs={{0,1},{1,2},{2,3},{3,4},{4,5},{5,6},{6,7},{7,8},{8,9},{9,10},{10,1... | collective-permute-start | bytes 688136 | tf_op jit(solution)/shard_map/ppermute | solution.py:30
  12.5 15.7 %collective-permute-start.9 = (bf16[2,112,512]{2,1,0:T(8,128)(2,1)S(1)}, bf16[2,112,512]{2,1,0:T(8,128)(2,1)S(1)}, u32[]{:S(2)}, u32[]{:S(2)}) collective-permute-start(bf16[2,112,512]{2,1,0:T(8,128)(2,1)S(1)} %pad_maximum_fusion.3), channel_id=1, source_target_pairs={{0,15},{1,0},{2,1},{3,2},{4,3},{5,4},{6,5},{7,6},{8,7},{9,8},{10,9... | collective-permute-start | bytes 688136 | tf_op jit(solution)/shard_map/ppermute | solution.py:33
  22.0 72.6 %collective-permute-start.16 = (bf16[112,3584]{1,0:T(8,128)(2,1)}, bf16[112,3584]{1,0:T(8,128)(2,1)S(1)}, u32[]{:S(2)}, u32[]{:S(2)}) collective-permute-start(bf16[112,3584]{1,0:T(8,128)(2,1)} %param.2), channel_id=1, source_target_pairs={{0,16},{1,17},{2,18},{3,19},{4,20},{5,21},{6,22},{7,23},{8,24},{9,... | collective-permute-start | bytes 2408456 | tf_op jit(solution)/shard_map/ppermute | solution.py:104
  26.3 9.1 %collective-permute-start.2 = (bf16[2,112,512]{2,1,0:T(8,128)(2,1)S(1)}, bf16[2,112,512]{2,1,0:T(8,128)(2,1)S(1)}, u32[]{:S(2)}, u32[]{:S(2)}) collective-permute-start(bf16[2,112,512]{2,1,0:T(8,128)(2,1)S(1)} %collective-permute-done.1), channel_id=1, source_target_pairs={{0,1},{1,2},{2,3},{3,4},{4,5},{5,6},{6,7},{7,8},{8,9},{9,10},{10,1... | collective-permute-start | bytes 688136 | tf_op jit(solution)/shard_map/ppermute | solution.py:30
  28.2 9.1 %collective-permute-start.10 = (bf16[2,112,512]{2,1,0:T(8,128)(2,1)S(1)}, bf16[2,112,512]{2,1,0:T(8,128)(2,1)S(1)}, u32[]{:S(2)}, u32[]{:S(2)}) collective-permute-start(bf16[2,112,512]{2,1,0:T(8,128)(2,1)S(1)} %collective-permute-done.9), channel_id=1, source_target_pairs={{0,15},{1,0},{2,1},{3,2},{4,3},{5,4},{6,5},{7,6},{8,7},{9,8},{10,9... | collective-permute-start | bytes 688136 | tf_op jit(solution)/shard_map/ppermute | solution.py:33
  35.4 9.1 %collective-permute-start.3 = (bf16[2,112,512]{2,1,0:T(8,128)(2,1)S(1)}, bf16[2,112,512]{2,1,0:T(8,128)(2,1)S(1)}, u32[]{:S(2)}, u32[]{:S(2)}) collective-permute-start(bf16[2,112,512]{2,1,0:T(8,128)(2,1)S(1)} %collective-permute-done.2), channel_id=1, source_target_pairs={{0,1},{1,2},{2,3},{3,4},{4,5},{5,6},{6,7},{7,8},{8,9},{9,10},{10,1... | collective-permute-start | bytes 688136 | tf_op jit(solution)/shard_map/ppermute | solution.py:30
  37.3 9.1 %collective-permute-start.11 = (bf16[2,112,512]{2,1,0:T(8,128)(2,1)S(1)}, bf16[2,112,512]{2,1,0:T(8,128)(2,1)S(1)}, u32[]{:S(2)}, u32[]{:S(2)}) collective-permute-start(bf16[2,112,512]{2,1,0:T(8,128)(2,1)S(1)} %collective-permute-done.10), channel_id=1, source_target_pairs={{0,15},{1,0},{2,1},{3,2},{4,3},{5,4},{6,5},{7,6},{8,7},{9,8},{10,9... | collective-permute-start | bytes 688136 | tf_op jit(solution)/shard_map/ppermute | solution.py:33
  44.5 9.1 %collective-permute-start.4 = (bf16[2,112,512]{2,1,0:T(8,128)(2,1)S(1)}, bf16[2,112,512]{2,1,0:T(8,128)(2,1)S(1)}, u32[]{:S(2)}, u32[]{:S(2)}) collective-permute-start(bf16[2,112,512]{2,1,0:T(8,128)(2,1)S(1)} %collective-permute-done.3), channel_id=1, source_target_pairs={{0,1},{1,2},{2,3},{3,4},{4,5},{5,6},{6,7},{7,8},{8,9},{9,10},{10,1... | collective-permute-start | bytes 688136 | tf_op jit(solution)/shard_map/ppermute | solution.py:30
  46.5 9.1 %collective-permute-start.12 = (bf16[2,112,512]{2,1,0:T(8,128)(2,1)S(1)}, bf16[2,112,512]{2,1,0:T(8,128)(2,1)S(1)}, u32[]{:S(2)}, u32[]{:S(2)}) collective-permute-start(bf16[2,112,512]{2,1,0:T(8,128)(2,1)S(1)} %collective-permute-done.11), channel_id=1, source_target_pairs={{0,15},{1,0},{2,1},{3,2},{4,3},{5,4},{6,5},{7,6},{8,7},{9,8},{10,9... | collective-permute-start | bytes 688136 | tf_op jit(solution)/shard_map/ppermute | solution.py:33
  53.6 9.6 %collective-permute-start.5 = (bf16[2,112,512]{2,1,0:T(8,128)(2,1)S(1)}, bf16[2,112,512]{2,1,0:T(8,128)(2,1)S(1)}, u32[]{:S(2)}, u32[]{:S(2)}) collective-permute-start(bf16[2,112,512]{2,1,0:T(8,128)(2,1)S(1)} %collective-permute-done.4), channel_id=1, source_target_pairs={{0,1},{1,2},{2,3},{3,4},{4,5},{5,6},{6,7},{7,8},{8,9},{9,10},{10,1... | collective-permute-start | bytes 688136 | tf_op jit(solution)/shard_map/ppermute | solution.py:30
  55.6 9.5 %collective-permute-start.13 = (bf16[2,112,512]{2,1,0:T(8,128)(2,1)S(1)}, bf16[2,112,512]{2,1,0:T(8,128)(2,1)S(1)}, u32[]{:S(2)}, u32[]{:S(2)}) collective-permute-start(bf16[2,112,512]{2,1,0:T(8,128)(2,1)S(1)} %collective-permute-done.12), channel_id=1, source_target_pairs={{0,15},{1,0},{2,1},{3,2},{4,3},{5,4},{6,5},{7,6},{8,7},{9,8},{10,9... | collective-permute-start | bytes 688136 | tf_op jit(solution)/shard_map/ppermute | solution.py:33
  63.2 10.7 %collective-permute-start.6 = (bf16[2,112,512]{2,1,0:T(8,128)(2,1)S(1)}, bf16[2,112,512]{2,1,0:T(8,128)(2,1)S(1)}, u32[]{:S(2)}, u32[]{:S(2)}) collective-permute-start(bf16[2,112,512]{2,1,0:T(8,128)(2,1)S(1)} %collective-permute-done.5), channel_id=1, source_target_pairs={{0,1},{1,2},{2,3},{3,4},{4,5},{5,6},{6,7},{7,8},{8,9},{9,10},{10,1... | collective-permute-start | bytes 688136 | tf_op jit(solution)/shard_map/ppermute | solution.py:30
  65.1 10.9 %collective-permute-start.14 = (bf16[2,112,512]{2,1,0:T(8,128)(2,1)S(1)}, bf16[2,112,512]{2,1,0:T(8,128)(2,1)S(1)}, u32[]{:S(2)}, u32[]{:S(2)}) collective-permute-start(bf16[2,112,512]{2,1,0:T(8,128)(2,1)S(1)} %collective-permute-done.13), channel_id=1, source_target_pairs={{0,15},{1,0},{2,1},{3,2},{4,3},{5,4},{6,5},{7,6},{8,7},{9,8},{10,9... | collective-permute-start | bytes 688136 | tf_op jit(solution)/shard_map/ppermute | solution.py:33
  73.9 11.3 %collective-permute-start.7 = (bf16[2,112,512]{2,1,0:T(8,128)(2,1)S(1)}, bf16[2,112,512]{2,1,0:T(8,128)(2,1)S(1)}, u32[]{:S(2)}, u32[]{:S(2)}) collective-permute-start(bf16[2,112,512]{2,1,0:T(8,128)(2,1)S(1)} %collective-permute-done.6), channel_id=1, source_target_pairs={{0,1},{1,2},{2,3},{3,4},{4,5},{5,6},{6,7},{7,8},{8,9},{9,10},{10,1... | collective-permute-start | bytes 688136 | tf_op jit(solution)/shard_map/ppermute | solution.py:30
  76.0 18.5 %collective-permute-start.15 = (bf16[2,112,512]{2,1,0:T(8,128)(2,1)S(1)}, bf16[2,112,512]{2,1,0:T(8,128)(2,1)S(1)}, u32[]{:S(2)}, u32[]{:S(2)}) collective-permute-start(bf16[2,112,512]{2,1,0:T(8,128)(2,1)S(1)} %collective-permute-done.14), channel_id=1, source_target_pairs={{0,15},{1,0},{2,1},{3,2},{4,3},{5,4},{6,5},{7,6},{8,7},{9,8},{10,9... | collective-permute-start | bytes 688136 | tf_op jit(solution)/shard_map/ppermute | solution.py:33
  85.2 9.1 %collective-permute-start.8 = (bf16[2,112,512]{2,1,0:T(8,128)(2,1)S(1)}, bf16[2,112,512]{2,1,0:T(8,128)(2,1)S(1)}, u32[]{:S(2)}, u32[]{:S(2)}) collective-permute-start(bf16[2,112,512]{2,1,0:T(8,128)(2,1)S(1)} %collective-permute-done.7), channel_id=1, source_target_pairs={{0,1},{1,2},{2,3},{3,4},{4,5},{5,6},{6,7},{7,8},{8,9},{9,10},{10,1... | collective-permute-start | bytes 688136 | tf_op jit(solution)/shard_map/ppermute | solution.py:30
  94.4 1.1 copy-start
  153.0 17.2 %collective-permute-start.17 = (bf16[320,256]{1,0:T(8,128)(2,1)S(1)}, bf16[320,256]{1,0:T(8,128)(2,1)S(1)}, u32[]{:S(2)}, u32[]{:S(2)}) collective-permute-start(bf16[320,256]{1,0:T(8,128)(2,1)S(1)} %reduce_sum.25), channel_id=1, source_target_pairs={{0,16},{1,17},{2,18},{3,19},{4,20},{5,21},{6,22},{7,23},{8,24},{9,... | collective-permute-start | bytes 491528 | tf_op jit(solution)/shard_map/ppermute | solution.py:137

commit v5 on v4

--- a/solution.py
+++ b/solution.py
@@ -24,14 +24,12 @@
 
 
 def ring(block):
-    up, down = [], []
-    a = b = block
-    for step in range(Z // 2):
-        a = lax.ppermute(a, AXIS, shift(1))
-        up.append(a)
-        if step < Z // 2 - 1:
-            b = lax.ppermute(b, AXIS, shift(-1))
-            down.append(b)
+    half_way = Z // 2
+    up, down = [lax.ppermute(block, AXIS, shift(1))], [lax.ppermute(block, AXIS, shift(-1))]
+    down.append(lax.ppermute(block, AXIS, shift(-2)))
+    for _ in range(half_way - 2):
+        up.append(lax.ppermute(up[-1], AXIS, shift(1)))
+        down.append(lax.ppermute(down[-1], AXIS, shift(-1)))
     return up, down
 
 
@@ -101,9 +99,10 @@
     other = lax.ppermute(other, AXIS, ACROSS)
     first_row = y == 0
     block = jnp.stack([jnp.where(first_row, mine, other), jnp.where(first_row, other, mine)])
-    far_rows = lax.ppermute(factor_rows, AXIS, ACROSS)
 
     up, down = ring(block)
+    sent_rows, up[0] = lax.optimization_barrier((factor_rows, up[0]))
+    far_rows = lax.ppermute(sent_rows, AXIS, ACROSS)
     full = jnp.zeros((2, Z, rows, half), basis.dtype)
     full = place(full, block, z)
     for step, part in enumerate(up):

time: 189 us -> 191 us (1.011)
  waiting for transfers between devices: 26 us -> 15.9 us
  blocking collectives: 86.8 us -> 93.7 us
  starting transfers between devices: 67.6 us -> 72.1 us
    all_gather x1, blocking collectives: 26.8 us -> 40.8 us  [body(): parts = lax.all_gather(part, AXIS, axis=0, axis_index_groups=FAR)]
    ppermute x16, waiting for transfers between devices: 22.8 us -> 12.7 us  [the longest x6 10.6 us: ring(): up.append(lax.ppermute(up[-1], AXIS, shift(1)))]
    all_to_all x1, blocking collectives: 22.2 us -> 15.7 us  [body(): lax.all_to_all(blocks.reshape(CUBE, -1, chunk), AXIS, 0, 0, axis_index_gr...]
    ppermute x16, starting transfers between devices: 61.7 us -> 65.4 us  [the longest x6 31.8 us: ring(): down.append(lax.ppermute(down[-1], AXIS, shift(-1)))]
  transfers between devices with their start and end apart: 18 -> 18, of which waited for: 9 -> 12; matrix products, arithmetic and copies ran while one was open for 0% -> 0% of each run, Pallas kernels for 0% -> 0%
where the time goes in v5:
time: 191 us; the launch traced here: 190 us
  blocking collectives  93.7 us (49%)
  starting transfers between devices  72.1 us (38%)
  waiting for transfers between devices  15.9 us (8%)
  matrix products  1.96 us (1%)
    all_gather x1, blocking collectives, body(): parts = lax.all_gather(part, AXIS, axis=0, axis_index_groups=FAR)  40.8 us
    ppermute x6, starting transfers between devices, ring(): down.append(lax.ppermute(down[-1], AXIS, shift(-1)))  31.8 us
    all_gather x2, blocking collectives, near(): return lax.all_gather(piece, AXIS, axis=0, axis_index_groups=NEAR)  30.5 us
    all_to_all x1, blocking collectives, body(): lax.all_to_all(blocks.reshape(CUBE, -1, chunk), AXIS, 0, 0, axis_index_gr...  15.7 us
    ppermute x6, starting transfers between devices, ring(): up.append(lax.ppermute(up[-1], AXIS, shift(1)))  12.5 us
    ppermute x1, starting transfers between devices, ring(): down.append(lax.ppermute(block, AXIS, shift(-2)))  10.9 us
    ppermute x6, waiting for transfers between devices, ring(): up.append(lax.ppermute(up[-1], AXIS, shift(1)))  10.6 us
    all_gather x1, blocking collectives, body(): both = lax.all_gather(tile, AXIS, axis=0, axis_index_groups=PAIRS)  6.7 us
  transfers between devices with their start and end apart: 18, of which 12 were waited for; matrix products, arithmetic and copies ran while one was open for 0% of the time, Pallas kernels for 0%

profile of v5, /device:TPU:6, one launch (start us, length us, event | category | flops | bytes accessed | tf_op | source)
XLA Modules:
  0.0 189.5 jit_solution(10985904647373065979)
XLA Ops:
  0.0 0.0 copy-start
  0.0 1.0 constant_dynamic-slice_fusion
  1.0 3.5 %collective-permute-start = (bf16[112,512]{1,0:T(8,128)(2,1)S(1)}, bf16[112,512]{1,0:T(8,128)(2,1)S(1)}, u32[]{:S(2)}, u32[]{:S(2)}) collective-permute-start(bf16[112,512]{1,0:T(8,128)(2,1)S(1)} %constant_dynamic-slice_fusion), channel_id=1, source_target_pairs={{0,16},{1,17},{2,18},{3,19},{4,20},{5,21},{6,22},{7,23},{8,24},{9,... | collective-permute-start | bytes 344072 | tf_op jit(solution)/shard_map/ppermute | solution.py:99
  4.5 3.3 %collective-permute-done = bf16[112,512]{1,0:T(8,128)(2,1)S(1)} collective-permute-done((bf16[112,512]{1,0:T(8,128)(2,1)S(1)}, bf16[112,512]{1,0:T(8,128)(2,1)S(1)}, u32[]{:S(2)}, u32[]{:S(2)}) %collective-permute-start) | collective-permute-done | bytes 114720 | tf_op jit(solution)/shard_map/ppermute | solution.py:99
  7.8 0.9 select_bitcast_fusion.1
  8.7 3.8 %collective-permute-start.1 = (bf16[2,112,512]{2,1,0:T(8,128)(2,1)S(1)}, bf16[2,112,512]{2,1,0:T(8,128)(2,1)S(1)}, u32[]{:S(2)}, u32[]{:S(2)}) collective-permute-start(bf16[2,112,512]{2,1,0:T(8,128)(2,1)S(1)} %pad_maximum_fusion.3), channel_id=1, source_target_pairs={{0,1},{1,2},{2,3},{3,4},{4,5},{5,6},{6,7},{7,8},{8,9},{9,10},{10,1... | collective-permute-start | bytes 688136 | tf_op jit(solution)/shard_map/ppermute | solution.py:28
  12.6 10.9 %collective-permute-start.9 = (bf16[2,112,512]{2,1,0:T(8,128)(2,1)S(1)}, bf16[2,112,512]{2,1,0:T(8,128)(2,1)S(1)}, u32[]{:S(2)}, u32[]{:S(2)}) collective-permute-start(bf16[2,112,512]{2,1,0:T(8,128)(2,1)S(1)} %pad_maximum_fusion.3), channel_id=1, source_target_pairs={{0,14},{1,15},{2,0},{3,1},{4,2},{5,3},{6,4},{7,5},{8,6},{9,7},{10,... | collective-permute-start | bytes 688136 | tf_op jit(solution)/shard_map/ppermute | solution.py:29
  23.9 2.9 %collective-permute-start.8 = (bf16[2,112,512]{2,1,0:T(8,128)(2,1)S(1)}, bf16[2,112,512]{2,1,0:T(8,128)(2,1)S(1)}, u32[]{:S(2)}, u32[]{:S(2)}) collective-permute-start(bf16[2,112,512]{2,1,0:T(8,128)(2,1)S(1)} %pad_maximum_fusion.3), channel_id=1, source_target_pairs={{0,15},{1,0},{2,1},{3,2},{4,3},{5,4},{6,5},{7,6},{8,7},{9,8},{10,9... | collective-permute-start | bytes 688136 | tf_op jit(solution)/shard_map/ppermute | solution.py:28
  26.8 0.4 broadcast_in_dim.51
  27.2 0.0 collective-permute-done.1
  27.2 0.0 copy-done
  27.3 3.5 %collective-permute-start.16 = (bf16[112,3584]{1,0:T(8,128)(2,1)S(1)}, bf16[112,3584]{1,0:T(8,128)(2,1)S(1)}, u32[]{:S(2)}, u32[]{:S(2)}) collective-permute-start(bf16[112,3584]{1,0:T(8,128)(2,1)S(1)} %copy-done), channel_id=1, source_target_pairs={{0,16},{1,17},{2,18},{3,19},{4,20},{5,21},{6,22},{7,23},{8,24},{9,... | collective-permute-start | bytes 2408456 | tf_op jit(solution)/shard_map/ppermute | solution.py:105
  30.7 2.9 %collective-permute-start.2 = (bf16[2,112,512]{2,1,0:T(8,128)(2,1)S(1)}, bf16[2,112,512]{2,1,0:T(8,128)(2,1)S(1)}, u32[]{:S(2)}, u32[]{:S(2)}) collective-permute-start(bf16[2,112,512]{2,1,0:T(8,128)(2,1)S(1)} %collective-permute-done.1), channel_id=1, source_target_pairs={{0,1},{1,2},{2,3},{3,4},{4,5},{5,6},{6,7},{7,8},{8,9},{9,10},{10,1... | collective-permute-start | bytes 688136 | tf_op jit(solution)/shard_map/ppermute | solution.py:31
  33.7 0.0 collective-permute-done.9
  33.7 4.1 %collective-permute-start.10 = (bf16[2,112,512]{2,1,0:T(8,128)(2,1)S(1)}, bf16[2,112,512]{2,1,0:T(8,128)(2,1)S(1)}, u32[]{:S(2)}, u32[]{:S(2)}) collective-permute-start(bf16[2,112,512]{2,1,0:T(8,128)(2,1)S(1)} %collective-permute-done.9), channel_id=1, source_target_pairs={{0,15},{1,0},{2,1},{3,2},{4,3},{5,4},{6,5},{7,6},{8,7},{9,8},{10,9... | collective-permute-start | bytes 688136 | tf_op jit(solution)/shard_map/ppermute | solution.py:32
  37.9 2.0 %collective-permute-done.2 = bf16[2,112,512]{2,1,0:T(8,128)(2,1)S(1)} collective-permute-done((bf16[2,112,512]{2,1,0:T(8,128)(2,1)S(1)}, bf16[2,112,512]{2,1,0:T(8,128)(2,1)S(1)}, u32[]{:S(2)}, u32[]{:S(2)}) %collective-permute-start.2) | collective-permute-done | bytes 229408 | tf_op jit(solution)/shard_map/ppermute | solution.py:31
  39.9 1.9 %collective-permute-start.3 = (bf16[2,112,512]{2,1,0:T(8,128)(2,1)S(1)}, bf16[2,112,512]{2,1,0:T(8,128)(2,1)S(1)}, u32[]{:S(2)}, u32[]{:S(2)}) collective-permute-start(bf16[2,112,512]{2,1,0:T(8,128)(2,1)S(1)} %collective-permute-done.2), channel_id=1, source_target_pairs={{0,1},{1,2},{2,3},{3,4},{4,5},{5,6},{6,7},{7,8},{8,9},{9,10},{10,1... | collective-permute-start | bytes 688136 | tf_op jit(solution)/shard_map/ppermute | solution.py:31
  41.8 0.2 collective-permute-done.10
  42.0 5.6 %collective-permute-start.11 = (bf16[2,112,512]{2,1,0:T(8,128)(2,1)S(1)}, bf16[2,112,512]{2,1,0:T(8,128)(2,1)S(1)}, u32[]{:S(2)}, u32[]{:S(2)}) collective-permute-start(bf16[2,112,512]{2,1,0:T(8,128)(2,1)S(1)} %collective-permute-done.10), channel_id=1, source_target_pairs={{0,15},{1,0},{2,1},{3,2},{4,3},{5,4},{6,5},{7,6},{8,7},{9,8},{10,9... | collective-permute-start | bytes 688136 | tf_op jit(solution)/shard_map/ppermute | solution.py:32
  47.6 1.4 collective-permute-done.3
  49.0 1.9 %collective-permute-start.4 = (bf16[2,112,512]{2,1,0:T(8,128)(2,1)S(1)}, bf16[2,112,512]{2,1,0:T(8,128)(2,1)S(1)}, u32[]{:S(2)}, u32[]{:S(2)}) collective-permute-start(bf16[2,112,512]{2,1,0:T(8,128)(2,1)S(1)} %collective-permute-done.3), channel_id=1, source_target_pairs={{0,1},{1,2},{2,3},{3,4},{4,5},{5,6},{6,7},{7,8},{8,9},{9,10},{10,1... | collective-permute-start | bytes 688136 | tf_op jit(solution)/shard_map/ppermute | solution.py:31
  50.9 0.2 collective-permute-done.11
  51.1 5.6 %collective-permute-start.12 = (bf16[2,112,512]{2,1,0:T(8,128)(2,1)S(1)}, bf16[2,112,512]{2,1,0:T(8,128)(2,1)S(1)}, u32[]{:S(2)}, u32[]{:S(2)}) collective-permute-start(bf16[2,112,512]{2,1,0:T(8,128)(2,1)S(1)} %collective-permute-done.11), channel_id=1, source_target_pairs={{0,15},{1,0},{2,1},{3,2},{4,3},{5,4},{6,5},{7,6},{8,7},{9,8},{10,9... | collective-permute-start | bytes 688136 | tf_op jit(solution)/shard_map/ppermute | solution.py:32
  56.7 1.4 collective-permute-done.4
  58.1 1.9 %collective-permute-start.5 = (bf16[2,112,512]{2,1,0:T(8,128)(2,1)S(1)}, bf16[2,112,512]{2,1,0:T(8,128)(2,1)S(1)}, u32[]{:S(2)}, u32[]{:S(2)}) collective-permute-start(bf16[2,112,512]{2,1,0:T(8,128)(2,1)S(1)} %collective-permute-done.4), channel_id=1, source_target_pairs={{0,1},{1,2},{2,3},{3,4},{4,5},{5,6},{6,7},{7,8},{8,9},{9,10},{10,1... | collective-permute-start | bytes 688136 | tf_op jit(solution)/shard_map/ppermute | solution.py:31
  60.0 0.2 collective-permute-done.12
  60.2 5.6 %collective-permute-start.13 = (bf16[2,112,512]{2,1,0:T(8,128)(2,1)S(1)}, bf16[2,112,512]{2,1,0:T(8,128)(2,1)S(1)}, u32[]{:S(2)}, u32[]{:S(2)}) collective-permute-start(bf16[2,112,512]{2,1,0:T(8,128)(2,1)S(1)} %collective-permute-done.12), channel_id=1, source_target_pairs={{0,15},{1,0},{2,1},{3,2},{4,3},{5,4},{6,5},{7,6},{8,7},{9,8},{10,9... | collective-permute-start | bytes 688136 | tf_op jit(solution)/shard_map/ppermute | solution.py:32
  65.8 1.4 collective-permute-done.5
  67.2 1.9 %collective-permute-start.6 = (bf16[2,112,512]{2,1,0:T(8,128)(2,1)S(1)}, bf16[2,112,512]{2,1,0:T(8,128)(2,1)S(1)}, u32[]{:S(2)}, u32[]{:S(2)}) collective-permute-start(bf16[2,112,512]{2,1,0:T(8,128)(2,1)S(1)} %collective-permute-done.5), channel_id=1, source_target_pairs={{0,1},{1,2},{2,3},{3,4},{4,5},{5,6},{6,7},{7,8},{8,9},{9,10},{10,1... | collective-permute-start | bytes 688136 | tf_op jit(solution)/shard_map/ppermute | solution.py:31
  69.1 0.2 collective-permute-done.13
  69.3 5.6 %collective-permute-start.14 = (bf16[2,112,512]{2,1,0:T(8,128)(2,1)S(1)}, bf16[2,112,512]{2,1,0:T(8,128)(2,1)S(1)}, u32[]{:S(2)}, u32[]{:S(2)}) collective-permute-start(bf16[2,112,512]{2,1,0:T(8,128)(2,1)S(1)} %collective-permute-done.13), channel_id=1, source_target_pairs={{0,15},{1,0},{2,1},{3,2},{4,3},{5,4},{6,5},{7,6},{8,7},{9,8},{10,9... | collective-permute-start | bytes 688136 | tf_op jit(solution)/shard_map/ppermute | solution.py:32
  74.9 2.5 %collective-permute-done.6 = bf16[2,112,512]{2,1,0:T(8,128)(2,1)S(1)} collective-permute-done((bf16[2,112,512]{2,1,0:T(8,128)(2,1)S(1)}, bf16[2,112,512]{2,1,0:T(8,128)(2,1)S(1)}, u32[]{:S(2)}, u32[]{:S(2)}) %collective-permute-start.6) | collective-permute-done | bytes 229408 | tf_op jit(solution)/shard_map/ppermute | solution.py:31
  77.4 1.9 %collective-permute-start.7 = (bf16[2,112,512]{2,1,0:T(8,128)(2,1)S(1)}, bf16[2,112,512]{2,1,0:T(8,128)(2,1)S(1)}, u32[]{:S(2)}, u32[]{:S(2)}) collective-permute-start(bf16[2,112,512]{2,1,0:T(8,128)(2,1)S(1)} %collective-permute-done.6), channel_id=1, source_target_pairs={{0,1},{1,2},{2,3},{3,4},{4,5},{5,6},{6,7},{7,8},{8,9},{9,10},{10,1... | collective-permute-start | bytes 688136 | tf_op jit(solution)/shard_map/ppermute | solution.py:31
  79.4 0.0 collective-permute-done.14
  79.4 5.3 %collective-permute-start.15 = (bf16[2,112,512]{2,1,0:T(8,128)(2,1)S(1)}, bf16[2,112,512]{2,1,0:T(8,128)(2,1)S(1)}, u32[]{:S(2)}, u32[]{:S(2)}) collective-permute-start(bf16[2,112,512]{2,1,0:T(8,128)(2,1)S(1)} %collective-permute-done.14), channel_id=1, source_target_pairs={{0,15},{1,0},{2,1},{3,2},{4,3},{5,4},{6,5},{7,6},{8,7},{9,8},{10,9... | collective-permute-start | bytes 688136 | tf_op jit(solution)/shard_map/ppermute | solution.py:32
  84.7 1.9 collective-permute-done.7
  86.6 0.0 collective-permute-done.8
  86.8 1.4 collective-permute-done.15
  88.2 0.0 collective-permute-done.16
  88.2 0.7 convolution_convert_fusion.3
  88.9 0.7 broadcast_select_fusion.3
  89.6 0.3 convolution_convert_fusion
  90.0 6.7 %all-gather = bf16[448,512]{1,0:T(8,128)(2,1)S(1)} all-gather(bf16[224,512]{1,0:T(8,128)(2,1)S(1)} %pad_maximum_fusion.4), channel_id=2, replica_groups={{0,16},{1,17},{2,18},{3,19},{4,20},{5,21},{6,22},{7,23},{8,24},{9,25},{..., dimensions={0}, use_global_device_ids=true | all-gather | bytes 688128 | tf_op jit(solution)/shard_map/all_gather | solution.py:117
  96.7 0.3 convolution_convert_fusion.1
  97.1 15.7 %all_to_all.5 = bf16[4,320,256]{2,1,0:T(8,128)(2,1)S(1)} all-to-all(bf16[4,320,256]{2,1,0:T(8,128)(2,1)S(1)} %bitcast.87), channel_id=1, replica_groups={{0,1,2,3},{4,5,6,7},{8,9,10,11},{12,13,14,15},{16,17,18,19},{20,21,22,2..., dimensions={0} | all-to-all | bytes 1310720 | tf_op jit(solution)/shard_map/all_to_all | solution.py:130
  112.8 0.1 reduce_sum.24
  112.9 40.8 %all-gather.1 = bf16[1280,256]{1,0:T(8,128)(2,1)S(1)} all-gather(bf16[320,256]{1,0:T(8,128)(2,1)S(1)} %reduce_sum.24), channel_id=3, replica_groups={{0,4,8,12},{1,5,9,13},{2,6,10,14},{3,7,11,15},{16,20,24,28},{17,21,25,2..., dimensions={0}, use_global_device_ids=true | all-gather | bytes 819200 | tf_op jit(solution)/shard_map/all_gather | solution.py:134
  153.7 0.1 reduce_sum.25
  153.8 3.2 %collective-permute-start.17 = (bf16[320,256]{1,0:T(8,128)(2,1)S(1)}, bf16[320,256]{1,0:T(8,128)(2,1)S(1)}, u32[]{:S(2)}, u32[]{:S(2)}) collective-permute-start(bf16[320,256]{1,0:T(8,128)(2,1)S(1)} %reduce_sum.25), channel_id=1, source_target_pairs={{0,16},{1,17},{2,18},{3,19},{4,20},{5,21},{6,22},{7,23},{8,24},{9,... | collective-permute-start | bytes 491528 | tf_op jit(solution)/shard_map/ppermute | solution.py:136
  157.1 14.2 %all-gather.2 = bf16[640,256]{1,0:T(8,128)(2,1)S(1)} all-gather(bf16[160,256]{1,0:T(8,128)(2,1)S(1)} %get-tuple-element.21), channel_id=4, replica_groups={{0,1,2,3},{4,5,6,7},{8,9,10,11},{12,13,14,15},{16,17,18,19},{20,21,22,2..., dimensions={0}, use_global_device_ids=true | all-gather | bytes 409600 | tf_op jit(solution)/shard_map/all_gather | solution.py:140
  171.3 0.0 collective-permute-done.17
  171.3 16.2 %all-gather.3 = bf16[1920,256]{1,0:T(8,128)(2,1)S(1)} all-gather(bf16[480,256]{1,0:T(8,128)(2,1)S(1)} %pad_maximum_fusion.2), channel_id=5, replica_groups={{0,1,2,3},{4,5,6,7},{8,9,10,11},{12,13,14,15},{16,17,18,19},{20,21,22,2..., dimensions={0}, use_global_device_ids=true | all-gather | bytes 1228800 | tf_op jit(solution)/shard_map/all_gather | solution.py:140
  187.6 0.3 broadcast_select_fusion
  187.9 1.7 finish.1
  (26 shorter events, 0.6 us)
Async XLA Ops:
  0.0 27.2 %copy-start = (bf16[112,3584]{1,0:T(8,128)(2,1)S(1)}, bf16[112,3584]{1,0:T(8,128)(2,1)}, u32[]{:S(2)}) copy-start(bf16[112,3584]{1,0:T(8,128)(2,1)} %param.2) | copy-start | bytes 2408452
  1.0 6.8 %collective-permute-start = (bf16[112,512]{1,0:T(8,128)(2,1)S(1)}, bf16[112,512]{1,0:T(8,128)(2,1)S(1)}, u32[]{:S(2)}, u32[]{:S(2)}) collective-permute-start(bf16[112,512]{1,0:T(8,128)(2,1)S(1)} %constant_dynamic-slice_fusion), channel_id=1, source_target_pairs={{0,16},{1,17},{2,18},{3,19},{4,20},{5,21},{6,22},{7,23},{8,24},{9,... | collective-permute-start | bytes 344072 | tf_op jit(solution)/shard_map/ppermute | solution.py:99
  8.7 18.5 %collective-permute-start.1 = (bf16[2,112,512]{2,1,0:T(8,128)(2,1)S(1)}, bf16[2,112,512]{2,1,0:T(8,128)(2,1)S(1)}, u32[]{:S(2)}, u32[]{:S(2)}) collective-permute-start(bf16[2,112,512]{2,1,0:T(8,128)(2,1)S(1)} %pad_maximum_fusion.3), channel_id=1, source_target_pairs={{0,1},{1,2},{2,3},{3,4},{4,5},{5,6},{6,7},{7,8},{8,9},{9,10},{10,1... | collective-permute-start | bytes 688136 | tf_op jit(solution)/shard_map/ppermute | solution.py:28
  12.6 21.1 %collective-permute-start.9 = (bf16[2,112,512]{2,1,0:T(8,128)(2,1)S(1)}, bf16[2,112,512]{2,1,0:T(8,128)(2,1)S(1)}, u32[]{:S(2)}, u32[]{:S(2)}) collective-permute-start(bf16[2,112,512]{2,1,0:T(8,128)(2,1)S(1)} %pad_maximum_fusion.3), channel_id=1, source_target_pairs={{0,14},{1,15},{2,0},{3,1},{4,2},{5,3},{6,4},{7,5},{8,6},{9,7},{10,... | collective-permute-start | bytes 688136 | tf_op jit(solution)/shard_map/ppermute | solution.py:29
  23.9 62.7 %collective-permute-start.8 = (bf16[2,112,512]{2,1,0:T(8,128)(2,1)S(1)}, bf16[2,112,512]{2,1,0:T(8,128)(2,1)S(1)}, u32[]{:S(2)}, u32[]{:S(2)}) collective-permute-start(bf16[2,112,512]{2,1,0:T(8,128)(2,1)S(1)} %pad_maximum_fusion.3), channel_id=1, source_target_pairs={{0,15},{1,0},{2,1},{3,2},{4,3},{5,4},{6,5},{7,6},{8,7},{9,8},{10,9... | collective-permute-start | bytes 688136 | tf_op jit(solution)/shard_map/ppermute | solution.py:28
  27.3 60.9 %collective-permute-start.16 = (bf16[112,3584]{1,0:T(8,128)(2,1)S(1)}, bf16[112,3584]{1,0:T(8,128)(2,1)S(1)}, u32[]{:S(2)}, u32[]{:S(2)}) collective-permute-start(bf16[112,3584]{1,0:T(8,128)(2,1)S(1)} %copy-done), channel_id=1, source_target_pairs={{0,16},{1,17},{2,18},{3,19},{4,20},{5,21},{6,22},{7,23},{8,24},{9,... | collective-permute-start | bytes 2408456 | tf_op jit(solution)/shard_map/ppermute | solution.py:105
  30.7 9.1 %collective-permute-start.2 = (bf16[2,112,512]{2,1,0:T(8,128)(2,1)S(1)}, bf16[2,112,512]{2,1,0:T(8,128)(2,1)S(1)}, u32[]{:S(2)}, u32[]{:S(2)}) collective-permute-start(bf16[2,112,512]{2,1,0:T(8,128)(2,1)S(1)} %collective-permute-done.1), channel_id=1, source_target_pairs={{0,1},{1,2},{2,3},{3,4},{4,5},{5,6},{6,7},{7,8},{8,9},{9,10},{10,1... | collective-permute-start | bytes 688136 | tf_op jit(solution)/shard_map/ppermute | solution.py:31
  33.7 8.3 %collective-permute-start.10 = (bf16[2,112,512]{2,1,0:T(8,128)(2,1)S(1)}, bf16[2,112,512]{2,1,0:T(8,128)(2,1)S(1)}, u32[]{:S(2)}, u32[]{:S(2)}) collective-permute-start(bf16[2,112,512]{2,1,0:T(8,128)(2,1)S(1)} %collective-permute-done.9), channel_id=1, source_target_pairs={{0,15},{1,0},{2,1},{3,2},{4,3},{5,4},{6,5},{7,6},{8,7},{9,8},{10,9... | collective-permute-start | bytes 688136 | tf_op jit(solution)/shard_map/ppermute | solution.py:32
  39.9 9.1 %collective-permute-start.3 = (bf16[2,112,512]{2,1,0:T(8,128)(2,1)S(1)}, bf16[2,112,512]{2,1,0:T(8,128)(2,1)S(1)}, u32[]{:S(2)}, u32[]{:S(2)}) collective-permute-start(bf16[2,112,512]{2,1,0:T(8,128)(2,1)S(1)} %collective-permute-done.2), channel_id=1, source_target_pairs={{0,1},{1,2},{2,3},{3,4},{4,5},{5,6},{6,7},{7,8},{8,9},{9,10},{10,1... | collective-permute-start | bytes 688136 | tf_op jit(solution)/shard_map/ppermute | solution.py:31
  42.0 9.1 %collective-permute-start.11 = (bf16[2,112,512]{2,1,0:T(8,128)(2,1)S(1)}, bf16[2,112,512]{2,1,0:T(8,128)(2,1)S(1)}, u32[]{:S(2)}, u32[]{:S(2)}) collective-permute-start(bf16[2,112,512]{2,1,0:T(8,128)(2,1)S(1)} %collective-permute-done.10), channel_id=1, source_target_pairs={{0,15},{1,0},{2,1},{3,2},{4,3},{5,4},{6,5},{7,6},{8,7},{9,8},{10,9... | collective-permute-start | bytes 688136 | tf_op jit(solution)/shard_map/ppermute | solution.py:32
  49.0 9.1 %collective-permute-start.4 = (bf16[2,112,512]{2,1,0:T(8,128)(2,1)S(1)}, bf16[2,112,512]{2,1,0:T(8,128)(2,1)S(1)}, u32[]{:S(2)}, u32[]{:S(2)}) collective-permute-start(bf16[2,112,512]{2,1,0:T(8,128)(2,1)S(1)} %collective-permute-done.3), channel_id=1, source_target_pairs={{0,1},{1,2},{2,3},{3,4},{4,5},{5,6},{6,7},{7,8},{8,9},{9,10},{10,1... | collective-permute-start | bytes 688136 | tf_op jit(solution)/shard_map/ppermute | solution.py:31
  51.1 9.1 %collective-permute-start.12 = (bf16[2,112,512]{2,1,0:T(8,128)(2,1)S(1)}, bf16[2,112,512]{2,1,0:T(8,128)(2,1)S(1)}, u32[]{:S(2)}, u32[]{:S(2)}) collective-permute-start(bf16[2,112,512]{2,1,0:T(8,128)(2,1)S(1)} %collective-permute-done.11), channel_id=1, source_target_pairs={{0,15},{1,0},{2,1},{3,2},{4,3},{5,4},{6,5},{7,6},{8,7},{9,8},{10,9... | collective-permute-start | bytes 688136 | tf_op jit(solution)/shard_map/ppermute | solution.py:32
  58.1 9.1 %collective-permute-start.5 = (bf16[2,112,512]{2,1,0:T(8,128)(2,1)S(1)}, bf16[2,112,512]{2,1,0:T(8,128)(2,1)S(1)}, u32[]{:S(2)}, u32[]{:S(2)}) collective-permute-start(bf16[2,112,512]{2,1,0:T(8,128)(2,1)S(1)} %collective-permute-done.4), channel_id=1, source_target_pairs={{0,1},{1,2},{2,3},{3,4},{4,5},{5,6},{6,7},{7,8},{8,9},{9,10},{10,1... | collective-permute-start | bytes 688136 | tf_op jit(solution)/shard_map/ppermute | solution.py:31
  60.2 9.1 %collective-permute-start.13 = (bf16[2,112,512]{2,1,0:T(8,128)(2,1)S(1)}, bf16[2,112,512]{2,1,0:T(8,128)(2,1)S(1)}, u32[]{:S(2)}, u32[]{:S(2)}) collective-permute-start(bf16[2,112,512]{2,1,0:T(8,128)(2,1)S(1)} %collective-permute-done.12), channel_id=1, source_target_pairs={{0,15},{1,0},{2,1},{3,2},{4,3},{5,4},{6,5},{7,6},{8,7},{9,8},{10,9... | collective-permute-start | bytes 688136 | tf_op jit(solution)/shard_map/ppermute | solution.py:32
  67.2 10.2 %collective-permute-start.6 = (bf16[2,112,512]{2,1,0:T(8,128)(2,1)S(1)}, bf16[2,112,512]{2,1,0:T(8,128)(2,1)S(1)}, u32[]{:S(2)}, u32[]{:S(2)}) collective-permute-start(bf16[2,112,512]{2,1,0:T(8,128)(2,1)S(1)} %collective-permute-done.5), channel_id=1, source_target_pairs={{0,1},{1,2},{2,3},{3,4},{4,5},{5,6},{6,7},{7,8},{8,9},{9,10},{10,1... | collective-permute-start | bytes 688136 | tf_op jit(solution)/shard_map/ppermute | solution.py:31
  69.3 10.0 %collective-permute-start.14 = (bf16[2,112,512]{2,1,0:T(8,128)(2,1)S(1)}, bf16[2,112,512]{2,1,0:T(8,128)(2,1)S(1)}, u32[]{:S(2)}, u32[]{:S(2)}) collective-permute-start(bf16[2,112,512]{2,1,0:T(8,128)(2,1)S(1)} %collective-permute-done.13), channel_id=1, source_target_pairs={{0,15},{1,0},{2,1},{3,2},{4,3},{5,4},{6,5},{7,6},{8,7},{9,8},{10,9... | collective-permute-start | bytes 688136 | tf_op jit(solution)/shard_map/ppermute | solution.py:32
  77.4 9.1 %collective-permute-start.7 = (bf16[2,112,512]{2,1,0:T(8,128)(2,1)S(1)}, bf16[2,112,512]{2,1,0:T(8,128)(2,1)S(1)}, u32[]{:S(2)}, u32[]{:S(2)}) collective-permute-start(bf16[2,112,512]{2,1,0:T(8,128)(2,1)S(1)} %collective-permute-done.6), channel_id=1, source_target_pairs={{0,1},{1,2},{2,3},{3,4},{4,5},{5,6},{6,7},{7,8},{8,9},{9,10},{10,1... | collective-permute-start | bytes 688136 | tf_op jit(solution)/shard_map/ppermute | solution.py:31
  79.4 8.8 %collective-permute-start.15 = (bf16[2,112,512]{2,1,0:T(8,128)(2,1)S(1)}, bf16[2,112,512]{2,1,0:T(8,128)(2,1)S(1)}, u32[]{:S(2)}, u32[]{:S(2)}) collective-permute-start(bf16[2,112,512]{2,1,0:T(8,128)(2,1)S(1)} %collective-permute-done.14), channel_id=1, source_target_pairs={{0,15},{1,0},{2,1},{3,2},{4,3},{5,4},{6,5},{7,6},{8,7},{9,8},{10,9... | collective-permute-start | bytes 688136 | tf_op jit(solution)/shard_map/ppermute | solution.py:32
  153.8 17.5 %collective-permute-start.17 = (bf16[320,256]{1,0:T(8,128)(2,1)S(1)}, bf16[320,256]{1,0:T(8,128)(2,1)S(1)}, u32[]{:S(2)}, u32[]{:S(2)}) collective-permute-start(bf16[320,256]{1,0:T(8,128)(2,1)S(1)} %reduce_sum.25), channel_id=1, source_target_pairs={{0,16},{1,17},{2,18},{3,19},{4,20},{5,21},{6,22},{7,23},{8,24},{9,... | collective-permute-start | bytes 491528 | tf_op jit(solution)/shard_map/ppermute | solution.py:136

commit v6 on v4

--- a/solution.py
+++ b/solution.py
@@ -36,7 +36,7 @@
 
 
 def place(full, block, z):
-    return lax.dynamic_update_slice(full, block[:, None], (0, z % Z, 0, 0))
+    return lax.dynamic_update_slice(full, block[None], (z % Z, 0, 0))
 
 
 def finish_kernel(order, low_ref, high_ref, power_ref, out_ref):
@@ -96,34 +96,33 @@
     position = lax.axis_index(AXIS)
     y, z = position // Z, position % Z
 
-    mine = lax.dynamic_slice_in_dim(basis, y * half, half, 1)
-    other = lax.dynamic_slice_in_dim(basis, (1 - y) * half, half, 1)
-    other = lax.ppermute(other, AXIS, ACROSS)
     first_row = y == 0
-    block = jnp.stack([jnp.where(first_row, mine, other), jnp.where(first_row, other, mine)])
-    far_rows = lax.ppermute(factor_rows, AXIS, ACROSS)
+    span = order // 2
+    own_columns = lax.dynamic_slice_in_dim(factor_rows, y * span, span, 1)
+    far_columns = lax.ppermute(lax.dynamic_slice_in_dim(factor_rows, (1 - y) * span, span, 1), AXIS, ACROSS)
 
-    up, down = ring(block)
-    full = jnp.zeros((2, Z, rows, half), basis.dtype)
-    full = place(full, block, z)
+    up, down = ring(basis)
+    full = jnp.zeros((Z, rows, columns), basis.dtype)
+    full = place(full, basis, z)
     for step, part in enumerate(up):
         full = place(full, part, z - step - 1 + Z)
     for step, part in enumerate(down):
         full = place(full, part, z + step + 1)
-    full = full.reshape(order, half)
+    full = full.reshape(span, columns)
 
-    near = jnp.dot(factor_rows, full, preferred_element_type=jnp.float32).astype(jnp.bfloat16)
-    far = jnp.dot(far_rows, full, preferred_element_type=jnp.float32).astype(jnp.bfloat16)
-    tile = jnp.concatenate([jnp.where(first_row, near, far), jnp.where(first_row, far, near)], 0)
-    both = lax.all_gather(tile, AXIS, axis=0, axis_index_groups=PAIRS)
-    plane = jnp.concatenate([both[0], both[1]], 1)
+    near = jnp.dot(own_columns, full, preferred_element_type=jnp.float32).astype(jnp.bfloat16)
+    far = jnp.dot(far_columns, full, preferred_element_type=jnp.float32).astype(jnp.bfloat16)
+    terms = jnp.concatenate([jnp.where(first_row, near, far), jnp.where(first_row, far, near)], 0)
+    terms = lax.all_gather(terms, AXIS, axis=0, axis_index_groups=PAIRS).astype(jnp.float32)
+    plane = (terms[0] + terms[1]).astype(jnp.bfloat16)
     power = lax.dynamic_slice_in_dim(plane, y * rows, rows, 0)
+    tile = lax.dynamic_slice_in_dim(plane, y * half, half, 1)
 
     def cross(a, b):
         return lax.dot_general(a, b, (((0,), (0,)), ((), ())), preferred_element_type=jnp.float32)
 
     square = cross(tile, tile).astype(jnp.bfloat16)
-    strip = cross(both[1], lax.dynamic_slice_in_dim(both[0], y * chunk, chunk, 1)).astype(jnp.bfloat16)
+    strip = cross(plane[:, half:], lax.dynamic_slice_in_dim(plane, y * chunk, chunk, 1)).astype(jnp.bfloat16)
     blocks = jnp.concatenate(
         [square[:chunk, :chunk], square[:chunk, chunk:], square[chunk:, chunk:], strip], 0
     )

time: 189 us -> 183 us (0.968)
  waiting for transfers between devices: 26 us -> 21.9 us
  starting transfers between devices: 67.6 us -> 64.1 us
  blocking collectives: 86.8 us -> 89.5 us
    ppermute x2 -> x1, starting transfers between devices: 6.96 us -> 3.48 us  [body(): lax.ppermute(lax.dynamic_slice_in_dim(factor_rows, (1 - y) * span, span,...]
    ppermute x2 -> x1, waiting for transfers between devices: 3.28 us -> 0.01 us  [body(): lax.ppermute(lax.dynamic_slice_in_dim(factor_rows, (1 - y) * span, span,...]
    all_gather x1, blocking collectives: 6.7 us -> 9.16 us  [body(): lax.all_gather(terms, AXIS, axis=0, axis_index_groups=PAIRS)]
  transfers between devices with their start and end apart: 18 -> 17, of which waited for: 9 -> 7; matrix products, arithmetic and copies ran while one was open for 0% -> 0% of each run, Pallas kernels for 0% -> 0%
where the time goes in v6:
time: 183 us; the launch traced here: 182 us
  blocking collectives  89.5 us (49%)
  starting transfers between devices  64.1 us (35%)
  waiting for transfers between devices  21.9 us (12%)
  matrix products  2.05 us (1%)
    ppermute x7, starting transfers between devices, ring(): b = lax.ppermute(b, AXIS, shift(-1))  40.6 us
    all_gather x2, blocking collectives, near(): return lax.all_gather(piece, AXIS, axis=0, axis_index_groups=NEAR)  31.7 us
    all_gather x1, blocking collectives, body(): parts = lax.all_gather(part, AXIS, axis=0, axis_index_groups=FAR)  26.5 us
    all_to_all x1, blocking collectives, body(): lax.all_to_all(blocks.reshape(CUBE, -1, chunk), AXIS, 0, 0, axis_index_gr...  22 us
    ppermute x8, waiting for transfers between devices, ring(): a = lax.ppermute(a, AXIS, shift(1))  21.9 us
    ppermute x8, starting transfers between devices, ring(): a = lax.ppermute(a, AXIS, shift(1))  17.3 us
    all_gather x1, blocking collectives, body(): lax.all_gather(terms, AXIS, axis=0, axis_index_groups=PAIRS)  9.16 us
  transfers between devices with their start and end apart: 17, of which 7 were waited for; matrix products, arithmetic and copies ran while one was open for 0% of the time, Pallas kernels for 0%

profile of v6, /device:TPU:6, one launch (start us, length us, event | category | flops | bytes accessed | tf_op | source)
XLA Modules:
  0.0 181.9 jit_solution(2424780572367375166)
XLA Ops:
  0.0 0.0 copy-start
  0.0 0.0 copy-start.1
  0.0 3.9 %collective-permute-start = (bf16[112,1024]{1,0:T(8,128)(2,1)}, bf16[112,1024]{1,0:T(8,128)(2,1)S(1)}, u32[]{:S(2)}, u32[]{:S(2)}) collective-permute-start(bf16[112,1024]{1,0:T(8,128)(2,1)} %param.3), channel_id=1, source_target_pairs={{0,1},{1,2},{2,3},{3,4},{4,5},{5,6},{6,7},{7,8},{8,9},{9,10},{10,1... | collective-permute-start | bytes 688136 | tf_op jit(solution)/shard_map/ppermute | solution.py:30
  4.0 9.5 %collective-permute-start.8 = (bf16[112,1024]{1,0:T(8,128)(2,1)}, bf16[112,1024]{1,0:T(8,128)(2,1)S(1)}, u32[]{:S(2)}, u32[]{:S(2)}) collective-permute-start(bf16[112,1024]{1,0:T(8,128)(2,1)} %param.3), channel_id=1, source_target_pairs={{0,15},{1,0},{2,1},{3,2},{4,3},{5,4},{6,5},{7,6},{8,7},{9,8},{10,9... | collective-permute-start | bytes 688136 | tf_op jit(solution)/shard_map/ppermute | solution.py:33
  13.5 0.0 copy-done
  13.5 3.5 %collective-permute-start.15 = (bf16[112,1792]{1,0:T(8,128)(2,1)S(1)}, bf16[112,1792]{1,0:T(8,128)(2,1)S(1)}, u32[]{:S(2)}, u32[]{:S(2)}) collective-permute-start(bf16[112,1792]{1,0:T(8,128)(2,1)S(1)} %constant_dynamic-slice_fusion.1), channel_id=1, source_target_pairs={{0,16},{1,17},{2,18},{3,19},{4,20},{5,21},{6,22},{7,23},{8,24},{9,... | collective-permute-start | bytes 1204232 | tf_op jit(solution)/shard_map/ppermute | solution.py:102
  17.4 0.5 broadcast_in_dim.51
  17.9 0.0 copy-done.1
  17.9 0.0 collective-permute-done
  17.9 1.9 %collective-permute-start.1 = (bf16[112,1024]{1,0:T(8,128)(2,1)S(1)}, bf16[112,1024]{1,0:T(8,128)(2,1)S(1)}, u32[]{:S(2)}, u32[]{:S(2)}) collective-permute-start(bf16[112,1024]{1,0:T(8,128)(2,1)S(1)} %collective-permute-done), channel_id=1, source_target_pairs={{0,1},{1,2},{2,3},{3,4},{4,5},{5,6},{6,7},{7,8},{8,9},{9,10},{10,1... | collective-permute-start | bytes 688136 | tf_op jit(solution)/shard_map/ppermute | solution.py:30
  19.8 0.0 collective-permute-done.8
  19.9 5.1 %collective-permute-start.9 = (bf16[112,1024]{1,0:T(8,128)(2,1)S(1)}, bf16[112,1024]{1,0:T(8,128)(2,1)S(1)}, u32[]{:S(2)}, u32[]{:S(2)}) collective-permute-start(bf16[112,1024]{1,0:T(8,128)(2,1)S(1)} %collective-permute-done.8), channel_id=1, source_target_pairs={{0,15},{1,0},{2,1},{3,2},{4,3},{5,4},{6,5},{7,6},{8,7},{9,8},{10,9... | collective-permute-start | bytes 688136 | tf_op jit(solution)/shard_map/ppermute | solution.py:33
  25.0 2.8 %collective-permute-done.1 = bf16[112,1024]{1,0:T(8,128)(2,1)S(1)} collective-permute-done((bf16[112,1024]{1,0:T(8,128)(2,1)S(1)}, bf16[112,1024]{1,0:T(8,128)(2,1)S(1)}, u32[]{:S(2)}, u32[]{:S(2)}) %collective-permute-start.1) | collective-permute-done | bytes 229408 | tf_op jit(solution)/shard_map/ppermute | solution.py:30
  27.8 1.9 %collective-permute-start.2 = (bf16[112,1024]{1,0:T(8,128)(2,1)S(1)}, bf16[112,1024]{1,0:T(8,128)(2,1)S(1)}, u32[]{:S(2)}, u32[]{:S(2)}) collective-permute-start(bf16[112,1024]{1,0:T(8,128)(2,1)S(1)} %collective-permute-done.1), channel_id=1, source_target_pairs={{0,1},{1,2},{2,3},{3,4},{4,5},{5,6},{6,7},{7,8},{8,9},{9,10},{10,1... | collective-permute-start | bytes 688136 | tf_op jit(solution)/shard_map/ppermute | solution.py:30
  29.7 0.0 collective-permute-done.9
  29.7 5.1 %collective-permute-start.10 = (bf16[112,1024]{1,0:T(8,128)(2,1)S(1)}, bf16[112,1024]{1,0:T(8,128)(2,1)S(1)}, u32[]{:S(2)}, u32[]{:S(2)}) collective-permute-start(bf16[112,1024]{1,0:T(8,128)(2,1)S(1)} %collective-permute-done.9), channel_id=1, source_target_pairs={{0,15},{1,0},{2,1},{3,2},{4,3},{5,4},{6,5},{7,6},{8,7},{9,8},{10,9... | collective-permute-start | bytes 688136 | tf_op jit(solution)/shard_map/ppermute | solution.py:33
  34.9 2.0 %collective-permute-done.2 = bf16[112,1024]{1,0:T(8,128)(2,1)S(1)} collective-permute-done((bf16[112,1024]{1,0:T(8,128)(2,1)S(1)}, bf16[112,1024]{1,0:T(8,128)(2,1)S(1)}, u32[]{:S(2)}, u32[]{:S(2)}) %collective-permute-start.2) | collective-permute-done | bytes 229408 | tf_op jit(solution)/shard_map/ppermute | solution.py:30
  36.9 1.9 %collective-permute-start.3 = (bf16[112,1024]{1,0:T(8,128)(2,1)S(1)}, bf16[112,1024]{1,0:T(8,128)(2,1)S(1)}, u32[]{:S(2)}, u32[]{:S(2)}) collective-permute-start(bf16[112,1024]{1,0:T(8,128)(2,1)S(1)} %collective-permute-done.2), channel_id=1, source_target_pairs={{0,1},{1,2},{2,3},{3,4},{4,5},{5,6},{6,7},{7,8},{8,9},{9,10},{10,1... | collective-permute-start | bytes 688136 | tf_op jit(solution)/shard_map/ppermute | solution.py:30
  38.8 0.0 collective-permute-done.10
  38.8 5.1 %collective-permute-start.11 = (bf16[112,1024]{1,0:T(8,128)(2,1)S(1)}, bf16[112,1024]{1,0:T(8,128)(2,1)S(1)}, u32[]{:S(2)}, u32[]{:S(2)}) collective-permute-start(bf16[112,1024]{1,0:T(8,128)(2,1)S(1)} %collective-permute-done.10), channel_id=1, source_target_pairs={{0,15},{1,0},{2,1},{3,2},{4,3},{5,4},{6,5},{7,6},{8,7},{9,8},{10,9... | collective-permute-start | bytes 688136 | tf_op jit(solution)/shard_map/ppermute | solution.py:33
  44.0 2.0 %collective-permute-done.3 = bf16[112,1024]{1,0:T(8,128)(2,1)S(1)} collective-permute-done((bf16[112,1024]{1,0:T(8,128)(2,1)S(1)}, bf16[112,1024]{1,0:T(8,128)(2,1)S(1)}, u32[]{:S(2)}, u32[]{:S(2)}) %collective-permute-start.3) | collective-permute-done | bytes 229408 | tf_op jit(solution)/shard_map/ppermute | solution.py:30
  46.0 1.9 %collective-permute-start.4 = (bf16[112,1024]{1,0:T(8,128)(2,1)S(1)}, bf16[112,1024]{1,0:T(8,128)(2,1)S(1)}, u32[]{:S(2)}, u32[]{:S(2)}) collective-permute-start(bf16[112,1024]{1,0:T(8,128)(2,1)S(1)} %collective-permute-done.3), channel_id=1, source_target_pairs={{0,1},{1,2},{2,3},{3,4},{4,5},{5,6},{6,7},{7,8},{8,9},{9,10},{10,1... | collective-permute-start | bytes 688136 | tf_op jit(solution)/shard_map/ppermute | solution.py:30
  48.0 0.0 collective-permute-done.11
  48.0 5.1 %collective-permute-start.12 = (bf16[112,1024]{1,0:T(8,128)(2,1)S(1)}, bf16[112,1024]{1,0:T(8,128)(2,1)S(1)}, u32[]{:S(2)}, u32[]{:S(2)}) collective-permute-start(bf16[112,1024]{1,0:T(8,128)(2,1)S(1)} %collective-permute-done.11), channel_id=1, source_target_pairs={{0,15},{1,0},{2,1},{3,2},{4,3},{5,4},{6,5},{7,6},{8,7},{9,8},{10,9... | collective-permute-start | bytes 688136 | tf_op jit(solution)/shard_map/ppermute | solution.py:33
  53.1 2.0 %collective-permute-done.4 = bf16[112,1024]{1,0:T(8,128)(2,1)S(1)} collective-permute-done((bf16[112,1024]{1,0:T(8,128)(2,1)S(1)}, bf16[112,1024]{1,0:T(8,128)(2,1)S(1)}, u32[]{:S(2)}, u32[]{:S(2)}) %collective-permute-start.4) | collective-permute-done | bytes 229408 | tf_op jit(solution)/shard_map/ppermute | solution.py:30
  55.1 1.9 %collective-permute-start.5 = (bf16[112,1024]{1,0:T(8,128)(2,1)S(1)}, bf16[112,1024]{1,0:T(8,128)(2,1)S(1)}, u32[]{:S(2)}, u32[]{:S(2)}) collective-permute-start(bf16[112,1024]{1,0:T(8,128)(2,1)S(1)} %collective-permute-done.4), channel_id=1, source_target_pairs={{0,1},{1,2},{2,3},{3,4},{4,5},{5,6},{6,7},{7,8},{8,9},{9,10},{10,1... | collective-permute-start | bytes 688136 | tf_op jit(solution)/shard_map/ppermute | solution.py:30
  57.1 0.0 collective-permute-done.12
  57.1 5.1 %collective-permute-start.13 = (bf16[112,1024]{1,0:T(8,128)(2,1)S(1)}, bf16[112,1024]{1,0:T(8,128)(2,1)S(1)}, u32[]{:S(2)}, u32[]{:S(2)}) collective-permute-start(bf16[112,1024]{1,0:T(8,128)(2,1)S(1)} %collective-permute-done.12), channel_id=1, source_target_pairs={{0,15},{1,0},{2,1},{3,2},{4,3},{5,4},{6,5},{7,6},{8,7},{9,8},{10,9... | collective-permute-start | bytes 688136 | tf_op jit(solution)/shard_map/ppermute | solution.py:33
  62.2 2.5 %collective-permute-done.5 = bf16[112,1024]{1,0:T(8,128)(2,1)S(1)} collective-permute-done((bf16[112,1024]{1,0:T(8,128)(2,1)S(1)}, bf16[112,1024]{1,0:T(8,128)(2,1)S(1)}, u32[]{:S(2)}, u32[]{:S(2)}) %collective-permute-start.5) | collective-permute-done | bytes 229408 | tf_op jit(solution)/shard_map/ppermute | solution.py:30
  64.8 1.9 %collective-permute-start.6 = (bf16[112,1024]{1,0:T(8,128)(2,1)S(1)}, bf16[112,1024]{1,0:T(8,128)(2,1)S(1)}, u32[]{:S(2)}, u32[]{:S(2)}) collective-permute-start(bf16[112,1024]{1,0:T(8,128)(2,1)S(1)} %collective-permute-done.5), channel_id=1, source_target_pairs={{0,1},{1,2},{2,3},{3,4},{4,5},{5,6},{6,7},{7,8},{8,9},{9,10},{10,1... | collective-permute-start | bytes 688136 | tf_op jit(solution)/shard_map/ppermute | solution.py:30
  66.7 0.0 collective-permute-done.13
  66.7 5.4 %collective-permute-start.14 = (bf16[112,1024]{1,0:T(8,128)(2,1)S(1)}, bf16[112,1024]{1,0:T(8,128)(2,1)S(1)}, u32[]{:S(2)}, u32[]{:S(2)}) collective-permute-start(bf16[112,1024]{1,0:T(8,128)(2,1)S(1)} %collective-permute-done.13), channel_id=1, source_target_pairs={{0,15},{1,0},{2,1},{3,2},{4,3},{5,4},{6,5},{7,6},{8,7},{9,8},{10,9... | collective-permute-start | bytes 688136 | tf_op jit(solution)/shard_map/ppermute | solution.py:33
  72.1 3.4 %collective-permute-done.6 = bf16[112,1024]{1,0:T(8,128)(2,1)S(1)} collective-permute-done((bf16[112,1024]{1,0:T(8,128)(2,1)S(1)}, bf16[112,1024]{1,0:T(8,128)(2,1)S(1)}, u32[]{:S(2)}, u32[]{:S(2)}) %collective-permute-start.6) | collective-permute-done | bytes 229408 | tf_op jit(solution)/shard_map/ppermute | solution.py:30
  75.5 1.9 %collective-permute-start.7 = (bf16[112,1024]{1,0:T(8,128)(2,1)S(1)}, bf16[112,1024]{1,0:T(8,128)(2,1)S(1)}, u32[]{:S(2)}, u32[]{:S(2)}) collective-permute-start(bf16[112,1024]{1,0:T(8,128)(2,1)S(1)} %collective-permute-done.6), channel_id=1, source_target_pairs={{0,1},{1,2},{2,3},{3,4},{4,5},{5,6},{6,7},{7,8},{8,9},{9,10},{10,1... | collective-permute-start | bytes 688136 | tf_op jit(solution)/shard_map/ppermute | solution.py:30
  77.5 7.2 %collective-permute-done.7 = bf16[112,1024]{1,0:T(8,128)(2,1)S(1)} collective-permute-done((bf16[112,1024]{1,0:T(8,128)(2,1)S(1)}, bf16[112,1024]{1,0:T(8,128)(2,1)S(1)}, u32[]{:S(2)}, u32[]{:S(2)}) %collective-permute-start.7) | collective-permute-done | bytes 229408 | tf_op jit(solution)/shard_map/ppermute | solution.py:30
  84.9 0.0 collective-permute-done.14
  84.9 0.0 collective-permute-done.15
  84.9 0.7 convolution_convert_fusion.2
  85.6 0.7 broadcast_select_fusion.3
  86.4 9.2 %all-gather = bf16[448,1024]{1,0:T(8,128)(2,1)S(1)} all-gather(bf16[224,1024]{1,0:T(8,128)(2,1)S(1)} %pad_maximum_fusion.2), channel_id=2, replica_groups={{0,16},{1,17},{2,18},{3,19},{4,20},{5,21},{6,22},{7,23},{8,24},{9,25},{..., dimensions={0}, use_global_device_ids=true | all-gather | bytes 1376256 | tf_op jit(solution)/shard_map/all_gather | solution.py:116
  95.6 0.2 convert_element_type.32
  95.8 0.1 fusion
  95.9 0.3 convolution_convert_fusion
  96.3 0.3 convolution_convert_fusion.1
  96.6 22.0 %all_to_all.5 = bf16[4,320,256]{2,1,0:T(8,128)(2,1)S(1)} all-to-all(bf16[4,320,256]{2,1,0:T(8,128)(2,1)S(1)} %bitcast.48), channel_id=1, replica_groups={{0,1,2,3},{4,5,6,7},{8,9,10,11},{12,13,14,15},{16,17,18,19},{20,21,22,2..., dimensions={0} | all-to-all | bytes 1310720 | tf_op jit(solution)/shard_map/all_to_all | solution.py:130
  118.7 0.1 reduce_sum.24
  118.8 26.5 %all-gather.1 = bf16[1280,256]{1,0:T(8,128)(2,1)S(1)} all-gather(bf16[320,256]{1,0:T(8,128)(2,1)S(1)} %reduce_sum.24), channel_id=3, replica_groups={{0,4,8,12},{1,5,9,13},{2,6,10,14},{3,7,11,15},{16,20,24,28},{17,21,25,2..., dimensions={0}, use_global_device_ids=true | all-gather | bytes 819200 | tf_op jit(solution)/shard_map/all_gather | solution.py:134
  145.3 0.1 reduce_sum.25
  145.5 2.7 %collective-permute-start.16 = (bf16[320,256]{1,0:T(8,128)(2,1)S(1)}, bf16[320,256]{1,0:T(8,128)(2,1)S(1)}, u32[]{:S(2)}, u32[]{:S(2)}) collective-permute-start(bf16[320,256]{1,0:T(8,128)(2,1)S(1)} %reduce_sum.25), channel_id=1, source_target_pairs={{0,16},{1,17},{2,18},{3,19},{4,20},{5,21},{6,22},{7,23},{8,24},{9,... | collective-permute-start | bytes 491528 | tf_op jit(solution)/shard_map/ppermute | solution.py:136
  148.2 15.4 %all-gather.2 = bf16[640,256]{1,0:T(8,128)(2,1)S(1)} all-gather(bf16[160,256]{1,0:T(8,128)(2,1)S(1)} %get-tuple-element.13), channel_id=4, replica_groups={{0,1,2,3},{4,5,6,7},{8,9,10,11},{12,13,14,15},{16,17,18,19},{20,21,22,2..., dimensions={0}, use_global_device_ids=true | all-gather | bytes 409600 | tf_op jit(solution)/shard_map/all_gather | solution.py:140
  163.6 0.0 collective-permute-done.16
  163.6 16.4 %all-gather.3 = bf16[1920,256]{1,0:T(8,128)(2,1)S(1)} all-gather(bf16[480,256]{1,0:T(8,128)(2,1)S(1)} %pad_maximum_fusion.3), channel_id=5, replica_groups={{0,1,2,3},{4,5,6,7},{8,9,10,11},{12,13,14,15},{16,17,18,19},{20,21,22,2..., dimensions={0}, use_global_device_ids=true | all-gather | bytes 1228800 | tf_op jit(solution)/shard_map/all_gather | solution.py:140
  180.0 0.3 broadcast_select_fusion
  180.2 1.7 finish.1
  (25 shorter events, 0.6 us)
Async XLA Ops:
  0.0 13.5 %copy-start = (bf16[112,3584]{1,0:T(8,128)(2,1)S(1)}, bf16[112,3584]{1,0:T(8,128)(2,1)}, u32[]{:S(2)}) copy-start(bf16[112,3584]{1,0:T(8,128)(2,1)} %param.2) | copy-start | bytes 2408452
  0.0 17.9 %copy-start.1 = (bf16[112,1024]{1,0:T(8,128)(2,1)S(1)}, bf16[112,1024]{1,0:T(8,128)(2,1)}, u32[]{:S(2)}) copy-start(bf16[112,1024]{1,0:T(8,128)(2,1)} %param.3) | copy-start | bytes 688132
  0.0 17.9 %collective-permute-start = (bf16[112,1024]{1,0:T(8,128)(2,1)}, bf16[112,1024]{1,0:T(8,128)(2,1)S(1)}, u32[]{:S(2)}, u32[]{:S(2)}) collective-permute-start(bf16[112,1024]{1,0:T(8,128)(2,1)} %param.3), channel_id=1, source_target_pairs={{0,1},{1,2},{2,3},{3,4},{4,5},{5,6},{6,7},{7,8},{8,9},{9,10},{10,1... | collective-permute-start | bytes 688136 | tf_op jit(solution)/shard_map/ppermute | solution.py:30
  4.0 15.9 %collective-permute-start.8 = (bf16[112,1024]{1,0:T(8,128)(2,1)}, bf16[112,1024]{1,0:T(8,128)(2,1)S(1)}, u32[]{:S(2)}, u32[]{:S(2)}) collective-permute-start(bf16[112,1024]{1,0:T(8,128)(2,1)} %param.3), channel_id=1, source_target_pairs={{0,15},{1,0},{2,1},{3,2},{4,3},{5,4},{6,5},{7,6},{8,7},{9,8},{10,9... | collective-permute-start | bytes 688136 | tf_op jit(solution)/shard_map/ppermute | solution.py:33
  13.5 71.4 %collective-permute-start.15 = (bf16[112,1792]{1,0:T(8,128)(2,1)S(1)}, bf16[112,1792]{1,0:T(8,128)(2,1)S(1)}, u32[]{:S(2)}, u32[]{:S(2)}) collective-permute-start(bf16[112,1792]{1,0:T(8,128)(2,1)S(1)} %constant_dynamic-slice_fusion.1), channel_id=1, source_target_pairs={{0,16},{1,17},{2,18},{3,19},{4,20},{5,21},{6,22},{7,23},{8,24},{9,... | collective-permute-start | bytes 1204232 | tf_op jit(solution)/shard_map/ppermute | solution.py:102
  17.9 9.9 %collective-permute-start.1 = (bf16[112,1024]{1,0:T(8,128)(2,1)S(1)}, bf16[112,1024]{1,0:T(8,128)(2,1)S(1)}, u32[]{:S(2)}, u32[]{:S(2)}) collective-permute-start(bf16[112,1024]{1,0:T(8,128)(2,1)S(1)} %collective-permute-done), channel_id=1, source_target_pairs={{0,1},{1,2},{2,3},{3,4},{4,5},{5,6},{6,7},{7,8},{8,9},{9,10},{10,1... | collective-permute-start | bytes 688136 | tf_op jit(solution)/shard_map/ppermute | solution.py:30
  19.9 9.9 %collective-permute-start.9 = (bf16[112,1024]{1,0:T(8,128)(2,1)S(1)}, bf16[112,1024]{1,0:T(8,128)(2,1)S(1)}, u32[]{:S(2)}, u32[]{:S(2)}) collective-permute-start(bf16[112,1024]{1,0:T(8,128)(2,1)S(1)} %collective-permute-done.8), channel_id=1, source_target_pairs={{0,15},{1,0},{2,1},{3,2},{4,3},{5,4},{6,5},{7,6},{8,7},{9,8},{10,9... | collective-permute-start | bytes 688136 | tf_op jit(solution)/shard_map/ppermute | solution.py:33
  27.8 9.1 %collective-permute-start.2 = (bf16[112,1024]{1,0:T(8,128)(2,1)S(1)}, bf16[112,1024]{1,0:T(8,128)(2,1)S(1)}, u32[]{:S(2)}, u32[]{:S(2)}) collective-permute-start(bf16[112,1024]{1,0:T(8,128)(2,1)S(1)} %collective-permute-done.1), channel_id=1, source_target_pairs={{0,1},{1,2},{2,3},{3,4},{4,5},{5,6},{6,7},{7,8},{8,9},{9,10},{10,1... | collective-permute-start | bytes 688136 | tf_op jit(solution)/shard_map/ppermute | solution.py:30
  29.7 9.1 %collective-permute-start.10 = (bf16[112,1024]{1,0:T(8,128)(2,1)S(1)}, bf16[112,1024]{1,0:T(8,128)(2,1)S(1)}, u32[]{:S(2)}, u32[]{:S(2)}) collective-permute-start(bf16[112,1024]{1,0:T(8,128)(2,1)S(1)} %collective-permute-done.9), channel_id=1, source_target_pairs={{0,15},{1,0},{2,1},{3,2},{4,3},{5,4},{6,5},{7,6},{8,7},{9,8},{10,9... | collective-permute-start | bytes 688136 | tf_op jit(solution)/shard_map/ppermute | solution.py:33
  36.9 9.1 %collective-permute-start.3 = (bf16[112,1024]{1,0:T(8,128)(2,1)S(1)}, bf16[112,1024]{1,0:T(8,128)(2,1)S(1)}, u32[]{:S(2)}, u32[]{:S(2)}) collective-permute-start(bf16[112,1024]{1,0:T(8,128)(2,1)S(1)} %collective-permute-done.2), channel_id=1, source_target_pairs={{0,1},{1,2},{2,3},{3,4},{4,5},{5,6},{6,7},{7,8},{8,9},{9,10},{10,1... | collective-permute-start | bytes 688136 | tf_op jit(solution)/shard_map/ppermute | solution.py:30
  38.8 9.1 %collective-permute-start.11 = (bf16[112,1024]{1,0:T(8,128)(2,1)S(1)}, bf16[112,1024]{1,0:T(8,128)(2,1)S(1)}, u32[]{:S(2)}, u32[]{:S(2)}) collective-permute-start(bf16[112,1024]{1,0:T(8,128)(2,1)S(1)} %collective-permute-done.10), channel_id=1, source_target_pairs={{0,15},{1,0},{2,1},{3,2},{4,3},{5,4},{6,5},{7,6},{8,7},{9,8},{10,9... | collective-permute-start | bytes 688136 | tf_op jit(solution)/shard_map/ppermute | solution.py:33
  46.0 9.1 %collective-permute-start.4 = (bf16[112,1024]{1,0:T(8,128)(2,1)S(1)}, bf16[112,1024]{1,0:T(8,128)(2,1)S(1)}, u32[]{:S(2)}, u32[]{:S(2)}) collective-permute-start(bf16[112,1024]{1,0:T(8,128)(2,1)S(1)} %collective-permute-done.3), channel_id=1, source_target_pairs={{0,1},{1,2},{2,3},{3,4},{4,5},{5,6},{6,7},{7,8},{8,9},{9,10},{10,1... | collective-permute-start | bytes 688136 | tf_op jit(solution)/shard_map/ppermute | solution.py:30
  48.0 9.1 %collective-permute-start.12 = (bf16[112,1024]{1,0:T(8,128)(2,1)S(1)}, bf16[112,1024]{1,0:T(8,128)(2,1)S(1)}, u32[]{:S(2)}, u32[]{:S(2)}) collective-permute-start(bf16[112,1024]{1,0:T(8,128)(2,1)S(1)} %collective-permute-done.11), channel_id=1, source_target_pairs={{0,15},{1,0},{2,1},{3,2},{4,3},{5,4},{6,5},{7,6},{8,7},{9,8},{10,9... | collective-permute-start | bytes 688136 | tf_op jit(solution)/shard_map/ppermute | solution.py:33
  55.1 9.6 %collective-permute-start.5 = (bf16[112,1024]{1,0:T(8,128)(2,1)S(1)}, bf16[112,1024]{1,0:T(8,128)(2,1)S(1)}, u32[]{:S(2)}, u32[]{:S(2)}) collective-permute-start(bf16[112,1024]{1,0:T(8,128)(2,1)S(1)} %collective-permute-done.4), channel_id=1, source_target_pairs={{0,1},{1,2},{2,3},{3,4},{4,5},{5,6},{6,7},{7,8},{8,9},{9,10},{10,1... | collective-permute-start | bytes 688136 | tf_op jit(solution)/shard_map/ppermute | solution.py:30
  57.1 9.6 %collective-permute-start.13 = (bf16[112,1024]{1,0:T(8,128)(2,1)S(1)}, bf16[112,1024]{1,0:T(8,128)(2,1)S(1)}, u32[]{:S(2)}, u32[]{:S(2)}) collective-permute-start(bf16[112,1024]{1,0:T(8,128)(2,1)S(1)} %collective-permute-done.12), channel_id=1, source_target_pairs={{0,15},{1,0},{2,1},{3,2},{4,3},{5,4},{6,5},{7,6},{8,7},{9,8},{10,9... | collective-permute-start | bytes 688136 | tf_op jit(solution)/shard_map/ppermute | solution.py:33
  64.8 10.8 %collective-permute-start.6 = (bf16[112,1024]{1,0:T(8,128)(2,1)S(1)}, bf16[112,1024]{1,0:T(8,128)(2,1)S(1)}, u32[]{:S(2)}, u32[]{:S(2)}) collective-permute-start(bf16[112,1024]{1,0:T(8,128)(2,1)S(1)} %collective-permute-done.5), channel_id=1, source_target_pairs={{0,1},{1,2},{2,3},{3,4},{4,5},{5,6},{6,7},{7,8},{8,9},{9,10},{10,1... | collective-permute-start | bytes 688136 | tf_op jit(solution)/shard_map/ppermute | solution.py:30
  66.7 18.2 %collective-permute-start.14 = (bf16[112,1024]{1,0:T(8,128)(2,1)S(1)}, bf16[112,1024]{1,0:T(8,128)(2,1)S(1)}, u32[]{:S(2)}, u32[]{:S(2)}) collective-permute-start(bf16[112,1024]{1,0:T(8,128)(2,1)S(1)} %collective-permute-done.13), channel_id=1, source_target_pairs={{0,15},{1,0},{2,1},{3,2},{4,3},{5,4},{6,5},{7,6},{8,7},{9,8},{10,9... | collective-permute-start | bytes 688136 | tf_op jit(solution)/shard_map/ppermute | solution.py:33
  75.5 9.1 %collective-permute-start.7 = (bf16[112,1024]{1,0:T(8,128)(2,1)S(1)}, bf16[112,1024]{1,0:T(8,128)(2,1)S(1)}, u32[]{:S(2)}, u32[]{:S(2)}) collective-permute-start(bf16[112,1024]{1,0:T(8,128)(2,1)S(1)} %collective-permute-done.6), channel_id=1, source_target_pairs={{0,1},{1,2},{2,3},{3,4},{4,5},{5,6},{6,7},{7,8},{8,9},{9,10},{10,1... | collective-permute-start | bytes 688136 | tf_op jit(solution)/shard_map/ppermute | solution.py:30
  145.5 18.1 %collective-permute-start.16 = (bf16[320,256]{1,0:T(8,128)(2,1)S(1)}, bf16[320,256]{1,0:T(8,128)(2,1)S(1)}, u32[]{:S(2)}, u32[]{:S(2)}) collective-permute-start(bf16[320,256]{1,0:T(8,128)(2,1)S(1)} %reduce_sum.25), channel_id=1, source_target_pairs={{0,16},{1,17},{2,18},{3,19},{4,20},{5,21},{6,22},{7,23},{8,24},{9,... | collective-permute-start | bytes 491528 | tf_op jit(solution)/shard_map/ppermute | solution.py:136

commit v7 on v6

--- a/solution.py
+++ b/solution.py
@@ -39,34 +39,48 @@
     return lax.dynamic_update_slice(full, block[None], (z % Z, 0, 0))
 
 
-def finish_kernel(order, low_ref, high_ref, power_ref, out_ref):
-    held = {
-        (0, 0): (low_ref, 0), (0, 1): (low_ref, 1), (1, 1): (low_ref, 2), (2, 0): (low_ref, 3), (3, 0): (low_ref, 4),
-        (2, 2): (high_ref, 0), (2, 3): (high_ref, 1), (3, 3): (high_ref, 2), (2, 1): (high_ref, 3), (3, 1): (high_ref, 4),
-    }
+def finish_kernel(order, low_ref, high_ref, power_ref, out_ref, square_ref):
     columns = power_ref.shape[1]
     chunk = columns // 4
+    q = chunk // 2
+    held = {
+        (0, 1): (low_ref, 3 * q), (2, 0): (low_ref, 5 * q), (3, 0): (low_ref, 7 * q),
+        (2, 3): (high_ref, 3 * q), (2, 1): (high_ref, 5 * q), (3, 1): (high_ref, 7 * q),
+    }
+    row = lax.broadcasted_iota(jnp.int32, (q, q), 0)
+    column = lax.broadcasted_iota(jnp.int32, (q, q), 1)
+    diagonal = jnp.zeros((q, q), jnp.float32)
+    for d in range(4):
+        ref, i = (low_ref, high_ref)[d // 2], d % 2
+        upper, lower = ref[i * q:(i + 1) * q, :q], ref[i * q:(i + 1) * q, q:]
+        side = ref[2 * q:3 * q, i * q:(i + 1) * q]
+        square_ref[d, :q, :q] = upper
+        square_ref[d, :q, q:] = side
+        square_ref[d, q:, :q] = side.astype(jnp.float32).T.astype(jnp.bfloat16)
+        square_ref[d, q:, q:] = lower
+        both = upper.astype(jnp.float32) + lower.astype(jnp.float32)
+        diagonal += jnp.where(row == column, both, 0.0)
+    ratio = columns / (3.0 * jnp.sum(diagonal, keepdims=True))
+    scale = math.sqrt(order) * jnp.sqrt(ratio)
 
     def times_gram(left, c):
         total = None
         for d in range(4):
-            ref, i = held[(d, c)] if (d, c) in held else held[(c, d)]
-            contract = 0 if (d, c) in held else 1
+            contract = 0
+            if d == c:
+                block = square_ref[d]
+            elif (d, c) in held:
+                ref, start = held[(d, c)]
+                block = ref[start:start + chunk, :]
+            else:
+                ref, start = held[(c, d)]
+                block = ref[start:start + chunk, :]
+                contract = 1
             term = lax.dot_general(
-                left[d], ref[i * chunk:(i + 1) * chunk, :], (((1,), (contract,)), ((), ())),
-                preferred_element_type=jnp.float32,
+                left[d], block, (((1,), (contract,)), ((), ())), preferred_element_type=jnp.float32
             )
             total = term if total is None else total + term
         return total
-
-    row = lax.broadcasted_iota(jnp.int32, (chunk, chunk), 0)
-    column = lax.broadcasted_iota(jnp.int32, (chunk, chunk), 1)
-    diagonal = jnp.zeros((chunk, chunk), jnp.float32)
-    for ref, i in (held[(d, d)] for d in range(4)):
-        block = ref[i * chunk:(i + 1) * chunk, :].astype(jnp.float32)
-        diagonal += jnp.where(row == column, block, 0.0)
-    ratio = columns / (3.0 * jnp.sum(diagonal, keepdims=True))
-    scale = math.sqrt(order) * jnp.sqrt(ratio)
 
     power = [power_ref[:, d * chunk:(d + 1) * chunk] for d in range(4)]
     first_full = [times_gram(power, c) * ratio for c in range(4)]
@@ -77,12 +91,48 @@
         out_ref[:, c * chunk:(c + 1) * chunk] = (scale * mixed).astype(jnp.bfloat16)
 
 
+def unique_kernel(y_ref, plane_ref, out_ref):
+    chunk = plane_ref.shape[1] // 4
+    q = chunk // 2
+
+    def cross(a, b):
+        left, right = plane_ref[:, a * chunk:(a + 1) * chunk], plane_ref[:, b * chunk:(b + 1) * chunk]
+        product = lax.dot_general(left, right, (((0,), (0,)), ((), ())), preferred_element_type=jnp.float32)
+        return product.astype(jnp.bfloat16)
+
+    for side in range(2):
+
+        @pl.when(y_ref[0] == side)
+        def _(side=side):
+            for i in range(2):
+                square = cross(2 * side + i, 2 * side + i)
+                out_ref[i * q:(i + 1) * q, :q] = square[:q, :q]
+                out_ref[i * q:(i + 1) * q, q:] = square[q:, q:]
+                out_ref[2 * q:3 * q, i * q:(i + 1) * q] = square[:q, q:]
+            out_ref[3 * q:5 * q, :] = cross(2 * side, 2 * side + 1)
+            out_ref[5 * q:7 * q, :] = cross(2, side)
+            out_ref[7 * q:9 * q, :] = cross(3, side)
+
+
+def unique_blocks(plane, y):
+    chunk = plane.shape[1] // 4
+    return pl.pallas_call(
+        unique_kernel,
+        out_shape=jax.ShapeDtypeStruct((9 * chunk // 2, chunk), jnp.bfloat16),
+        in_specs=[pl.BlockSpec(memory_space=pltpu.SMEM), pl.BlockSpec(memory_space=pltpu.VMEM)],
+        out_specs=pl.BlockSpec(memory_space=pltpu.VMEM),
+        compiler_params=pltpu.CompilerParams(vmem_limit_bytes=32 * 1024 * 1024),
+        name="unique_blocks",
+    )(y.astype(jnp.int32).reshape(1), plane)
+
+
 def finish(low, high, power, order):
     return pl.pallas_call(
         functools.partial(finish_kernel, order),
         out_shape=jax.ShapeDtypeStruct(power.shape, jnp.bfloat16),
         in_specs=[pl.BlockSpec(memory_space=pltpu.VMEM)] * 3,
         out_specs=pl.BlockSpec(memory_space=pltpu.VMEM),
+        scratch_shapes=[pltpu.VMEM((4, power.shape[1] // 4, power.shape[1] // 4), jnp.bfloat16)],
         compiler_params=pltpu.CompilerParams(vmem_limit_bytes=32 * 1024 * 1024),
         name="finish",
     )(low, high, power)
@@ -91,7 +141,6 @@
 def body(factor_rows, basis):
     rows, order = factor_rows.shape
     columns = basis.shape[1]
-    half = columns // 2
     chunk = columns // 4
     position = lax.axis_index(AXIS)
     y, z = position // Z, position % Z
@@ -110,22 +159,13 @@
         full = place(full, part, z + step + 1)
     full = full.reshape(span, columns)
 
-    near = jnp.dot(own_columns, full, preferred_element_type=jnp.float32).astype(jnp.bfloat16)
-    far = jnp.dot(far_columns, full, preferred_element_type=jnp.float32).astype(jnp.bfloat16)
+    near = jnp.dot(own_columns, full, preferred_element_type=jnp.float32)
+    far = jnp.dot(far_columns, full, preferred_element_type=jnp.float32)
     terms = jnp.concatenate([jnp.where(first_row, near, far), jnp.where(first_row, far, near)], 0)
-    terms = lax.all_gather(terms, AXIS, axis=0, axis_index_groups=PAIRS).astype(jnp.float32)
-    plane = (terms[0] + terms[1]).astype(jnp.bfloat16)
+    sent = lax.all_gather(terms.astype(jnp.bfloat16), AXIS, axis=0, axis_index_groups=PAIRS)
+    plane = (terms + jnp.where(first_row, sent[1], sent[0]).astype(jnp.float32)).astype(jnp.bfloat16)
     power = lax.dynamic_slice_in_dim(plane, y * rows, rows, 0)
-    tile = lax.dynamic_slice_in_dim(plane, y * half, half, 1)
-
-    def cross(a, b):
-        return lax.dot_general(a, b, (((0,), (0,)), ((), ())), preferred_element_type=jnp.float32)
-
-    square = cross(tile, tile).astype(jnp.bfloat16)
-    strip = cross(plane[:, half:], lax.dynamic_slice_in_dim(plane, y * chunk, chunk, 1)).astype(jnp.bfloat16)
-    blocks = jnp.concatenate(
-        [square[:chunk, :chunk], square[:chunk, chunk:], square[chunk:, chunk:], strip], 0
-    )
+    blocks = unique_blocks(plane, y)
     blocks, power = lax.optimization_barrier((blocks, power))
     parts = lax.all_to_all(
         blocks.reshape(CUBE, -1, chunk), AXIS, 0, 0, axis_index_groups=NEAR

time: 183 us -> 178 us (0.973)
  blocking collectives: 89.5 us -> 85.5 us
    all_to_all x1, blocking collectives: 22 us -> 20.1 us  [body(): lax.all_to_all(blocks.reshape(CUBE, -1, chunk), AXIS, 0, 0, axis_index_gr...]
    all_gather x1, blocking collectives: 26.5 us -> 24.6 us  [body(): parts = lax.all_gather(part, AXIS, axis=0, axis_index_groups=FAR)]
where the time goes in v7:
time: 178 us
  blocking collectives  85.5 us (48%)
  starting transfers between devices  64.3 us (36%)
  waiting for transfers between devices  21.9 us (12%)
  Pallas kernels  2.21 us (1%)
    ppermute x7, starting transfers between devices, ring(): b = lax.ppermute(b, AXIS, shift(-1))  40.6 us
    all_gather x2, blocking collectives, near(): return lax.all_gather(piece, AXIS, axis=0, axis_index_groups=NEAR)  31.7 us
    all_gather x1, blocking collectives, body(): parts = lax.all_gather(part, AXIS, axis=0, axis_index_groups=FAR)  24.6 us
    ppermute x8, waiting for transfers between devices, ring(): a = lax.ppermute(a, AXIS, shift(1))  21.9 us
    all_to_all x1, blocking collectives, body(): lax.all_to_all(blocks.reshape(CUBE, -1, chunk), AXIS, 0, 0, axis_index_gr...  20.1 us
    ppermute x8, starting transfers between devices, ring(): a = lax.ppermute(a, AXIS, shift(1))  17.3 us
    all_gather x1, blocking collectives, body(): lax.all_gather(terms.astype(jnp.bfloat16), AXIS, axis=0, axis_index_group...  9.16 us
  transfers between devices with their start and end apart: 17, of which 7 were waited for; matrix products, arithmetic and copies ran while one was open for 0% of the time, Pallas kernels for 0%

profile of v7, /device:TPU:6, one launch (start us, length us, event | category | flops | bytes accessed | tf_op | source)
XLA Modules:
  0.0 177.8 jit_solution(14177177256086244943)
XLA Ops:
  0.0 0.0 copy-start
  0.0 0.0 copy-start.1
  0.0 3.9 %collective-permute-start = (bf16[112,1024]{1,0:T(8,128)(2,1)}, bf16[112,1024]{1,0:T(8,128)(2,1)S(1)}, u32[]{:S(2)}, u32[]{:S(2)}) collective-permute-start(bf16[112,1024]{1,0:T(8,128)(2,1)} %param.3), channel_id=1, source_target_pairs={{0,1},{1,2},{2,3},{3,4},{4,5},{5,6},{6,7},{7,8},{8,9},{9,10},{10,1... | collective-permute-start | bytes 688136 | tf_op jit(solution)/shard_map/ppermute | solution.py:30
  4.0 9.5 %collective-permute-start.8 = (bf16[112,1024]{1,0:T(8,128)(2,1)}, bf16[112,1024]{1,0:T(8,128)(2,1)S(1)}, u32[]{:S(2)}, u32[]{:S(2)}) collective-permute-start(bf16[112,1024]{1,0:T(8,128)(2,1)} %param.3), channel_id=1, source_target_pairs={{0,15},{1,0},{2,1},{3,2},{4,3},{5,4},{6,5},{7,6},{8,7},{9,8},{10,9... | collective-permute-start | bytes 688136 | tf_op jit(solution)/shard_map/ppermute | solution.py:33
  13.5 0.0 copy-done
  13.5 3.5 %collective-permute-start.15 = (bf16[112,1792]{1,0:T(8,128)(2,1)S(1)}, bf16[112,1792]{1,0:T(8,128)(2,1)S(1)}, u32[]{:S(2)}, u32[]{:S(2)}) collective-permute-start(bf16[112,1792]{1,0:T(8,128)(2,1)S(1)} %constant_dynamic-slice_fusion.1), channel_id=1, source_target_pairs={{0,16},{1,17},{2,18},{3,19},{4,20},{5,21},{6,22},{7,23},{8,24},{9,... | collective-permute-start | bytes 1204232 | tf_op jit(solution)/shard_map/ppermute | solution.py:151
  17.4 0.5 broadcast_in_dim.51
  17.8 0.0 copy-done.1
  17.9 0.0 collective-permute-done
  17.9 1.9 %collective-permute-start.1 = (bf16[112,1024]{1,0:T(8,128)(2,1)S(1)}, bf16[112,1024]{1,0:T(8,128)(2,1)S(1)}, u32[]{:S(2)}, u32[]{:S(2)}) collective-permute-start(bf16[112,1024]{1,0:T(8,128)(2,1)S(1)} %collective-permute-done), channel_id=1, source_target_pairs={{0,1},{1,2},{2,3},{3,4},{4,5},{5,6},{6,7},{7,8},{8,9},{9,10},{10,1... | collective-permute-start | bytes 688136 | tf_op jit(solution)/shard_map/ppermute | solution.py:30
  19.8 0.0 collective-permute-done.8
  19.8 5.1 %collective-permute-start.9 = (bf16[112,1024]{1,0:T(8,128)(2,1)S(1)}, bf16[112,1024]{1,0:T(8,128)(2,1)S(1)}, u32[]{:S(2)}, u32[]{:S(2)}) collective-permute-start(bf16[112,1024]{1,0:T(8,128)(2,1)S(1)} %collective-permute-done.8), channel_id=1, source_target_pairs={{0,15},{1,0},{2,1},{3,2},{4,3},{5,4},{6,5},{7,6},{8,7},{9,8},{10,9... | collective-permute-start | bytes 688136 | tf_op jit(solution)/shard_map/ppermute | solution.py:33
  25.0 2.8 %collective-permute-done.1 = bf16[112,1024]{1,0:T(8,128)(2,1)S(1)} collective-permute-done((bf16[112,1024]{1,0:T(8,128)(2,1)S(1)}, bf16[112,1024]{1,0:T(8,128)(2,1)S(1)}, u32[]{:S(2)}, u32[]{:S(2)}) %collective-permute-start.1) | collective-permute-done | bytes 229408 | tf_op jit(solution)/shard_map/ppermute | solution.py:30
  27.8 1.9 %collective-permute-start.2 = (bf16[112,1024]{1,0:T(8,128)(2,1)S(1)}, bf16[112,1024]{1,0:T(8,128)(2,1)S(1)}, u32[]{:S(2)}, u32[]{:S(2)}) collective-permute-start(bf16[112,1024]{1,0:T(8,128)(2,1)S(1)} %collective-permute-done.1), channel_id=1, source_target_pairs={{0,1},{1,2},{2,3},{3,4},{4,5},{5,6},{6,7},{7,8},{8,9},{9,10},{10,1... | collective-permute-start | bytes 688136 | tf_op jit(solution)/shard_map/ppermute | solution.py:30
  29.7 0.0 collective-permute-done.9
  29.7 5.1 %collective-permute-start.10 = (bf16[112,1024]{1,0:T(8,128)(2,1)S(1)}, bf16[112,1024]{1,0:T(8,128)(2,1)S(1)}, u32[]{:S(2)}, u32[]{:S(2)}) collective-permute-start(bf16[112,1024]{1,0:T(8,128)(2,1)S(1)} %collective-permute-done.9), channel_id=1, source_target_pairs={{0,15},{1,0},{2,1},{3,2},{4,3},{5,4},{6,5},{7,6},{8,7},{9,8},{10,9... | collective-permute-start | bytes 688136 | tf_op jit(solution)/shard_map/ppermute | solution.py:33
  34.9 2.0 %collective-permute-done.2 = bf16[112,1024]{1,0:T(8,128)(2,1)S(1)} collective-permute-done((bf16[112,1024]{1,0:T(8,128)(2,1)S(1)}, bf16[112,1024]{1,0:T(8,128)(2,1)S(1)}, u32[]{:S(2)}, u32[]{:S(2)}) %collective-permute-start.2) | collective-permute-done | bytes 229408 | tf_op jit(solution)/shard_map/ppermute | solution.py:30
  36.9 1.9 %collective-permute-start.3 = (bf16[112,1024]{1,0:T(8,128)(2,1)S(1)}, bf16[112,1024]{1,0:T(8,128)(2,1)S(1)}, u32[]{:S(2)}, u32[]{:S(2)}) collective-permute-start(bf16[112,1024]{1,0:T(8,128)(2,1)S(1)} %collective-permute-done.2), channel_id=1, source_target_pairs={{0,1},{1,2},{2,3},{3,4},{4,5},{5,6},{6,7},{7,8},{8,9},{9,10},{10,1... | collective-permute-start | bytes 688136 | tf_op jit(solution)/shard_map/ppermute | solution.py:30
  38.8 0.0 collective-permute-done.10
  38.8 5.1 %collective-permute-start.11 = (bf16[112,1024]{1,0:T(8,128)(2,1)S(1)}, bf16[112,1024]{1,0:T(8,128)(2,1)S(1)}, u32[]{:S(2)}, u32[]{:S(2)}) collective-permute-start(bf16[112,1024]{1,0:T(8,128)(2,1)S(1)} %collective-permute-done.10), channel_id=1, source_target_pairs={{0,15},{1,0},{2,1},{3,2},{4,3},{5,4},{6,5},{7,6},{8,7},{9,8},{10,9... | collective-permute-start | bytes 688136 | tf_op jit(solution)/shard_map/ppermute | solution.py:33
  44.0 2.0 %collective-permute-done.3 = bf16[112,1024]{1,0:T(8,128)(2,1)S(1)} collective-permute-done((bf16[112,1024]{1,0:T(8,128)(2,1)S(1)}, bf16[112,1024]{1,0:T(8,128)(2,1)S(1)}, u32[]{:S(2)}, u32[]{:S(2)}) %collective-permute-start.3) | collective-permute-done | bytes 229408 | tf_op jit(solution)/shard_map/ppermute | solution.py:30
  46.0 1.9 %collective-permute-start.4 = (bf16[112,1024]{1,0:T(8,128)(2,1)S(1)}, bf16[112,1024]{1,0:T(8,128)(2,1)S(1)}, u32[]{:S(2)}, u32[]{:S(2)}) collective-permute-start(bf16[112,1024]{1,0:T(8,128)(2,1)S(1)} %collective-permute-done.3), channel_id=1, source_target_pairs={{0,1},{1,2},{2,3},{3,4},{4,5},{5,6},{6,7},{7,8},{8,9},{9,10},{10,1... | collective-permute-start | bytes 688136 | tf_op jit(solution)/shard_map/ppermute | solution.py:30
  47.9 0.0 collective-permute-done.11
  47.9 5.1 %collective-permute-start.12 = (bf16[112,1024]{1,0:T(8,128)(2,1)S(1)}, bf16[112,1024]{1,0:T(8,128)(2,1)S(1)}, u32[]{:S(2)}, u32[]{:S(2)}) collective-permute-start(bf16[112,1024]{1,0:T(8,128)(2,1)S(1)} %collective-permute-done.11), channel_id=1, source_target_pairs={{0,15},{1,0},{2,1},{3,2},{4,3},{5,4},{6,5},{7,6},{8,7},{9,8},{10,9... | collective-permute-start | bytes 688136 | tf_op jit(solution)/shard_map/ppermute | solution.py:33
  53.1 2.0 %collective-permute-done.4 = bf16[112,1024]{1,0:T(8,128)(2,1)S(1)} collective-permute-done((bf16[112,1024]{1,0:T(8,128)(2,1)S(1)}, bf16[112,1024]{1,0:T(8,128)(2,1)S(1)}, u32[]{:S(2)}, u32[]{:S(2)}) %collective-permute-start.4) | collective-permute-done | bytes 229408 | tf_op jit(solution)/shard_map/ppermute | solution.py:30
  55.1 1.9 %collective-permute-start.5 = (bf16[112,1024]{1,0:T(8,128)(2,1)S(1)}, bf16[112,1024]{1,0:T(8,128)(2,1)S(1)}, u32[]{:S(2)}, u32[]{:S(2)}) collective-permute-start(bf16[112,1024]{1,0:T(8,128)(2,1)S(1)} %collective-permute-done.4), channel_id=1, source_target_pairs={{0,1},{1,2},{2,3},{3,4},{4,5},{5,6},{6,7},{7,8},{8,9},{9,10},{10,1... | collective-permute-start | bytes 688136 | tf_op jit(solution)/shard_map/ppermute | solution.py:30
  57.0 0.0 collective-permute-done.12
  57.1 5.1 %collective-permute-start.13 = (bf16[112,1024]{1,0:T(8,128)(2,1)S(1)}, bf16[112,1024]{1,0:T(8,128)(2,1)S(1)}, u32[]{:S(2)}, u32[]{:S(2)}) collective-permute-start(bf16[112,1024]{1,0:T(8,128)(2,1)S(1)} %collective-permute-done.12), channel_id=1, source_target_pairs={{0,15},{1,0},{2,1},{3,2},{4,3},{5,4},{6,5},{7,6},{8,7},{9,8},{10,9... | collective-permute-start | bytes 688136 | tf_op jit(solution)/shard_map/ppermute | solution.py:33
  62.2 2.5 %collective-permute-done.5 = bf16[112,1024]{1,0:T(8,128)(2,1)S(1)} collective-permute-done((bf16[112,1024]{1,0:T(8,128)(2,1)S(1)}, bf16[112,1024]{1,0:T(8,128)(2,1)S(1)}, u32[]{:S(2)}, u32[]{:S(2)}) %collective-permute-start.5) | collective-permute-done | bytes 229408 | tf_op jit(solution)/shard_map/ppermute | solution.py:30
  64.7 1.9 %collective-permute-start.6 = (bf16[112,1024]{1,0:T(8,128)(2,1)S(1)}, bf16[112,1024]{1,0:T(8,128)(2,1)S(1)}, u32[]{:S(2)}, u32[]{:S(2)}) collective-permute-start(bf16[112,1024]{1,0:T(8,128)(2,1)S(1)} %collective-permute-done.5), channel_id=1, source_target_pairs={{0,1},{1,2},{2,3},{3,4},{4,5},{5,6},{6,7},{7,8},{8,9},{9,10},{10,1... | collective-permute-start | bytes 688136 | tf_op jit(solution)/shard_map/ppermute | solution.py:30
  66.7 0.0 collective-permute-done.13
  66.7 5.4 %collective-permute-start.14 = (bf16[112,1024]{1,0:T(8,128)(2,1)S(1)}, bf16[112,1024]{1,0:T(8,128)(2,1)S(1)}, u32[]{:S(2)}, u32[]{:S(2)}) collective-permute-start(bf16[112,1024]{1,0:T(8,128)(2,1)S(1)} %collective-permute-done.13), channel_id=1, source_target_pairs={{0,15},{1,0},{2,1},{3,2},{4,3},{5,4},{6,5},{7,6},{8,7},{9,8},{10,9... | collective-permute-start | bytes 688136 | tf_op jit(solution)/shard_map/ppermute | solution.py:33
  72.1 3.4 %collective-permute-done.6 = bf16[112,1024]{1,0:T(8,128)(2,1)S(1)} collective-permute-done((bf16[112,1024]{1,0:T(8,128)(2,1)S(1)}, bf16[112,1024]{1,0:T(8,128)(2,1)S(1)}, u32[]{:S(2)}, u32[]{:S(2)}) %collective-permute-start.6) | collective-permute-done | bytes 229408 | tf_op jit(solution)/shard_map/ppermute | solution.py:30
  75.5 1.9 %collective-permute-start.7 = (bf16[112,1024]{1,0:T(8,128)(2,1)S(1)}, bf16[112,1024]{1,0:T(8,128)(2,1)S(1)}, u32[]{:S(2)}, u32[]{:S(2)}) collective-permute-start(bf16[112,1024]{1,0:T(8,128)(2,1)S(1)} %collective-permute-done.6), channel_id=1, source_target_pairs={{0,1},{1,2},{2,3},{3,4},{4,5},{5,6},{6,7},{7,8},{8,9},{9,10},{10,1... | collective-permute-start | bytes 688136 | tf_op jit(solution)/shard_map/ppermute | solution.py:30
  77.5 7.2 %collective-permute-done.7 = bf16[112,1024]{1,0:T(8,128)(2,1)S(1)} collective-permute-done((bf16[112,1024]{1,0:T(8,128)(2,1)S(1)}, bf16[112,1024]{1,0:T(8,128)(2,1)S(1)}, u32[]{:S(2)}, u32[]{:S(2)}) %collective-permute-start.7) | collective-permute-done | bytes 229408 | tf_op jit(solution)/shard_map/ppermute | solution.py:30
  84.8 0.0 collective-permute-done.14
  84.9 0.0 collective-permute-done.15
  84.9 0.7 fusion.8
  85.6 0.8 convert_bitcast_fusion.1
  86.4 9.2 %all_gather.22 = bf16[2,224,1024]{2,1,0:T(8,128)(2,1)S(1)} all-gather(bf16[1,224,1024]{2,1,0:T(8,128)(2,1)S(1)} %pad_maximum_fusion.1), channel_id=1, replica_groups={{0,16},{1,17},{2,18},{3,19},{4,20},{5,21},{6,22},{7,23},{8,24},{9,25},{..., dimensions={0}, use_global_device_ids=true | all-gather | bytes 1376256 | tf_op jit(solution)/shard_map/all_gather | solution.py:165
  95.6 0.2 fusion.plane_ref
  95.8 0.4 unique_blocks.1
  96.2 20.1 %all_to_all.5 = bf16[4,288,256]{2,1,0:T(8,128)(2,1)S(1)} all-to-all(bf16[4,288,256]{2,1,0:T(8,128)(2,1)S(1)} %bitcast.54), channel_id=1, replica_groups={{0,1,2,3},{4,5,6,7},{8,9,10,11},{12,13,14,15},{16,17,18,19},{20,21,22,2..., dimensions={0} | all-to-all | bytes 1179648 | tf_op jit(solution)/shard_map/all_to_all | solution.py:170
  116.3 0.1 reduce_sum.24
  116.4 24.6 %all-gather = bf16[1152,256]{1,0:T(8,128)(2,1)S(1)} all-gather(bf16[288,256]{1,0:T(8,128)(2,1)S(1)} %reduce_sum.24), channel_id=2, replica_groups={{0,4,8,12},{1,5,9,13},{2,6,10,14},{3,7,11,15},{16,20,24,28},{17,21,25,2..., dimensions={0}, use_global_device_ids=true | all-gather | bytes 737280 | tf_op jit(solution)/shard_map/all_gather | solution.py:174
  141.0 0.1 reduce_sum.25
  141.1 2.9 %collective-permute-start.16 = (bf16[288,256]{1,0:T(8,128)(2,1)S(1)}, bf16[288,256]{1,0:T(8,128)(2,1)S(1)}, u32[]{:S(2)}, u32[]{:S(2)}) collective-permute-start(bf16[288,256]{1,0:T(8,128)(2,1)S(1)} %reduce_sum.25), channel_id=1, source_target_pairs={{0,16},{1,17},{2,18},{3,19},{4,20},{5,21},{6,22},{7,23},{8,24},{9,... | collective-permute-start | bytes 442376 | tf_op jit(solution)/shard_map/ppermute | solution.py:176
  144.0 15.7 %all-gather.1 = bf16[576,256]{1,0:T(8,128)(2,1)S(1)} all-gather(bf16[144,256]{1,0:T(8,128)(2,1)S(1)} %get-tuple-element.17), channel_id=3, replica_groups={{0,1,2,3},{4,5,6,7},{8,9,10,11},{12,13,14,15},{16,17,18,19},{20,21,22,2..., dimensions={0}, use_global_device_ids=true | all-gather | bytes 368640 | tf_op jit(solution)/shard_map/all_gather | solution.py:180
  159.7 0.0 collective-permute-done.16
  159.7 16.0 %all-gather.2 = bf16[1728,256]{1,0:T(8,128)(2,1)S(1)} all-gather(bf16[432,256]{1,0:T(8,128)(2,1)S(1)} %pad_maximum_fusion.2), channel_id=4, replica_groups={{0,1,2,3},{4,5,6,7},{8,9,10,11},{12,13,14,15},{16,17,18,19},{20,21,22,2..., dimensions={0}, use_global_device_ids=true | all-gather | bytes 1105920 | tf_op jit(solution)/shard_map/all_gather | solution.py:180
  175.7 0.2 broadcast_select_fusion
  176.0 1.8 %finish.1 = bf16[112,1024]{1,0:T(8,128)(2,1)} custom-call(bf16[1152,256]{1,0:T(8,128)(2,1)S(1)} %bitcast.53, bf16[1152,256]{1,0:T(8,128)(2,1)S(1)} %bitcast.52, bf16[112,1024]{1,0:T(8,128)(2,1)S(1)} %constant_dynamic-slice_fusion.power_ref), custom_call_target="tpu_custom_call" | custom-call | tf_op jit(solution)/shard_map/finish/pallas_call | solution.py:130
  (22 shorter events, 0.5 us)
Async XLA Ops:
  0.0 13.5 %copy-start = (bf16[112,3584]{1,0:T(8,128)(2,1)S(1)}, bf16[112,3584]{1,0:T(8,128)(2,1)}, u32[]{:S(2)}) copy-start(bf16[112,3584]{1,0:T(8,128)(2,1)} %param.2) | copy-start | bytes 2408452
  0.0 17.8 %copy-start.1 = (bf16[112,1024]{1,0:T(8,128)(2,1)S(1)}, bf16[112,1024]{1,0:T(8,128)(2,1)}, u32[]{:S(2)}) copy-start(bf16[112,1024]{1,0:T(8,128)(2,1)} %param.3) | copy-start | bytes 688132
  0.0 17.9 %collective-permute-start = (bf16[112,1024]{1,0:T(8,128)(2,1)}, bf16[112,1024]{1,0:T(8,128)(2,1)S(1)}, u32[]{:S(2)}, u32[]{:S(2)}) collective-permute-start(bf16[112,1024]{1,0:T(8,128)(2,1)} %param.3), channel_id=1, source_target_pairs={{0,1},{1,2},{2,3},{3,4},{4,5},{5,6},{6,7},{7,8},{8,9},{9,10},{10,1... | collective-permute-start | bytes 688136 | tf_op jit(solution)/shard_map/ppermute | solution.py:30
  4.0 15.9 %collective-permute-start.8 = (bf16[112,1024]{1,0:T(8,128)(2,1)}, bf16[112,1024]{1,0:T(8,128)(2,1)S(1)}, u32[]{:S(2)}, u32[]{:S(2)}) collective-permute-start(bf16[112,1024]{1,0:T(8,128)(2,1)} %param.3), channel_id=1, source_target_pairs={{0,15},{1,0},{2,1},{3,2},{4,3},{5,4},{6,5},{7,6},{8,7},{9,8},{10,9... | collective-permute-start | bytes 688136 | tf_op jit(solution)/shard_map/ppermute | solution.py:33
  13.5 71.3 %collective-permute-start.15 = (bf16[112,1792]{1,0:T(8,128)(2,1)S(1)}, bf16[112,1792]{1,0:T(8,128)(2,1)S(1)}, u32[]{:S(2)}, u32[]{:S(2)}) collective-permute-start(bf16[112,1792]{1,0:T(8,128)(2,1)S(1)} %constant_dynamic-slice_fusion.1), channel_id=1, source_target_pairs={{0,16},{1,17},{2,18},{3,19},{4,20},{5,21},{6,22},{7,23},{8,24},{9,... | collective-permute-start | bytes 1204232 | tf_op jit(solution)/shard_map/ppermute | solution.py:151
  17.9 9.9 %collective-permute-start.1 = (bf16[112,1024]{1,0:T(8,128)(2,1)S(1)}, bf16[112,1024]{1,0:T(8,128)(2,1)S(1)}, u32[]{:S(2)}, u32[]{:S(2)}) collective-permute-start(bf16[112,1024]{1,0:T(8,128)(2,1)S(1)} %collective-permute-done), channel_id=1, source_target_pairs={{0,1},{1,2},{2,3},{3,4},{4,5},{5,6},{6,7},{7,8},{8,9},{9,10},{10,1... | collective-permute-start | bytes 688136 | tf_op jit(solution)/shard_map/ppermute | solution.py:30
  19.8 9.9 %collective-permute-start.9 = (bf16[112,1024]{1,0:T(8,128)(2,1)S(1)}, bf16[112,1024]{1,0:T(8,128)(2,1)S(1)}, u32[]{:S(2)}, u32[]{:S(2)}) collective-permute-start(bf16[112,1024]{1,0:T(8,128)(2,1)S(1)} %collective-permute-done.8), channel_id=1, source_target_pairs={{0,15},{1,0},{2,1},{3,2},{4,3},{5,4},{6,5},{7,6},{8,7},{9,8},{10,9... | collective-permute-start | bytes 688136 | tf_op jit(solution)/shard_map/ppermute | solution.py:33
  27.8 9.1 %collective-permute-start.2 = (bf16[112,1024]{1,0:T(8,128)(2,1)S(1)}, bf16[112,1024]{1,0:T(8,128)(2,1)S(1)}, u32[]{:S(2)}, u32[]{:S(2)}) collective-permute-start(bf16[112,1024]{1,0:T(8,128)(2,1)S(1)} %collective-permute-done.1), channel_id=1, source_target_pairs={{0,1},{1,2},{2,3},{3,4},{4,5},{5,6},{6,7},{7,8},{8,9},{9,10},{10,1... | collective-permute-start | bytes 688136 | tf_op jit(solution)/shard_map/ppermute | solution.py:30
  29.7 9.1 %collective-permute-start.10 = (bf16[112,1024]{1,0:T(8,128)(2,1)S(1)}, bf16[112,1024]{1,0:T(8,128)(2,1)S(1)}, u32[]{:S(2)}, u32[]{:S(2)}) collective-permute-start(bf16[112,1024]{1,0:T(8,128)(2,1)S(1)} %collective-permute-done.9), channel_id=1, source_target_pairs={{0,15},{1,0},{2,1},{3,2},{4,3},{5,4},{6,5},{7,6},{8,7},{9,8},{10,9... | collective-permute-start | bytes 688136 | tf_op jit(solution)/shard_map/ppermute | solution.py:33
  36.9 9.1 %collective-permute-start.3 = (bf16[112,1024]{1,0:T(8,128)(2,1)S(1)}, bf16[112,1024]{1,0:T(8,128)(2,1)S(1)}, u32[]{:S(2)}, u32[]{:S(2)}) collective-permute-start(bf16[112,1024]{1,0:T(8,128)(2,1)S(1)} %collective-permute-done.2), channel_id=1, source_target_pairs={{0,1},{1,2},{2,3},{3,4},{4,5},{5,6},{6,7},{7,8},{8,9},{9,10},{10,1... | collective-permute-start | bytes 688136 | tf_op jit(solution)/shard_map/ppermute | solution.py:30
  38.8 9.1 %collective-permute-start.11 = (bf16[112,1024]{1,0:T(8,128)(2,1)S(1)}, bf16[112,1024]{1,0:T(8,128)(2,1)S(1)}, u32[]{:S(2)}, u32[]{:S(2)}) collective-permute-start(bf16[112,1024]{1,0:T(8,128)(2,1)S(1)} %collective-permute-done.10), channel_id=1, source_target_pairs={{0,15},{1,0},{2,1},{3,2},{4,3},{5,4},{6,5},{7,6},{8,7},{9,8},{10,9... | collective-permute-start | bytes 688136 | tf_op jit(solution)/shard_map/ppermute | solution.py:33
  46.0 9.1 %collective-permute-start.4 = (bf16[112,1024]{1,0:T(8,128)(2,1)S(1)}, bf16[112,1024]{1,0:T(8,128)(2,1)S(1)}, u32[]{:S(2)}, u32[]{:S(2)}) collective-permute-start(bf16[112,1024]{1,0:T(8,128)(2,1)S(1)} %collective-permute-done.3), channel_id=1, source_target_pairs={{0,1},{1,2},{2,3},{3,4},{4,5},{5,6},{6,7},{7,8},{8,9},{9,10},{10,1... | collective-permute-start | bytes 688136 | tf_op jit(solution)/shard_map/ppermute | solution.py:30
  47.9 9.1 %collective-permute-start.12 = (bf16[112,1024]{1,0:T(8,128)(2,1)S(1)}, bf16[112,1024]{1,0:T(8,128)(2,1)S(1)}, u32[]{:S(2)}, u32[]{:S(2)}) collective-permute-start(bf16[112,1024]{1,0:T(8,128)(2,1)S(1)} %collective-permute-done.11), channel_id=1, source_target_pairs={{0,15},{1,0},{2,1},{3,2},{4,3},{5,4},{6,5},{7,6},{8,7},{9,8},{10,9... | collective-permute-start | bytes 688136 | tf_op jit(solution)/shard_map/ppermute | solution.py:33
  55.1 9.6 %collective-permute-start.5 = (bf16[112,1024]{1,0:T(8,128)(2,1)S(1)}, bf16[112,1024]{1,0:T(8,128)(2,1)S(1)}, u32[]{:S(2)}, u32[]{:S(2)}) collective-permute-start(bf16[112,1024]{1,0:T(8,128)(2,1)S(1)} %collective-permute-done.4), channel_id=1, source_target_pairs={{0,1},{1,2},{2,3},{3,4},{4,5},{5,6},{6,7},{7,8},{8,9},{9,10},{10,1... | collective-permute-start | bytes 688136 | tf_op jit(solution)/shard_map/ppermute | solution.py:30
  57.1 9.6 %collective-permute-start.13 = (bf16[112,1024]{1,0:T(8,128)(2,1)S(1)}, bf16[112,1024]{1,0:T(8,128)(2,1)S(1)}, u32[]{:S(2)}, u32[]{:S(2)}) collective-permute-start(bf16[112,1024]{1,0:T(8,128)(2,1)S(1)} %collective-permute-done.12), channel_id=1, source_target_pairs={{0,15},{1,0},{2,1},{3,2},{4,3},{5,4},{6,5},{7,6},{8,7},{9,8},{10,9... | collective-permute-start | bytes 688136 | tf_op jit(solution)/shard_map/ppermute | solution.py:33
  64.7 10.8 %collective-permute-start.6 = (bf16[112,1024]{1,0:T(8,128)(2,1)S(1)}, bf16[112,1024]{1,0:T(8,128)(2,1)S(1)}, u32[]{:S(2)}, u32[]{:S(2)}) collective-permute-start(bf16[112,1024]{1,0:T(8,128)(2,1)S(1)} %collective-permute-done.5), channel_id=1, source_target_pairs={{0,1},{1,2},{2,3},{3,4},{4,5},{5,6},{6,7},{7,8},{8,9},{9,10},{10,1... | collective-permute-start | bytes 688136 | tf_op jit(solution)/shard_map/ppermute | solution.py:30
  66.7 18.2 %collective-permute-start.14 = (bf16[112,1024]{1,0:T(8,128)(2,1)S(1)}, bf16[112,1024]{1,0:T(8,128)(2,1)S(1)}, u32[]{:S(2)}, u32[]{:S(2)}) collective-permute-start(bf16[112,1024]{1,0:T(8,128)(2,1)S(1)} %collective-permute-done.13), channel_id=1, source_target_pairs={{0,15},{1,0},{2,1},{3,2},{4,3},{5,4},{6,5},{7,6},{8,7},{9,8},{10,9... | collective-permute-start | bytes 688136 | tf_op jit(solution)/shard_map/ppermute | solution.py:33
  75.5 9.1 %collective-permute-start.7 = (bf16[112,1024]{1,0:T(8,128)(2,1)S(1)}, bf16[112,1024]{1,0:T(8,128)(2,1)S(1)}, u32[]{:S(2)}, u32[]{:S(2)}) collective-permute-start(bf16[112,1024]{1,0:T(8,128)(2,1)S(1)} %collective-permute-done.6), channel_id=1, source_target_pairs={{0,1},{1,2},{2,3},{3,4},{4,5},{5,6},{6,7},{7,8},{8,9},{9,10},{10,1... | collective-permute-start | bytes 688136 | tf_op jit(solution)/shard_map/ppermute | solution.py:30
  141.1 18.6 %collective-permute-start.16 = (bf16[288,256]{1,0:T(8,128)(2,1)S(1)}, bf16[288,256]{1,0:T(8,128)(2,1)S(1)}, u32[]{:S(2)}, u32[]{:S(2)}) collective-permute-start(bf16[288,256]{1,0:T(8,128)(2,1)S(1)} %reduce_sum.25), channel_id=1, source_target_pairs={{0,16},{1,17},{2,18},{3,19},{4,20},{5,21},{6,22},{7,23},{8,24},{9,... | collective-permute-start | bytes 442376 | tf_op jit(solution)/shard_map/ppermute | solution.py:176

commit v8 on v7

--- a/solution.py
+++ b/solution.py
@@ -173,16 +173,18 @@
     part = jnp.sum(parts.astype(jnp.float32), 0).astype(jnp.bfloat16)
     parts = lax.all_gather(part, AXIS, axis=0, axis_index_groups=FAR)
     part = jnp.sum(parts.astype(jnp.float32), 0).astype(jnp.bfloat16)
-    other_part = lax.ppermute(part, AXIS, ACROSS)
-    cut = part.shape[0] // 2
+    cut = part.shape[0] // 3 * 2
 
-    def near(piece):
-        return lax.all_gather(piece, AXIS, axis=0, axis_index_groups=NEAR)
+    def trade(piece):
+        both = lax.all_gather(piece, AXIS, axis=0, axis_index_groups=PAIRS)
+        return jnp.where(first_row, both[1], both[0])
 
-    head = near(part[:cut])
-    tail = near(jnp.concatenate([part[cut:], other_part], 0))
-    own_blocks = jnp.concatenate([head, tail[:, :cut]], 1).reshape(blocks.shape)
-    other_blocks = tail[:, cut:].reshape(blocks.shape)
+    part = jnp.concatenate([part, trade(part[:cut])], 0)
+    gathered = lax.all_gather(part, AXIS, axis=0, axis_index_groups=NEAR)
+    own_blocks, head = gathered[:, :-cut], gathered[:, -cut:]
+    tail = trade(own_blocks[:, cut:])
+    own_blocks = own_blocks.reshape(blocks.shape)
+    other_blocks = jnp.concatenate([head, tail], 1).reshape(blocks.shape)
     low = jnp.where(first_row, own_blocks, other_blocks)
     high = jnp.where(first_row, other_blocks, own_blocks)
     return finish(low, high, power, order)

time: 178 us -> 176 us (0.989)
  starting transfers between devices: 64.3 us -> 61.4 us
    ppermute x1 -> x0, starting transfers between devices: 2.91 us -> none  [body(): other_part = lax.ppermute(part, AXIS, ACROSS)]
    all_gather x2 -> x3, blocking collectives: 31.7 us -> 32 us  [the longest x1 20.3 us: body(): gathered = lax.all_gather(part, AXIS, axis=0, axis_index_groups=NEAR)]
  transfers between devices with their start and end apart: 17 -> 16, of which waited for: 7 -> 7; matrix products, arithmetic and copies ran while one was open for 0% -> 0% of each run, Pallas kernels for 0% -> 0%
where the time goes in v8:
time: 176 us; the launch traced here: 175 us
  blocking collectives  85.5 us (49%)
  starting transfers between devices  61.4 us (35%)
  waiting for transfers between devices  21.9 us (12%)
  Pallas kernels  2.22 us (1%)
    ppermute x7, starting transfers between devices, ring(): b = lax.ppermute(b, AXIS, shift(-1))  40.6 us
    all_gather x1, blocking collectives, body(): parts = lax.all_gather(part, AXIS, axis=0, axis_index_groups=FAR)  24.3 us
    ppermute x8, waiting for transfers between devices, ring(): a = lax.ppermute(a, AXIS, shift(1))  21.9 us
    all_gather x1, blocking collectives, body(): gathered = lax.all_gather(part, AXIS, axis=0, axis_index_groups=NEAR)  20.3 us
    all_to_all x1, blocking collectives, body(): lax.all_to_all(blocks.reshape(CUBE, -1, chunk), AXIS, 0, 0, axis_index_gr...  20.1 us
    ppermute x8, starting transfers between devices, ring(): a = lax.ppermute(a, AXIS, shift(1))  17.3 us
    all_gather x2, blocking collectives, trade(): both = lax.all_gather(piece, AXIS, axis=0, axis_index_groups=PAIRS)  11.6 us
    all_gather x1, blocking collectives, body(): lax.all_gather(terms.astype(jnp.bfloat16), AXIS, axis=0, axis_index_group...  9.16 us
  transfers between devices with their start and end apart: 16, of which 7 were waited for; matrix products, arithmetic and copies ran while one was open for 0% of the time, Pallas kernels for 0%

profile of v8, /device:TPU:6, one launch (start us, length us, event | category | flops | bytes accessed | tf_op | source)
XLA Modules:
  0.0 174.9 jit_solution(8731080775924650347)
XLA Ops:
  0.0 0.0 copy-start
  0.0 0.0 copy-start.1
  0.0 3.9 %collective-permute-start = (bf16[112,1024]{1,0:T(8,128)(2,1)}, bf16[112,1024]{1,0:T(8,128)(2,1)S(1)}, u32[]{:S(2)}, u32[]{:S(2)}) collective-permute-start(bf16[112,1024]{1,0:T(8,128)(2,1)} %param.3), channel_id=1, source_target_pairs={{0,1},{1,2},{2,3},{3,4},{4,5},{5,6},{6,7},{7,8},{8,9},{9,10},{10,1... | collective-permute-start | bytes 688136 | tf_op jit(solution)/shard_map/ppermute | solution.py:30
  4.0 9.5 %collective-permute-start.8 = (bf16[112,1024]{1,0:T(8,128)(2,1)}, bf16[112,1024]{1,0:T(8,128)(2,1)S(1)}, u32[]{:S(2)}, u32[]{:S(2)}) collective-permute-start(bf16[112,1024]{1,0:T(8,128)(2,1)} %param.3), channel_id=1, source_target_pairs={{0,15},{1,0},{2,1},{3,2},{4,3},{5,4},{6,5},{7,6},{8,7},{9,8},{10,9... | collective-permute-start | bytes 688136 | tf_op jit(solution)/shard_map/ppermute | solution.py:33
  13.5 0.0 copy-done
  13.5 3.5 %collective-permute-start.15 = (bf16[112,1792]{1,0:T(8,128)(2,1)S(1)}, bf16[112,1792]{1,0:T(8,128)(2,1)S(1)}, u32[]{:S(2)}, u32[]{:S(2)}) collective-permute-start(bf16[112,1792]{1,0:T(8,128)(2,1)S(1)} %constant_dynamic-slice_fusion.1), channel_id=1, source_target_pairs={{0,16},{1,17},{2,18},{3,19},{4,20},{5,21},{6,22},{7,23},{8,24},{9,... | collective-permute-start | bytes 1204232 | tf_op jit(solution)/shard_map/ppermute | solution.py:151
  17.4 0.5 broadcast_in_dim.51
  17.8 0.0 copy-done.1
  17.9 0.0 collective-permute-done
  17.9 1.9 %collective-permute-start.1 = (bf16[112,1024]{1,0:T(8,128)(2,1)S(1)}, bf16[112,1024]{1,0:T(8,128)(2,1)S(1)}, u32[]{:S(2)}, u32[]{:S(2)}) collective-permute-start(bf16[112,1024]{1,0:T(8,128)(2,1)S(1)} %collective-permute-done), channel_id=1, source_target_pairs={{0,1},{1,2},{2,3},{3,4},{4,5},{5,6},{6,7},{7,8},{8,9},{9,10},{10,1... | collective-permute-start | bytes 688136 | tf_op jit(solution)/shard_map/ppermute | solution.py:30
  19.8 0.0 collective-permute-done.8
  19.8 5.1 %collective-permute-start.9 = (bf16[112,1024]{1,0:T(8,128)(2,1)S(1)}, bf16[112,1024]{1,0:T(8,128)(2,1)S(1)}, u32[]{:S(2)}, u32[]{:S(2)}) collective-permute-start(bf16[112,1024]{1,0:T(8,128)(2,1)S(1)} %collective-permute-done.8), channel_id=1, source_target_pairs={{0,15},{1,0},{2,1},{3,2},{4,3},{5,4},{6,5},{7,6},{8,7},{9,8},{10,9... | collective-permute-start | bytes 688136 | tf_op jit(solution)/shard_map/ppermute | solution.py:33
  25.0 2.8 %collective-permute-done.1 = bf16[112,1024]{1,0:T(8,128)(2,1)S(1)} collective-permute-done((bf16[112,1024]{1,0:T(8,128)(2,1)S(1)}, bf16[112,1024]{1,0:T(8,128)(2,1)S(1)}, u32[]{:S(2)}, u32[]{:S(2)}) %collective-permute-start.1) | collective-permute-done | bytes 229408 | tf_op jit(solution)/shard_map/ppermute | solution.py:30
  27.8 1.9 %collective-permute-start.2 = (bf16[112,1024]{1,0:T(8,128)(2,1)S(1)}, bf16[112,1024]{1,0:T(8,128)(2,1)S(1)}, u32[]{:S(2)}, u32[]{:S(2)}) collective-permute-start(bf16[112,1024]{1,0:T(8,128)(2,1)S(1)} %collective-permute-done.1), channel_id=1, source_target_pairs={{0,1},{1,2},{2,3},{3,4},{4,5},{5,6},{6,7},{7,8},{8,9},{9,10},{10,1... | collective-permute-start | bytes 688136 | tf_op jit(solution)/shard_map/ppermute | solution.py:30
  29.7 0.0 collective-permute-done.9
  29.7 5.1 %collective-permute-start.10 = (bf16[112,1024]{1,0:T(8,128)(2,1)S(1)}, bf16[112,1024]{1,0:T(8,128)(2,1)S(1)}, u32[]{:S(2)}, u32[]{:S(2)}) collective-permute-start(bf16[112,1024]{1,0:T(8,128)(2,1)S(1)} %collective-permute-done.9), channel_id=1, source_target_pairs={{0,15},{1,0},{2,1},{3,2},{4,3},{5,4},{6,5},{7,6},{8,7},{9,8},{10,9... | collective-permute-start | bytes 688136 | tf_op jit(solution)/shard_map/ppermute | solution.py:33
  34.9 2.0 %collective-permute-done.2 = bf16[112,1024]{1,0:T(8,128)(2,1)S(1)} collective-permute-done((bf16[112,1024]{1,0:T(8,128)(2,1)S(1)}, bf16[112,1024]{1,0:T(8,128)(2,1)S(1)}, u32[]{:S(2)}, u32[]{:S(2)}) %collective-permute-start.2) | collective-permute-done | bytes 229408 | tf_op jit(solution)/shard_map/ppermute | solution.py:30
  36.9 1.9 %collective-permute-start.3 = (bf16[112,1024]{1,0:T(8,128)(2,1)S(1)}, bf16[112,1024]{1,0:T(8,128)(2,1)S(1)}, u32[]{:S(2)}, u32[]{:S(2)}) collective-permute-start(bf16[112,1024]{1,0:T(8,128)(2,1)S(1)} %collective-permute-done.2), channel_id=1, source_target_pairs={{0,1},{1,2},{2,3},{3,4},{4,5},{5,6},{6,7},{7,8},{8,9},{9,10},{10,1... | collective-permute-start | bytes 688136 | tf_op jit(solution)/shard_map/ppermute | solution.py:30
  38.8 0.0 collective-permute-done.10
  38.8 5.1 %collective-permute-start.11 = (bf16[112,1024]{1,0:T(8,128)(2,1)S(1)}, bf16[112,1024]{1,0:T(8,128)(2,1)S(1)}, u32[]{:S(2)}, u32[]{:S(2)}) collective-permute-start(bf16[112,1024]{1,0:T(8,128)(2,1)S(1)} %collective-permute-done.10), channel_id=1, source_target_pairs={{0,15},{1,0},{2,1},{3,2},{4,3},{5,4},{6,5},{7,6},{8,7},{9,8},{10,9... | collective-permute-start | bytes 688136 | tf_op jit(solution)/shard_map/ppermute | solution.py:33
  44.0 2.0 %collective-permute-done.3 = bf16[112,1024]{1,0:T(8,128)(2,1)S(1)} collective-permute-done((bf16[112,1024]{1,0:T(8,128)(2,1)S(1)}, bf16[112,1024]{1,0:T(8,128)(2,1)S(1)}, u32[]{:S(2)}, u32[]{:S(2)}) %collective-permute-start.3) | collective-permute-done | bytes 229408 | tf_op jit(solution)/shard_map/ppermute | solution.py:30
  46.0 1.9 %collective-permute-start.4 = (bf16[112,1024]{1,0:T(8,128)(2,1)S(1)}, bf16[112,1024]{1,0:T(8,128)(2,1)S(1)}, u32[]{:S(2)}, u32[]{:S(2)}) collective-permute-start(bf16[112,1024]{1,0:T(8,128)(2,1)S(1)} %collective-permute-done.3), channel_id=1, source_target_pairs={{0,1},{1,2},{2,3},{3,4},{4,5},{5,6},{6,7},{7,8},{8,9},{9,10},{10,1... | collective-permute-start | bytes 688136 | tf_op jit(solution)/shard_map/ppermute | solution.py:30
  47.9 0.0 collective-permute-done.11
  47.9 5.1 %collective-permute-start.12 = (bf16[112,1024]{1,0:T(8,128)(2,1)S(1)}, bf16[112,1024]{1,0:T(8,128)(2,1)S(1)}, u32[]{:S(2)}, u32[]{:S(2)}) collective-permute-start(bf16[112,1024]{1,0:T(8,128)(2,1)S(1)} %collective-permute-done.11), channel_id=1, source_target_pairs={{0,15},{1,0},{2,1},{3,2},{4,3},{5,4},{6,5},{7,6},{8,7},{9,8},{10,9... | collective-permute-start | bytes 688136 | tf_op jit(solution)/shard_map/ppermute | solution.py:33
  53.1 2.0 %collective-permute-done.4 = bf16[112,1024]{1,0:T(8,128)(2,1)S(1)} collective-permute-done((bf16[112,1024]{1,0:T(8,128)(2,1)S(1)}, bf16[112,1024]{1,0:T(8,128)(2,1)S(1)}, u32[]{:S(2)}, u32[]{:S(2)}) %collective-permute-start.4) | collective-permute-done | bytes 229408 | tf_op jit(solution)/shard_map/ppermute | solution.py:30
  55.1 1.9 %collective-permute-start.5 = (bf16[112,1024]{1,0:T(8,128)(2,1)S(1)}, bf16[112,1024]{1,0:T(8,128)(2,1)S(1)}, u32[]{:S(2)}, u32[]{:S(2)}) collective-permute-start(bf16[112,1024]{1,0:T(8,128)(2,1)S(1)} %collective-permute-done.4), channel_id=1, source_target_pairs={{0,1},{1,2},{2,3},{3,4},{4,5},{5,6},{6,7},{7,8},{8,9},{9,10},{10,1... | collective-permute-start | bytes 688136 | tf_op jit(solution)/shard_map/ppermute | solution.py:30
  57.0 0.0 collective-permute-done.12
  57.1 5.1 %collective-permute-start.13 = (bf16[112,1024]{1,0:T(8,128)(2,1)S(1)}, bf16[112,1024]{1,0:T(8,128)(2,1)S(1)}, u32[]{:S(2)}, u32[]{:S(2)}) collective-permute-start(bf16[112,1024]{1,0:T(8,128)(2,1)S(1)} %collective-permute-done.12), channel_id=1, source_target_pairs={{0,15},{1,0},{2,1},{3,2},{4,3},{5,4},{6,5},{7,6},{8,7},{9,8},{10,9... | collective-permute-start | bytes 688136 | tf_op jit(solution)/shard_map/ppermute | solution.py:33
  62.2 2.5 %collective-permute-done.5 = bf16[112,1024]{1,0:T(8,128)(2,1)S(1)} collective-permute-done((bf16[112,1024]{1,0:T(8,128)(2,1)S(1)}, bf16[112,1024]{1,0:T(8,128)(2,1)S(1)}, u32[]{:S(2)}, u32[]{:S(2)}) %collective-permute-start.5) | collective-permute-done | bytes 229408 | tf_op jit(solution)/shard_map/ppermute | solution.py:30
  64.7 1.9 %collective-permute-start.6 = (bf16[112,1024]{1,0:T(8,128)(2,1)S(1)}, bf16[112,1024]{1,0:T(8,128)(2,1)S(1)}, u32[]{:S(2)}, u32[]{:S(2)}) collective-permute-start(bf16[112,1024]{1,0:T(8,128)(2,1)S(1)} %collective-permute-done.5), channel_id=1, source_target_pairs={{0,1},{1,2},{2,3},{3,4},{4,5},{5,6},{6,7},{7,8},{8,9},{9,10},{10,1... | collective-permute-start | bytes 688136 | tf_op jit(solution)/shard_map/ppermute | solution.py:30
  66.7 0.0 collective-permute-done.13
  66.7 5.4 %collective-permute-start.14 = (bf16[112,1024]{1,0:T(8,128)(2,1)S(1)}, bf16[112,1024]{1,0:T(8,128)(2,1)S(1)}, u32[]{:S(2)}, u32[]{:S(2)}) collective-permute-start(bf16[112,1024]{1,0:T(8,128)(2,1)S(1)} %collective-permute-done.13), channel_id=1, source_target_pairs={{0,15},{1,0},{2,1},{3,2},{4,3},{5,4},{6,5},{7,6},{8,7},{9,8},{10,9... | collective-permute-start | bytes 688136 | tf_op jit(solution)/shard_map/ppermute | solution.py:33
  72.1 3.4 %collective-permute-done.6 = bf16[112,1024]{1,0:T(8,128)(2,1)S(1)} collective-permute-done((bf16[112,1024]{1,0:T(8,128)(2,1)S(1)}, bf16[112,1024]{1,0:T(8,128)(2,1)S(1)}, u32[]{:S(2)}, u32[]{:S(2)}) %collective-permute-start.6) | collective-permute-done | bytes 229408 | tf_op jit(solution)/shard_map/ppermute | solution.py:30
  75.5 1.9 %collective-permute-start.7 = (bf16[112,1024]{1,0:T(8,128)(2,1)S(1)}, bf16[112,1024]{1,0:T(8,128)(2,1)S(1)}, u32[]{:S(2)}, u32[]{:S(2)}) collective-permute-start(bf16[112,1024]{1,0:T(8,128)(2,1)S(1)} %collective-permute-done.6), channel_id=1, source_target_pairs={{0,1},{1,2},{2,3},{3,4},{4,5},{5,6},{6,7},{7,8},{8,9},{9,10},{10,1... | collective-permute-start | bytes 688136 | tf_op jit(solution)/shard_map/ppermute | solution.py:30
  77.5 7.2 %collective-permute-done.7 = bf16[112,1024]{1,0:T(8,128)(2,1)S(1)} collective-permute-done((bf16[112,1024]{1,0:T(8,128)(2,1)S(1)}, bf16[112,1024]{1,0:T(8,128)(2,1)S(1)}, u32[]{:S(2)}, u32[]{:S(2)}) %collective-permute-start.7) | collective-permute-done | bytes 229408 | tf_op jit(solution)/shard_map/ppermute | solution.py:30
  84.8 0.0 collective-permute-done.14
  84.9 0.0 collective-permute-done.15
  84.9 0.7 fusion.7
  85.6 0.8 convert_bitcast_fusion.1
  86.4 9.2 %all_gather.28 = bf16[2,224,1024]{2,1,0:T(8,128)(2,1)S(1)} all-gather(bf16[1,224,1024]{2,1,0:T(8,128)(2,1)S(1)} %pad_maximum_fusion.1), channel_id=1, replica_groups={{0,16},{1,17},{2,18},{3,19},{4,20},{5,21},{6,22},{7,23},{8,24},{9,25},{..., dimensions={0}, use_global_device_ids=true | all-gather | bytes 1376256 | tf_op jit(solution)/shard_map/all_gather | solution.py:165
  95.6 0.2 fusion.plane_ref
  95.8 0.4 unique_blocks.1
  96.2 20.1 %all_to_all.5 = bf16[4,288,256]{2,1,0:T(8,128)(2,1)S(1)} all-to-all(bf16[4,288,256]{2,1,0:T(8,128)(2,1)S(1)} %bitcast.53), channel_id=1, replica_groups={{0,1,2,3},{4,5,6,7},{8,9,10,11},{12,13,14,15},{16,17,18,19},{20,21,22,2..., dimensions={0} | all-to-all | bytes 1179648 | tf_op jit(solution)/shard_map/all_to_all | solution.py:170
  116.3 0.1 reduce_sum.24
  116.4 24.3 %all-gather = bf16[1152,256]{1,0:T(8,128)(2,1)S(1)} all-gather(bf16[288,256]{1,0:T(8,128)(2,1)S(1)} %reduce_sum.24), channel_id=2, replica_groups={{0,4,8,12},{1,5,9,13},{2,6,10,14},{3,7,11,15},{16,20,24,28},{17,21,25,2..., dimensions={0}, use_global_device_ids=true | all-gather | bytes 737280 | tf_op jit(solution)/shard_map/all_gather | solution.py:174
  140.7 0.1 reduce_sum.25
  140.8 5.3 %all-gather.1 = bf16[384,256]{1,0:T(8,128)(2,1)S(1)} all-gather(bf16[192,256]{1,0:T(8,128)(2,1)S(1)} %slice.47), channel_id=3, replica_groups={{0,16},{1,17},{2,18},{3,19},{4,20},{5,21},{6,22},{7,23},{8,24},{9,25},{..., dimensions={0}, use_global_device_ids=true | all-gather | bytes 294912 | tf_op jit(solution)/shard_map/all_gather | solution.py:179
  146.1 20.3 %all-gather.2 = bf16[1920,256]{1,0:T(8,128)(2,1)S(1)} all-gather(bf16[480,256]{1,0:T(8,128)(2,1)S(1)} %pad_maximum_fusion.2), channel_id=4, replica_groups={{0,1,2,3},{4,5,6,7},{8,9,10,11},{12,13,14,15},{16,17,18,19},{20,21,22,2..., dimensions={0}, use_global_device_ids=true | all-gather | bytes 1228800 | tf_op jit(solution)/shard_map/all_gather | solution.py:183
  166.5 6.3 %all-gather.3 = bf16[8,96,256]{2,1,0:T(8,128)(2,1)S(1)} all-gather(bf16[4,96,256]{2,1,0:T(8,128)(2,1)S(1)} %slice.52), channel_id=5, replica_groups={{0,16},{1,17},{2,18},{3,19},{4,20},{5,21},{6,22},{7,23},{8,24},{9,25},{..., dimensions={0}, use_global_device_ids=true | all-gather | bytes 589824 | tf_op jit(solution)/shard_map/all_gather | solution.py:179
  172.9 0.2 broadcast_select_fusion
  173.1 1.8 %finish.1 = bf16[112,1024]{1,0:T(8,128)(2,1)} custom-call(bf16[1152,256]{1,0:T(8,128)(2,1)S(1)} %bitcast.52, bf16[1152,256]{1,0:T(8,128)(2,1)S(1)} %bitcast.51, bf16[112,1024]{1,0:T(8,128)(2,1)S(1)} %constant_dynamic-slice_fusion.power_ref), custom_call_target="tpu_custom_call" | custom-call | tf_op jit(solution)/shard_map/finish/pallas_call | solution.py:130
  (25 shorter events, 0.6 us)
Async XLA Ops:
  0.0 13.5 %copy-start = (bf16[112,3584]{1,0:T(8,128)(2,1)S(1)}, bf16[112,3584]{1,0:T(8,128)(2,1)}, u32[]{:S(2)}) copy-start(bf16[112,3584]{1,0:T(8,128)(2,1)} %param.2) | copy-start | bytes 2408452
  0.0 17.8 %copy-start.1 = (bf16[112,1024]{1,0:T(8,128)(2,1)S(1)}, bf16[112,1024]{1,0:T(8,128)(2,1)}, u32[]{:S(2)}) copy-start(bf16[112,1024]{1,0:T(8,128)(2,1)} %param.3) | copy-start | bytes 688132
  0.0 17.9 %collective-permute-start = (bf16[112,1024]{1,0:T(8,128)(2,1)}, bf16[112,1024]{1,0:T(8,128)(2,1)S(1)}, u32[]{:S(2)}, u32[]{:S(2)}) collective-permute-start(bf16[112,1024]{1,0:T(8,128)(2,1)} %param.3), channel_id=1, source_target_pairs={{0,1},{1,2},{2,3},{3,4},{4,5},{5,6},{6,7},{7,8},{8,9},{9,10},{10,1... | collective-permute-start | bytes 688136 | tf_op jit(solution)/shard_map/ppermute | solution.py:30
  4.0 15.9 %collective-permute-start.8 = (bf16[112,1024]{1,0:T(8,128)(2,1)}, bf16[112,1024]{1,0:T(8,128)(2,1)S(1)}, u32[]{:S(2)}, u32[]{:S(2)}) collective-permute-start(bf16[112,1024]{1,0:T(8,128)(2,1)} %param.3), channel_id=1, source_target_pairs={{0,15},{1,0},{2,1},{3,2},{4,3},{5,4},{6,5},{7,6},{8,7},{9,8},{10,9... | collective-permute-start | bytes 688136 | tf_op jit(solution)/shard_map/ppermute | solution.py:33
  13.5 71.3 %collective-permute-start.15 = (bf16[112,1792]{1,0:T(8,128)(2,1)S(1)}, bf16[112,1792]{1,0:T(8,128)(2,1)S(1)}, u32[]{:S(2)}, u32[]{:S(2)}) collective-permute-start(bf16[112,1792]{1,0:T(8,128)(2,1)S(1)} %constant_dynamic-slice_fusion.1), channel_id=1, source_target_pairs={{0,16},{1,17},{2,18},{3,19},{4,20},{5,21},{6,22},{7,23},{8,24},{9,... | collective-permute-start | bytes 1204232 | tf_op jit(solution)/shard_map/ppermute | solution.py:151
  17.9 9.9 %collective-permute-start.1 = (bf16[112,1024]{1,0:T(8,128)(2,1)S(1)}, bf16[112,1024]{1,0:T(8,128)(2,1)S(1)}, u32[]{:S(2)}, u32[]{:S(2)}) collective-permute-start(bf16[112,1024]{1,0:T(8,128)(2,1)S(1)} %collective-permute-done), channel_id=1, source_target_pairs={{0,1},{1,2},{2,3},{3,4},{4,5},{5,6},{6,7},{7,8},{8,9},{9,10},{10,1... | collective-permute-start | bytes 688136 | tf_op jit(solution)/shard_map/ppermute | solution.py:30
  19.8 9.9 %collective-permute-start.9 = (bf16[112,1024]{1,0:T(8,128)(2,1)S(1)}, bf16[112,1024]{1,0:T(8,128)(2,1)S(1)}, u32[]{:S(2)}, u32[]{:S(2)}) collective-permute-start(bf16[112,1024]{1,0:T(8,128)(2,1)S(1)} %collective-permute-done.8), channel_id=1, source_target_pairs={{0,15},{1,0},{2,1},{3,2},{4,3},{5,4},{6,5},{7,6},{8,7},{9,8},{10,9... | collective-permute-start | bytes 688136 | tf_op jit(solution)/shard_map/ppermute | solution.py:33
  27.8 9.1 %collective-permute-start.2 = (bf16[112,1024]{1,0:T(8,128)(2,1)S(1)}, bf16[112,1024]{1,0:T(8,128)(2,1)S(1)}, u32[]{:S(2)}, u32[]{:S(2)}) collective-permute-start(bf16[112,1024]{1,0:T(8,128)(2,1)S(1)} %collective-permute-done.1), channel_id=1, source_target_pairs={{0,1},{1,2},{2,3},{3,4},{4,5},{5,6},{6,7},{7,8},{8,9},{9,10},{10,1... | collective-permute-start | bytes 688136 | tf_op jit(solution)/shard_map/ppermute | solution.py:30
  29.7 9.1 %collective-permute-start.10 = (bf16[112,1024]{1,0:T(8,128)(2,1)S(1)}, bf16[112,1024]{1,0:T(8,128)(2,1)S(1)}, u32[]{:S(2)}, u32[]{:S(2)}) collective-permute-start(bf16[112,1024]{1,0:T(8,128)(2,1)S(1)} %collective-permute-done.9), channel_id=1, source_target_pairs={{0,15},{1,0},{2,1},{3,2},{4,3},{5,4},{6,5},{7,6},{8,7},{9,8},{10,9... | collective-permute-start | bytes 688136 | tf_op jit(solution)/shard_map/ppermute | solution.py:33
  36.9 9.1 %collective-permute-start.3 = (bf16[112,1024]{1,0:T(8,128)(2,1)S(1)}, bf16[112,1024]{1,0:T(8,128)(2,1)S(1)}, u32[]{:S(2)}, u32[]{:S(2)}) collective-permute-start(bf16[112,1024]{1,0:T(8,128)(2,1)S(1)} %collective-permute-done.2), channel_id=1, source_target_pairs={{0,1},{1,2},{2,3},{3,4},{4,5},{5,6},{6,7},{7,8},{8,9},{9,10},{10,1... | collective-permute-start | bytes 688136 | tf_op jit(solution)/shard_map/ppermute | solution.py:30
  38.8 9.1 %collective-permute-start.11 = (bf16[112,1024]{1,0:T(8,128)(2,1)S(1)}, bf16[112,1024]{1,0:T(8,128)(2,1)S(1)}, u32[]{:S(2)}, u32[]{:S(2)}) collective-permute-start(bf16[112,1024]{1,0:T(8,128)(2,1)S(1)} %collective-permute-done.10), channel_id=1, source_target_pairs={{0,15},{1,0},{2,1},{3,2},{4,3},{5,4},{6,5},{7,6},{8,7},{9,8},{10,9... | collective-permute-start | bytes 688136 | tf_op jit(solution)/shard_map/ppermute | solution.py:33
  46.0 9.1 %collective-permute-start.4 = (bf16[112,1024]{1,0:T(8,128)(2,1)S(1)}, bf16[112,1024]{1,0:T(8,128)(2,1)S(1)}, u32[]{:S(2)}, u32[]{:S(2)}) collective-permute-start(bf16[112,1024]{1,0:T(8,128)(2,1)S(1)} %collective-permute-done.3), channel_id=1, source_target_pairs={{0,1},{1,2},{2,3},{3,4},{4,5},{5,6},{6,7},{7,8},{8,9},{9,10},{10,1... | collective-permute-start | bytes 688136 | tf_op jit(solution)/shard_map/ppermute | solution.py:30
  47.9 9.1 %collective-permute-start.12 = (bf16[112,1024]{1,0:T(8,128)(2,1)S(1)}, bf16[112,1024]{1,0:T(8,128)(2,1)S(1)}, u32[]{:S(2)}, u32[]{:S(2)}) collective-permute-start(bf16[112,1024]{1,0:T(8,128)(2,1)S(1)} %collective-permute-done.11), channel_id=1, source_target_pairs={{0,15},{1,0},{2,1},{3,2},{4,3},{5,4},{6,5},{7,6},{8,7},{9,8},{10,9... | collective-permute-start | bytes 688136 | tf_op jit(solution)/shard_map/ppermute | solution.py:33
  55.1 9.6 %collective-permute-start.5 = (bf16[112,1024]{1,0:T(8,128)(2,1)S(1)}, bf16[112,1024]{1,0:T(8,128)(2,1)S(1)}, u32[]{:S(2)}, u32[]{:S(2)}) collective-permute-start(bf16[112,1024]{1,0:T(8,128)(2,1)S(1)} %collective-permute-done.4), channel_id=1, source_target_pairs={{0,1},{1,2},{2,3},{3,4},{4,5},{5,6},{6,7},{7,8},{8,9},{9,10},{10,1... | collective-permute-start | bytes 688136 | tf_op jit(solution)/shard_map/ppermute | solution.py:30
  57.1 9.6 %collective-permute-start.13 = (bf16[112,1024]{1,0:T(8,128)(2,1)S(1)}, bf16[112,1024]{1,0:T(8,128)(2,1)S(1)}, u32[]{:S(2)}, u32[]{:S(2)}) collective-permute-start(bf16[112,1024]{1,0:T(8,128)(2,1)S(1)} %collective-permute-done.12), channel_id=1, source_target_pairs={{0,15},{1,0},{2,1},{3,2},{4,3},{5,4},{6,5},{7,6},{8,7},{9,8},{10,9... | collective-permute-start | bytes 688136 | tf_op jit(solution)/shard_map/ppermute | solution.py:33
  64.7 10.8 %collective-permute-start.6 = (bf16[112,1024]{1,0:T(8,128)(2,1)S(1)}, bf16[112,1024]{1,0:T(8,128)(2,1)S(1)}, u32[]{:S(2)}, u32[]{:S(2)}) collective-permute-start(bf16[112,1024]{1,0:T(8,128)(2,1)S(1)} %collective-permute-done.5), channel_id=1, source_target_pairs={{0,1},{1,2},{2,3},{3,4},{4,5},{5,6},{6,7},{7,8},{8,9},{9,10},{10,1... | collective-permute-start | bytes 688136 | tf_op jit(solution)/shard_map/ppermute | solution.py:30
  66.7 18.2 %collective-permute-start.14 = (bf16[112,1024]{1,0:T(8,128)(2,1)S(1)}, bf16[112,1024]{1,0:T(8,128)(2,1)S(1)}, u32[]{:S(2)}, u32[]{:S(2)}) collective-permute-start(bf16[112,1024]{1,0:T(8,128)(2,1)S(1)} %collective-permute-done.13), channel_id=1, source_target_pairs={{0,15},{1,0},{2,1},{3,2},{4,3},{5,4},{6,5},{7,6},{8,7},{9,8},{10,9... | collective-permute-start | bytes 688136 | tf_op jit(solution)/shard_map/ppermute | solution.py:33
  75.5 9.1 %collective-permute-start.7 = (bf16[112,1024]{1,0:T(8,128)(2,1)S(1)}, bf16[112,1024]{1,0:T(8,128)(2,1)S(1)}, u32[]{:S(2)}, u32[]{:S(2)}) collective-permute-start(bf16[112,1024]{1,0:T(8,128)(2,1)S(1)} %collective-permute-done.6), channel_id=1, source_target_pairs={{0,1},{1,2},{2,3},{3,4},{4,5},{5,6},{6,7},{7,8},{8,9},{9,10},{10,1... | collective-permute-start | bytes 688136 | tf_op jit(solution)/shard_map/ppermute | solution.py:30

commit v9 on v8

--- a/solution.py
+++ b/solution.py
@@ -153,15 +153,21 @@
     up, down = ring(basis)
     full = jnp.zeros((Z, rows, columns), basis.dtype)
     full = place(full, basis, z)
-    for step, part in enumerate(up):
+    for step, part in enumerate(up[:-1]):
         full = place(full, part, z - step - 1 + Z)
     for step, part in enumerate(down):
         full = place(full, part, z + step + 1)
     full = full.reshape(span, columns)
 
-    near = jnp.dot(own_columns, full, preferred_element_type=jnp.float32)
-    far = jnp.dot(far_columns, full, preferred_element_type=jnp.float32)
+    def product(left):
+        last = lax.dynamic_slice_in_dim(left, (z - len(up) + Z) % Z * rows, rows, 1)
+        return jnp.dot(left, full, preferred_element_type=jnp.float32), last
+
+    near, near_last = product(own_columns)
+    far, far_last = product(far_columns)
     terms = jnp.concatenate([jnp.where(first_row, near, far), jnp.where(first_row, far, near)], 0)
+    lasts = jnp.concatenate([jnp.where(first_row, near_last, far_last), jnp.where(first_row, far_last, near_last)], 0)
+    terms = terms + jnp.dot(lasts, up[-1], preferred_element_type=jnp.float32)
     sent = lax.all_gather(terms.astype(jnp.bfloat16), AXIS, axis=0, axis_index_groups=PAIRS)
     plane = (terms + jnp.where(first_row, sent[1], sent[0]).astype(jnp.float32)).astype(jnp.bfloat16)
     power = lax.dynamic_slice_in_dim(plane, y * rows, rows, 0)

time: 176 us -> 174 us (0.989)
  waiting for transfers between devices: 21.9 us -> 20.1 us
    ppermute x8, waiting for transfers between devices: 21.9 us -> 19 us  [ring(): a = lax.ppermute(a, AXIS, shift(1))]
  transfers between devices with their start and end apart: 16 -> 16, of which waited for: 7 -> 8; matrix products, arithmetic and copies ran while one was open for 0% -> 2% of each run, Pallas kernels for 0% -> 0%
where the time goes in v9:
time: 174 us
  blocking collectives  84.7 us (49%)
  starting transfers between devices  61.4 us (35%)
  waiting for transfers between devices  20.1 us (12%)
  Pallas kernels  2.22 us (1%)
  local copies, waits for them, and re-layouts  1.91 us (1%)
    ppermute x7, starting transfers between devices, ring(): b = lax.ppermute(b, AXIS, shift(-1))  40.6 us
    all_gather x1, blocking collectives, body(): parts = lax.all_gather(part, AXIS, axis=0, axis_index_groups=FAR)  25.8 us
    all_gather x1, blocking collectives, body(): gathered = lax.all_gather(part, AXIS, axis=0, axis_index_groups=NEAR)  19.1 us
    ppermute x8, waiting for transfers between devices, ring(): a = lax.ppermute(a, AXIS, shift(1))  19 us
    all_to_all x1, blocking collectives, body(): lax.all_to_all(blocks.reshape(CUBE, -1, chunk), AXIS, 0, 0, axis_index_gr...  19 us
    ppermute x8, starting transfers between devices, ring(): a = lax.ppermute(a, AXIS, shift(1))  17.3 us
    all_gather x2, blocking collectives, trade(): both = lax.all_gather(piece, AXIS, axis=0, axis_index_groups=PAIRS)  11.6 us
    all_gather x1, blocking collectives, body(): lax.all_gather(terms.astype(jnp.bfloat16), AXIS, axis=0, axis_index_group...  9.16 us
  transfers between devices with their start and end apart: 16, of which 8 were waited for; matrix products, arithmetic and copies ran while one was open for 2% of the time, Pallas kernels for 0%

profile of v9, /device:TPU:6, one launch (start us, length us, event | category | flops | bytes accessed | tf_op | source)
XLA Modules:
  0.0 173.6 jit_solution(9807119937760144260)
XLA Ops:
  0.0 0.0 copy-start.1
  0.0 0.0 copy-start
  0.0 3.9 %collective-permute-start = (bf16[112,1024]{1,0:T(8,128)(2,1)}, bf16[112,1024]{1,0:T(8,128)(2,1)S(1)}, u32[]{:S(2)}, u32[]{:S(2)}) collective-permute-start(bf16[112,1024]{1,0:T(8,128)(2,1)} %param.3), channel_id=1, source_target_pairs={{0,1},{1,2},{2,3},{3,4},{4,5},{5,6},{6,7},{7,8},{8,9},{9,10},{10,1... | collective-permute-start | bytes 688136 | tf_op jit(solution)/shard_map/ppermute | solution.py:30
  4.0 9.5 %collective-permute-start.7 = (bf16[112,1024]{1,0:T(8,128)(2,1)}, bf16[112,1024]{1,0:T(8,128)(2,1)S(1)}, u32[]{:S(2)}, u32[]{:S(2)}) collective-permute-start(bf16[112,1024]{1,0:T(8,128)(2,1)} %param.3), channel_id=1, source_target_pairs={{0,15},{1,0},{2,1},{3,2},{4,3},{5,4},{6,5},{7,6},{8,7},{9,8},{10,9... | collective-permute-start | bytes 688136 | tf_op jit(solution)/shard_map/ppermute | solution.py:33
  13.5 1.0 constant_dynamic-slice_fusion.1
  14.5 3.5 %collective-permute-start.14 = (bf16[112,1792]{1,0:T(8,128)(2,1)S(1)}, bf16[112,1792]{1,0:T(8,128)(2,1)S(1)}, u32[]{:S(2)}, u32[]{:S(2)}) collective-permute-start(bf16[112,1792]{1,0:T(8,128)(2,1)S(1)} %constant_dynamic-slice_fusion.1), channel_id=1, source_target_pairs={{0,16},{1,17},{2,18},{3,19},{4,20},{5,21},{6,22},{7,23},{8,24},{9,... | collective-permute-start | bytes 1204232 | tf_op jit(solution)/shard_map/ppermute | solution.py:151
  18.4 0.5 broadcast_in_dim.48
  18.8 0.0 copy-done.1
  18.9 0.0 collective-permute-done
  18.9 1.9 %collective-permute-start.1 = (bf16[112,1024]{1,0:T(8,128)(2,1)S(1)}, bf16[112,1024]{1,0:T(8,128)(2,1)S(1)}, u32[]{:S(2)}, u32[]{:S(2)}) collective-permute-start(bf16[112,1024]{1,0:T(8,128)(2,1)S(1)} %collective-permute-done), channel_id=1, source_target_pairs={{0,1},{1,2},{2,3},{3,4},{4,5},{5,6},{6,7},{7,8},{8,9},{9,10},{10,1... | collective-permute-start | bytes 688136 | tf_op jit(solution)/shard_map/ppermute | solution.py:30
  20.8 0.0 collective-permute-done.7
  20.8 5.1 %collective-permute-start.8 = (bf16[112,1024]{1,0:T(8,128)(2,1)S(1)}, bf16[112,1024]{1,0:T(8,128)(2,1)S(1)}, u32[]{:S(2)}, u32[]{:S(2)}) collective-permute-start(bf16[112,1024]{1,0:T(8,128)(2,1)S(1)} %collective-permute-done.7), channel_id=1, source_target_pairs={{0,15},{1,0},{2,1},{3,2},{4,3},{5,4},{6,5},{7,6},{8,7},{9,8},{10,9... | collective-permute-start | bytes 688136 | tf_op jit(solution)/shard_map/ppermute | solution.py:33
  26.0 1.2 collective-permute-done.14
  27.2 0.0 copy-done
  27.2 0.1 broadcast_select_fusion.5
  27.3 1.5 collective-permute-done.1
  28.8 1.9 %collective-permute-start.2 = (bf16[112,1024]{1,0:T(8,128)(2,1)S(1)}, bf16[112,1024]{1,0:T(8,128)(2,1)S(1)}, u32[]{:S(2)}, u32[]{:S(2)}) collective-permute-start(bf16[112,1024]{1,0:T(8,128)(2,1)S(1)} %collective-permute-done.1), channel_id=1, source_target_pairs={{0,1},{1,2},{2,3},{3,4},{4,5},{5,6},{6,7},{7,8},{8,9},{9,10},{10,1... | collective-permute-start | bytes 688136 | tf_op jit(solution)/shard_map/ppermute | solution.py:30
  30.7 0.0 collective-permute-done.8
  30.7 5.1 %collective-permute-start.9 = (bf16[112,1024]{1,0:T(8,128)(2,1)S(1)}, bf16[112,1024]{1,0:T(8,128)(2,1)S(1)}, u32[]{:S(2)}, u32[]{:S(2)}) collective-permute-start(bf16[112,1024]{1,0:T(8,128)(2,1)S(1)} %collective-permute-done.8), channel_id=1, source_target_pairs={{0,15},{1,0},{2,1},{3,2},{4,3},{5,4},{6,5},{7,6},{8,7},{9,8},{10,9... | collective-permute-start | bytes 688136 | tf_op jit(solution)/shard_map/ppermute | solution.py:33
  35.9 2.0 %collective-permute-done.2 = bf16[112,1024]{1,0:T(8,128)(2,1)S(1)} collective-permute-done((bf16[112,1024]{1,0:T(8,128)(2,1)S(1)}, bf16[112,1024]{1,0:T(8,128)(2,1)S(1)}, u32[]{:S(2)}, u32[]{:S(2)}) %collective-permute-start.2) | collective-permute-done | bytes 229408 | tf_op jit(solution)/shard_map/ppermute | solution.py:30
  37.9 1.9 %collective-permute-start.3 = (bf16[112,1024]{1,0:T(8,128)(2,1)S(1)}, bf16[112,1024]{1,0:T(8,128)(2,1)S(1)}, u32[]{:S(2)}, u32[]{:S(2)}) collective-permute-start(bf16[112,1024]{1,0:T(8,128)(2,1)S(1)} %collective-permute-done.2), channel_id=1, source_target_pairs={{0,1},{1,2},{2,3},{3,4},{4,5},{5,6},{6,7},{7,8},{8,9},{9,10},{10,1... | collective-permute-start | bytes 688136 | tf_op jit(solution)/shard_map/ppermute | solution.py:30
  39.8 0.0 collective-permute-done.9
  39.8 5.1 %collective-permute-start.10 = (bf16[112,1024]{1,0:T(8,128)(2,1)S(1)}, bf16[112,1024]{1,0:T(8,128)(2,1)S(1)}, u32[]{:S(2)}, u32[]{:S(2)}) collective-permute-start(bf16[112,1024]{1,0:T(8,128)(2,1)S(1)} %collective-permute-done.9), channel_id=1, source_target_pairs={{0,15},{1,0},{2,1},{3,2},{4,3},{5,4},{6,5},{7,6},{8,7},{9,8},{10,9... | collective-permute-start | bytes 688136 | tf_op jit(solution)/shard_map/ppermute | solution.py:33
  45.0 2.0 %collective-permute-done.3 = bf16[112,1024]{1,0:T(8,128)(2,1)S(1)} collective-permute-done((bf16[112,1024]{1,0:T(8,128)(2,1)S(1)}, bf16[112,1024]{1,0:T(8,128)(2,1)S(1)}, u32[]{:S(2)}, u32[]{:S(2)}) %collective-permute-start.3) | collective-permute-done | bytes 229408 | tf_op jit(solution)/shard_map/ppermute | solution.py:30
  47.0 1.9 %collective-permute-start.4 = (bf16[112,1024]{1,0:T(8,128)(2,1)S(1)}, bf16[112,1024]{1,0:T(8,128)(2,1)S(1)}, u32[]{:S(2)}, u32[]{:S(2)}) collective-permute-start(bf16[112,1024]{1,0:T(8,128)(2,1)S(1)} %collective-permute-done.3), channel_id=1, source_target_pairs={{0,1},{1,2},{2,3},{3,4},{4,5},{5,6},{6,7},{7,8},{8,9},{9,10},{10,1... | collective-permute-start | bytes 688136 | tf_op jit(solution)/shard_map/ppermute | solution.py:30
  48.9 0.0 collective-permute-done.10
  48.9 5.1 %collective-permute-start.11 = (bf16[112,1024]{1,0:T(8,128)(2,1)S(1)}, bf16[112,1024]{1,0:T(8,128)(2,1)S(1)}, u32[]{:S(2)}, u32[]{:S(2)}) collective-permute-start(bf16[112,1024]{1,0:T(8,128)(2,1)S(1)} %collective-permute-done.10), channel_id=1, source_target_pairs={{0,15},{1,0},{2,1},{3,2},{4,3},{5,4},{6,5},{7,6},{8,7},{9,8},{10,9... | collective-permute-start | bytes 688136 | tf_op jit(solution)/shard_map/ppermute | solution.py:33
  54.1 2.0 %collective-permute-done.4 = bf16[112,1024]{1,0:T(8,128)(2,1)S(1)} collective-permute-done((bf16[112,1024]{1,0:T(8,128)(2,1)S(1)}, bf16[112,1024]{1,0:T(8,128)(2,1)S(1)}, u32[]{:S(2)}, u32[]{:S(2)}) %collective-permute-start.4) | collective-permute-done | bytes 229408 | tf_op jit(solution)/shard_map/ppermute | solution.py:30
  56.1 1.9 %collective-permute-start.5 = (bf16[112,1024]{1,0:T(8,128)(2,1)S(1)}, bf16[112,1024]{1,0:T(8,128)(2,1)S(1)}, u32[]{:S(2)}, u32[]{:S(2)}) collective-permute-start(bf16[112,1024]{1,0:T(8,128)(2,1)S(1)} %collective-permute-done.4), channel_id=1, source_target_pairs={{0,1},{1,2},{2,3},{3,4},{4,5},{5,6},{6,7},{7,8},{8,9},{9,10},{10,1... | collective-permute-start | bytes 688136 | tf_op jit(solution)/shard_map/ppermute | solution.py:30
  58.0 0.0 collective-permute-done.11
  58.1 5.1 %collective-permute-start.12 = (bf16[112,1024]{1,0:T(8,128)(2,1)S(1)}, bf16[112,1024]{1,0:T(8,128)(2,1)S(1)}, u32[]{:S(2)}, u32[]{:S(2)}) collective-permute-start(bf16[112,1024]{1,0:T(8,128)(2,1)S(1)} %collective-permute-done.11), channel_id=1, source_target_pairs={{0,15},{1,0},{2,1},{3,2},{4,3},{5,4},{6,5},{7,6},{8,7},{9,8},{10,9... | collective-permute-start | bytes 688136 | tf_op jit(solution)/shard_map/ppermute | solution.py:33
  63.2 2.5 %collective-permute-done.5 = bf16[112,1024]{1,0:T(8,128)(2,1)S(1)} collective-permute-done((bf16[112,1024]{1,0:T(8,128)(2,1)S(1)}, bf16[112,1024]{1,0:T(8,128)(2,1)S(1)}, u32[]{:S(2)}, u32[]{:S(2)}) %collective-permute-start.5) | collective-permute-done | bytes 229408 | tf_op jit(solution)/shard_map/ppermute | solution.py:30
  65.7 1.9 %collective-permute-start.6 = (bf16[112,1024]{1,0:T(8,128)(2,1)S(1)}, bf16[112,1024]{1,0:T(8,128)(2,1)S(1)}, u32[]{:S(2)}, u32[]{:S(2)}) collective-permute-start(bf16[112,1024]{1,0:T(8,128)(2,1)S(1)} %collective-permute-done.5), channel_id=1, source_target_pairs={{0,1},{1,2},{2,3},{3,4},{4,5},{5,6},{6,7},{7,8},{8,9},{9,10},{10,1... | collective-permute-start | bytes 688136 | tf_op jit(solution)/shard_map/ppermute | solution.py:30
  67.6 0.0 collective-permute-done.12
  67.7 5.4 %collective-permute-start.13 = (bf16[112,1024]{1,0:T(8,128)(2,1)S(1)}, bf16[112,1024]{1,0:T(8,128)(2,1)S(1)}, u32[]{:S(2)}, u32[]{:S(2)}) collective-permute-start(bf16[112,1024]{1,0:T(8,128)(2,1)S(1)} %collective-permute-done.12), channel_id=1, source_target_pairs={{0,15},{1,0},{2,1},{3,2},{4,3},{5,4},{6,5},{7,6},{8,7},{9,8},{10,9... | collective-permute-start | bytes 688136 | tf_op jit(solution)/shard_map/ppermute | solution.py:33
  73.1 3.4 %collective-permute-done.6 = bf16[112,1024]{1,0:T(8,128)(2,1)S(1)} collective-permute-done((bf16[112,1024]{1,0:T(8,128)(2,1)S(1)}, bf16[112,1024]{1,0:T(8,128)(2,1)S(1)}, u32[]{:S(2)}, u32[]{:S(2)}) %collective-permute-start.6) | collective-permute-done | bytes 229408 | tf_op jit(solution)/shard_map/ppermute | solution.py:30
  76.5 1.9 %collective-permute-start.15 = (bf16[112,1024]{1,0:T(8,128)(2,1)S(1)}, bf16[112,1024]{1,0:T(8,128)(2,1)S(1)}, u32[]{:S(2)}, u32[]{:S(2)}) collective-permute-start(bf16[112,1024]{1,0:T(8,128)(2,1)S(1)} %collective-permute-done.6), channel_id=1, source_target_pairs={{0,1},{1,2},{2,3},{3,4},{4,5},{5,6},{6,7},{7,8},{8,9},{9,10},{10,1... | collective-permute-start | bytes 688136 | tf_op jit(solution)/shard_map/ppermute | solution.py:30
  78.6 0.0 collective-permute-done.13
  78.7 0.7 fusion.9
  79.4 0.7 broadcast_select_fusion.3
  80.1 5.5 %collective-permute-done.15 = bf16[112,1024]{1,0:T(8,128)(2,1)S(1)} collective-permute-done((bf16[112,1024]{1,0:T(8,128)(2,1)S(1)}, bf16[112,1024]{1,0:T(8,128)(2,1)S(1)}, u32[]{:S(2)}, u32[]{:S(2)}) %collective-permute-start.15) | collective-permute-done | bytes 229408 | tf_op jit(solution)/shard_map/ppermute | solution.py:30
  85.6 0.3 fusion.8
  85.9 9.2 %all-gather = bf16[448,1024]{1,0:T(8,128)(2,1)S(1)} all-gather(bf16[224,1024]{1,0:T(8,128)(2,1)S(1)} %get-tuple-element.15), channel_id=2, replica_groups={{0,16},{1,17},{2,18},{3,19},{4,20},{5,21},{6,22},{7,23},{8,24},{9,25},{..., dimensions={0}, use_global_device_ids=true | all-gather | bytes 1376256 | tf_op jit(solution)/shard_map/all_gather | solution.py:171
  95.1 0.2 fusion.plane_ref
  95.3 0.4 unique_blocks.1
  95.7 19.0 %all_to_all.5 = bf16[4,288,256]{2,1,0:T(8,128)(2,1)S(1)} all-to-all(bf16[4,288,256]{2,1,0:T(8,128)(2,1)S(1)} %bitcast.43), channel_id=1, replica_groups={{0,1,2,3},{4,5,6,7},{8,9,10,11},{12,13,14,15},{16,17,18,19},{20,21,22,2..., dimensions={0} | all-to-all | bytes 1179648 | tf_op jit(solution)/shard_map/all_to_all | solution.py:176
  114.7 0.1 reduce_sum.24
  114.7 25.8 %all-gather.1 = bf16[1152,256]{1,0:T(8,128)(2,1)S(1)} all-gather(bf16[288,256]{1,0:T(8,128)(2,1)S(1)} %reduce_sum.24), channel_id=3, replica_groups={{0,4,8,12},{1,5,9,13},{2,6,10,14},{3,7,11,15},{16,20,24,28},{17,21,25,2..., dimensions={0}, use_global_device_ids=true | all-gather | bytes 737280 | tf_op jit(solution)/shard_map/all_gather | solution.py:180
  140.6 0.1 reduce_sum.25
  140.7 5.3 %all-gather.2 = bf16[384,256]{1,0:T(8,128)(2,1)S(1)} all-gather(bf16[192,256]{1,0:T(8,128)(2,1)S(1)} %slice.49), channel_id=4, replica_groups={{0,16},{1,17},{2,18},{3,19},{4,20},{5,21},{6,22},{7,23},{8,24},{9,25},{..., dimensions={0}, use_global_device_ids=true | all-gather | bytes 294912 | tf_op jit(solution)/shard_map/all_gather | solution.py:185
  146.0 19.1 %all-gather.3 = bf16[1920,256]{1,0:T(8,128)(2,1)S(1)} all-gather(bf16[480,256]{1,0:T(8,128)(2,1)S(1)} %pad_maximum_fusion.1), channel_id=5, replica_groups={{0,1,2,3},{4,5,6,7},{8,9,10,11},{12,13,14,15},{16,17,18,19},{20,21,22,2..., dimensions={0}, use_global_device_ids=true | all-gather | bytes 1228800 | tf_op jit(solution)/shard_map/all_gather | solution.py:189
  165.2 6.3 %all-gather.4 = bf16[8,96,256]{2,1,0:T(8,128)(2,1)S(1)} all-gather(bf16[4,96,256]{2,1,0:T(8,128)(2,1)S(1)} %slice.54), channel_id=6, replica_groups={{0,16},{1,17},{2,18},{3,19},{4,20},{5,21},{6,22},{7,23},{8,24},{9,25},{..., dimensions={0}, use_global_device_ids=true | all-gather | bytes 589824 | tf_op jit(solution)/shard_map/all_gather | solution.py:185
  171.5 0.2 broadcast_select_fusion
  171.8 1.8 %finish.1 = bf16[112,1024]{1,0:T(8,128)(2,1)} custom-call(bf16[1152,256]{1,0:T(8,128)(2,1)S(1)} %bitcast.42, bf16[1152,256]{1,0:T(8,128)(2,1)S(1)} %bitcast.41, bf16[112,1024]{1,0:T(8,128)(2,1)S(1)} %constant_dynamic-slice_fusion.power_ref), custom_call_target="tpu_custom_call" | custom-call | tf_op jit(solution)/shard_map/finish/pallas_call | solution.py:130
  (22 shorter events, 0.5 us)
Async XLA Ops:
  0.0 18.8 %copy-start.1 = (bf16[112,1024]{1,0:T(8,128)(2,1)S(1)}, bf16[112,1024]{1,0:T(8,128)(2,1)}, u32[]{:S(2)}) copy-start(bf16[112,1024]{1,0:T(8,128)(2,1)} %param.3) | copy-start | bytes 688132
  0.0 27.2 %copy-start = (bf16[112,3584]{1,0:T(8,128)(2,1)S(1)}, bf16[112,3584]{1,0:T(8,128)(2,1)}, u32[]{:S(2)}) copy-start(bf16[112,3584]{1,0:T(8,128)(2,1)} %param.2) | copy-start | bytes 2408452
  0.0 18.9 %collective-permute-start = (bf16[112,1024]{1,0:T(8,128)(2,1)}, bf16[112,1024]{1,0:T(8,128)(2,1)S(1)}, u32[]{:S(2)}, u32[]{:S(2)}) collective-permute-start(bf16[112,1024]{1,0:T(8,128)(2,1)} %param.3), channel_id=1, source_target_pairs={{0,1},{1,2},{2,3},{3,4},{4,5},{5,6},{6,7},{7,8},{8,9},{9,10},{10,1... | collective-permute-start | bytes 688136 | tf_op jit(solution)/shard_map/ppermute | solution.py:30
  4.0 16.9 %collective-permute-start.7 = (bf16[112,1024]{1,0:T(8,128)(2,1)}, bf16[112,1024]{1,0:T(8,128)(2,1)S(1)}, u32[]{:S(2)}, u32[]{:S(2)}) collective-permute-start(bf16[112,1024]{1,0:T(8,128)(2,1)} %param.3), channel_id=1, source_target_pairs={{0,15},{1,0},{2,1},{3,2},{4,3},{5,4},{6,5},{7,6},{8,7},{9,8},{10,9... | collective-permute-start | bytes 688136 | tf_op jit(solution)/shard_map/ppermute | solution.py:33
  14.5 12.6 %collective-permute-start.14 = (bf16[112,1792]{1,0:T(8,128)(2,1)S(1)}, bf16[112,1792]{1,0:T(8,128)(2,1)S(1)}, u32[]{:S(2)}, u32[]{:S(2)}) collective-permute-start(bf16[112,1792]{1,0:T(8,128)(2,1)S(1)} %constant_dynamic-slice_fusion.1), channel_id=1, source_target_pairs={{0,16},{1,17},{2,18},{3,19},{4,20},{5,21},{6,22},{7,23},{8,24},{9,... | collective-permute-start | bytes 1204232 | tf_op jit(solution)/shard_map/ppermute | solution.py:151
  18.9 9.9 %collective-permute-start.1 = (bf16[112,1024]{1,0:T(8,128)(2,1)S(1)}, bf16[112,1024]{1,0:T(8,128)(2,1)S(1)}, u32[]{:S(2)}, u32[]{:S(2)}) collective-permute-start(bf16[112,1024]{1,0:T(8,128)(2,1)S(1)} %collective-permute-done), channel_id=1, source_target_pairs={{0,1},{1,2},{2,3},{3,4},{4,5},{5,6},{6,7},{7,8},{8,9},{9,10},{10,1... | collective-permute-start | bytes 688136 | tf_op jit(solution)/shard_map/ppermute | solution.py:30
  20.8 9.9 %collective-permute-start.8 = (bf16[112,1024]{1,0:T(8,128)(2,1)S(1)}, bf16[112,1024]{1,0:T(8,128)(2,1)S(1)}, u32[]{:S(2)}, u32[]{:S(2)}) collective-permute-start(bf16[112,1024]{1,0:T(8,128)(2,1)S(1)} %collective-permute-done.7), channel_id=1, source_target_pairs={{0,15},{1,0},{2,1},{3,2},{4,3},{5,4},{6,5},{7,6},{8,7},{9,8},{10,9... | collective-permute-start | bytes 688136 | tf_op jit(solution)/shard_map/ppermute | solution.py:33
  28.8 9.1 %collective-permute-start.2 = (bf16[112,1024]{1,0:T(8,128)(2,1)S(1)}, bf16[112,1024]{1,0:T(8,128)(2,1)S(1)}, u32[]{:S(2)}, u32[]{:S(2)}) collective-permute-start(bf16[112,1024]{1,0:T(8,128)(2,1)S(1)} %collective-permute-done.1), channel_id=1, source_target_pairs={{0,1},{1,2},{2,3},{3,4},{4,5},{5,6},{6,7},{7,8},{8,9},{9,10},{10,1... | collective-permute-start | bytes 688136 | tf_op jit(solution)/shard_map/ppermute | solution.py:30
  30.7 9.1 %collective-permute-start.9 = (bf16[112,1024]{1,0:T(8,128)(2,1)S(1)}, bf16[112,1024]{1,0:T(8,128)(2,1)S(1)}, u32[]{:S(2)}, u32[]{:S(2)}) collective-permute-start(bf16[112,1024]{1,0:T(8,128)(2,1)S(1)} %collective-permute-done.8), channel_id=1, source_target_pairs={{0,15},{1,0},{2,1},{3,2},{4,3},{5,4},{6,5},{7,6},{8,7},{9,8},{10,9... | collective-permute-start | bytes 688136 | tf_op jit(solution)/shard_map/ppermute | solution.py:33
  37.9 9.1 %collective-permute-start.3 = (bf16[112,1024]{1,0:T(8,128)(2,1)S(1)}, bf16[112,1024]{1,0:T(8,128)(2,1)S(1)}, u32[]{:S(2)}, u32[]{:S(2)}) collective-permute-start(bf16[112,1024]{1,0:T(8,128)(2,1)S(1)} %collective-permute-done.2), channel_id=1, source_target_pairs={{0,1},{1,2},{2,3},{3,4},{4,5},{5,6},{6,7},{7,8},{8,9},{9,10},{10,1... | collective-permute-start | bytes 688136 | tf_op jit(solution)/shard_map/ppermute | solution.py:30
  39.8 9.1 %collective-permute-start.10 = (bf16[112,1024]{1,0:T(8,128)(2,1)S(1)}, bf16[112,1024]{1,0:T(8,128)(2,1)S(1)}, u32[]{:S(2)}, u32[]{:S(2)}) collective-permute-start(bf16[112,1024]{1,0:T(8,128)(2,1)S(1)} %collective-permute-done.9), channel_id=1, source_target_pairs={{0,15},{1,0},{2,1},{3,2},{4,3},{5,4},{6,5},{7,6},{8,7},{9,8},{10,9... | collective-permute-start | bytes 688136 | tf_op jit(solution)/shard_map/ppermute | solution.py:33
  47.0 9.1 %collective-permute-start.4 = (bf16[112,1024]{1,0:T(8,128)(2,1)S(1)}, bf16[112,1024]{1,0:T(8,128)(2,1)S(1)}, u32[]{:S(2)}, u32[]{:S(2)}) collective-permute-start(bf16[112,1024]{1,0:T(8,128)(2,1)S(1)} %collective-permute-done.3), channel_id=1, source_target_pairs={{0,1},{1,2},{2,3},{3,4},{4,5},{5,6},{6,7},{7,8},{8,9},{9,10},{10,1... | collective-permute-start | bytes 688136 | tf_op jit(solution)/shard_map/ppermute | solution.py:30
  48.9 9.1 %collective-permute-start.11 = (bf16[112,1024]{1,0:T(8,128)(2,1)S(1)}, bf16[112,1024]{1,0:T(8,128)(2,1)S(1)}, u32[]{:S(2)}, u32[]{:S(2)}) collective-permute-start(bf16[112,1024]{1,0:T(8,128)(2,1)S(1)} %collective-permute-done.10), channel_id=1, source_target_pairs={{0,15},{1,0},{2,1},{3,2},{4,3},{5,4},{6,5},{7,6},{8,7},{9,8},{10,9... | collective-permute-start | bytes 688136 | tf_op jit(solution)/shard_map/ppermute | solution.py:33
  56.1 9.6 %collective-permute-start.5 = (bf16[112,1024]{1,0:T(8,128)(2,1)S(1)}, bf16[112,1024]{1,0:T(8,128)(2,1)S(1)}, u32[]{:S(2)}, u32[]{:S(2)}) collective-permute-start(bf16[112,1024]{1,0:T(8,128)(2,1)S(1)} %collective-permute-done.4), channel_id=1, source_target_pairs={{0,1},{1,2},{2,3},{3,4},{4,5},{5,6},{6,7},{7,8},{8,9},{9,10},{10,1... | collective-permute-start | bytes 688136 | tf_op jit(solution)/shard_map/ppermute | solution.py:30
  58.1 9.6 %collective-permute-start.12 = (bf16[112,1024]{1,0:T(8,128)(2,1)S(1)}, bf16[112,1024]{1,0:T(8,128)(2,1)S(1)}, u32[]{:S(2)}, u32[]{:S(2)}) collective-permute-start(bf16[112,1024]{1,0:T(8,128)(2,1)S(1)} %collective-permute-done.11), channel_id=1, source_target_pairs={{0,15},{1,0},{2,1},{3,2},{4,3},{5,4},{6,5},{7,6},{8,7},{9,8},{10,9... | collective-permute-start | bytes 688136 | tf_op jit(solution)/shard_map/ppermute | solution.py:33
  65.7 10.8 %collective-permute-start.6 = (bf16[112,1024]{1,0:T(8,128)(2,1)S(1)}, bf16[112,1024]{1,0:T(8,128)(2,1)S(1)}, u32[]{:S(2)}, u32[]{:S(2)}) collective-permute-start(bf16[112,1024]{1,0:T(8,128)(2,1)S(1)} %collective-permute-done.5), channel_id=1, source_target_pairs={{0,1},{1,2},{2,3},{3,4},{4,5},{5,6},{6,7},{7,8},{8,9},{9,10},{10,1... | collective-permute-start | bytes 688136 | tf_op jit(solution)/shard_map/ppermute | solution.py:30
  67.7 11.0 %collective-permute-start.13 = (bf16[112,1024]{1,0:T(8,128)(2,1)S(1)}, bf16[112,1024]{1,0:T(8,128)(2,1)S(1)}, u32[]{:S(2)}, u32[]{:S(2)}) collective-permute-start(bf16[112,1024]{1,0:T(8,128)(2,1)S(1)} %collective-permute-done.12), channel_id=1, source_target_pairs={{0,15},{1,0},{2,1},{3,2},{4,3},{5,4},{6,5},{7,6},{8,7},{9,8},{10,9... | collective-permute-start | bytes 688136 | tf_op jit(solution)/shard_map/ppermute | solution.py:33
  76.5 9.1 %collective-permute-start.15 = (bf16[112,1024]{1,0:T(8,128)(2,1)S(1)}, bf16[112,1024]{1,0:T(8,128)(2,1)S(1)}, u32[]{:S(2)}, u32[]{:S(2)}) collective-permute-start(bf16[112,1024]{1,0:T(8,128)(2,1)S(1)} %collective-permute-done.6), channel_id=1, source_target_pairs={{0,1},{1,2},{2,3},{3,4},{4,5},{5,6},{6,7},{7,8},{8,9},{9,10},{10,1... | collective-permute-start | bytes 688136 | tf_op jit(solution)/shard_map/ppermute | solution.py:30

commit v10 on v9

--- a/solution.py
+++ b/solution.py
@@ -24,14 +24,11 @@
 
 
 def ring(block):
-    up, down = [], []
-    a = b = block
-    for step in range(Z // 2):
-        a = lax.ppermute(a, AXIS, shift(1))
-        up.append(a)
-        if step < Z // 2 - 1:
-            b = lax.ppermute(b, AXIS, shift(-1))
-            down.append(b)
+    up, down = [lax.ppermute(block, AXIS, shift(1))], [lax.ppermute(block, AXIS, shift(-1))]
+    down.append(lax.ppermute(block, AXIS, shift(-2)))
+    for _ in range(Z // 2 - 2):
+        up.append(lax.ppermute(up[-1], AXIS, shift(1)))
+        down.append(lax.ppermute(down[-1], AXIS, shift(-1)))
     return up, down
 
 
@@ -155,19 +152,21 @@
     full = place(full, basis, z)
     for step, part in enumerate(up[:-1]):
         full = place(full, part, z - step - 1 + Z)
-    for step, part in enumerate(down):
+    for step, part in enumerate(down[:-1]):
         full = place(full, part, z + step + 1)
     full = full.reshape(span, columns)
 
     def product(left):
-        last = lax.dynamic_slice_in_dim(left, (z - len(up) + Z) % Z * rows, rows, 1)
+        places = [(z - len(up) + Z) % Z, (z + len(down)) % Z]
+        last = jnp.stack([lax.dynamic_slice_in_dim(left, p * rows, rows, 1) for p in places])
         return jnp.dot(left, full, preferred_element_type=jnp.float32), last
 
     near, near_last = product(own_columns)
     far, far_last = product(far_columns)
     terms = jnp.concatenate([jnp.where(first_row, near, far), jnp.where(first_row, far, near)], 0)
-    lasts = jnp.concatenate([jnp.where(first_row, near_last, far_last), jnp.where(first_row, far_last, near_last)], 0)
-    terms = terms + jnp.dot(lasts, up[-1], preferred_element_type=jnp.float32)
+    lasts = jnp.concatenate([jnp.where(first_row, near_last, far_last), jnp.where(first_row, far_last, near_last)], 1)
+    terms = terms + jnp.dot(lasts[0], up[-1], preferred_element_type=jnp.float32)
+    terms = terms + jnp.dot(lasts[1], down[-1], preferred_element_type=jnp.float32)
     sent = lax.all_gather(terms.astype(jnp.bfloat16), AXIS, axis=0, axis_index_groups=PAIRS)
     plane = (terms + jnp.where(first_row, sent[1], sent[0]).astype(jnp.float32)).astype(jnp.bfloat16)
     power = lax.dynamic_slice_in_dim(plane, y * rows, rows, 0)

time: 174 us -> 185 us (1.063)
  local copies, waits for them, and re-layouts: 1.91 us -> 13.4 us
  waiting for transfers between devices: 20.1 us -> 8.87 us
  starting transfers between devices: 61.4 us -> 66.5 us
  matrix products: 1.7 us -> 5.99 us
    ppermute x15, waiting for transfers between devices: 19 us -> 8.87 us  [the longest x6 5.53 us: ring(): down.append(lax.ppermute(down[-1], AXIS, shift(-1)))]
    dynamic_update_slice x15 -> x14, local copies, waits for them, and re-layouts: 0.34 us -> 9.88 us  [place(): return lax.dynamic_update_slice(full, block[None], (z % Z, 0, 0))]
    ppermute x15, starting transfers between devices: 57.9 us -> 63 us  [the longest x6 32.7 us: ring(): down.append(lax.ppermute(down[-1], AXIS, shift(-1)))]
    all_gather x1, blocking collectives: 25.8 us -> 21.4 us  [body(): parts = lax.all_gather(part, AXIS, axis=0, axis_index_groups=FAR)]
    dot_general x2, matrix products: 1.43 us -> 5.45 us  [product(): return (jnp.dot(left, full, preferred_element_type=jnp.float32), last)]
    all_gather x1, blocking collectives: 19.1 us -> 21.2 us  [body(): gathered = lax.all_gather(part, AXIS, axis=0, axis_index_groups=NEAR)]
  transfers between devices with their start and end apart: 16 -> 16, of which waited for: 8 -> 7; matrix products, arithmetic and copies ran while one was open for 2% -> 10% of each run, Pallas kernels for 0% -> 0%
where the time goes in v10:
time: 185 us; the launch traced here: 184 us
  blocking collectives  85.7 us (46%)
  starting transfers between devices  66.5 us (36%)
  local copies, waits for them, and re-layouts  13.4 us (7%)
  waiting for transfers between devices  8.87 us (5%)
  matrix products  5.99 us (3%)
  Pallas kernels  2.21 us (1%)
    ppermute x6, starting transfers between devices, ring(): down.append(lax.ppermute(down[-1], AXIS, shift(-1)))  32.7 us
    all_gather x1, blocking collectives, body(): parts = lax.all_gather(part, AXIS, axis=0, axis_index_groups=FAR)  21.4 us
    all_gather x1, blocking collectives, body(): gathered = lax.all_gather(part, AXIS, axis=0, axis_index_groups=NEAR)  21.2 us
    all_to_all x1, blocking collectives, body(): lax.all_to_all(blocks.reshape(CUBE, -1, chunk), AXIS, 0, 0, axis_index_gr...  20.5 us
    ppermute x6, starting transfers between devices, ring(): up.append(lax.ppermute(up[-1], AXIS, shift(1)))  12.5 us
    all_gather x2, blocking collectives, trade(): both = lax.all_gather(piece, AXIS, axis=0, axis_index_groups=PAIRS)  11.9 us
    all_gather x1, blocking collectives, body(): lax.all_gather(terms.astype(jnp.bfloat16), AXIS, axis=0, axis_index_group...  10.6 us
    dynamic_update_slice x14, local copies, waits for them, and re-layouts, place(): return lax.dynamic_update_slice(full, block[None], (z % Z, 0, 0))  9.88 us
  transfers between devices with their start and end apart: 16, of which 7 were waited for; matrix products, arithmetic and copies ran while one was open for 10% of the time, Pallas kernels for 0%

profile of v10, /device:TPU:6, one launch (start us, length us, event | category | flops | bytes accessed | tf_op | source)
XLA Modules:
  0.0 183.7 jit_solution(1387684852197898617)
XLA Ops:
  0.0 3.9 %collective-permute-start = (bf16[112,1024]{1,0:T(8,128)(2,1)}, bf16[112,1024]{1,0:T(8,128)(2,1)S(1)}, u32[]{:S(2)}, u32[]{:S(2)}) collective-permute-start(bf16[112,1024]{1,0:T(8,128)(2,1)} %param.3), channel_id=1, source_target_pairs={{0,1},{1,2},{2,3},{3,4},{4,5},{5,6},{6,7},{7,8},{8,9},{9,10},{10,1... | collective-permute-start | bytes 688136 | tf_op jit(solution)/shard_map/ppermute | solution.py:27
  4.0 9.5 %collective-permute-start.6 = (bf16[112,1024]{1,0:T(8,128)(2,1)}, bf16[112,1024]{1,0:T(8,128)(2,1)S(1)}, u32[]{:S(2)}, u32[]{:S(2)}) collective-permute-start(bf16[112,1024]{1,0:T(8,128)(2,1)} %param.3), channel_id=1, source_target_pairs={{0,15},{1,0},{2,1},{3,2},{4,3},{5,4},{6,5},{7,6},{8,7},{9,8},{10,9... | collective-permute-start | bytes 688136 | tf_op jit(solution)/shard_map/ppermute | solution.py:27
  13.5 4.4 %collective-permute-start.7 = (bf16[112,1024]{1,0:T(8,128)(2,1)}, bf16[112,1024]{1,0:T(8,128)(2,1)S(1)}, u32[]{:S(2)}, u32[]{:S(2)}) collective-permute-start(bf16[112,1024]{1,0:T(8,128)(2,1)} %param.3), channel_id=1, source_target_pairs={{0,14},{1,15},{2,0},{3,1},{4,2},{5,3},{6,4},{7,5},{8,6},{9,7},{10,... | collective-permute-start | bytes 688136 | tf_op jit(solution)/shard_map/ppermute | solution.py:28
  17.9 1.0 constant_dynamic-slice_fusion.1
  18.9 3.5 %collective-permute-start.13 = (bf16[112,1792]{1,0:T(8,128)(2,1)S(1)}, bf16[112,1792]{1,0:T(8,128)(2,1)S(1)}, u32[]{:S(2)}, u32[]{:S(2)}) collective-permute-start(bf16[112,1792]{1,0:T(8,128)(2,1)S(1)} %constant_dynamic-slice_fusion.1), channel_id=1, source_target_pairs={{0,16},{1,17},{2,18},{3,19},{4,20},{5,21},{6,22},{7,23},{8,24},{9,... | collective-permute-start | bytes 1204232 | tf_op jit(solution)/shard_map/ppermute | solution.py:148
  22.4 2.3 %broadcast_in_dim.45 = bf16[16,112,1024]{2,1,0:T(8,128)(2,1)} broadcast(bf16[]{:T(256)} %constant.163.clone.1), dimensions={} | broadcast | bytes 3670018 | tf_op jit(solution)/shard_map/broadcast_in_dim | solution.py:151
  24.7 0.7 bitcast_dynamic-update-slice_fusion.13
  25.4 0.1 dynamic-slice_bitcast_fusion.3
  25.5 0.0 collective-permute-done
  25.5 2.9 %collective-permute-start.1 = (bf16[112,1024]{1,0:T(8,128)(2,1)S(1)}, bf16[112,1024]{1,0:T(8,128)(2,1)S(1)}, u32[]{:S(2)}, u32[]{:S(2)}) collective-permute-start(bf16[112,1024]{1,0:T(8,128)(2,1)S(1)} %collective-permute-done), channel_id=1, source_target_pairs={{0,1},{1,2},{2,3},{3,4},{4,5},{5,6},{6,7},{7,8},{8,9},{9,10},{10,1... | collective-permute-start | bytes 688136 | tf_op jit(solution)/shard_map/ppermute | solution.py:30
  28.4 0.1 collective-permute-done.7
  28.5 4.7 %collective-permute-start.8 = (bf16[112,1024]{1,0:T(8,128)(2,1)S(1)}, bf16[112,1024]{1,0:T(8,128)(2,1)S(1)}, u32[]{:S(2)}, u32[]{:S(2)}) collective-permute-start(bf16[112,1024]{1,0:T(8,128)(2,1)S(1)} %collective-permute-done.7), channel_id=1, source_target_pairs={{0,15},{1,0},{2,1},{3,2},{4,3},{5,4},{6,5},{7,6},{8,7},{9,8},{10,9... | collective-permute-start | bytes 688136 | tf_op jit(solution)/shard_map/ppermute | solution.py:31
  33.3 0.7 bitcast_dynamic-update-slice_fusion.12
  34.0 0.0 collective-permute-done.13
  34.0 0.1 dynamic-slice_bitcast_fusion.1
  34.1 0.7 collective-permute-done.1
  34.8 1.9 %collective-permute-start.2 = (bf16[112,1024]{1,0:T(8,128)(2,1)S(1)}, bf16[112,1024]{1,0:T(8,128)(2,1)S(1)}, u32[]{:S(2)}, u32[]{:S(2)}) collective-permute-start(bf16[112,1024]{1,0:T(8,128)(2,1)S(1)} %collective-permute-done.1), channel_id=1, source_target_pairs={{0,1},{1,2},{2,3},{3,4},{4,5},{5,6},{6,7},{7,8},{8,9},{9,10},{10,1... | collective-permute-start | bytes 688136 | tf_op jit(solution)/shard_map/ppermute | solution.py:30
  36.7 0.0 collective-permute-done.8
  36.8 5.6 %collective-permute-start.9 = (bf16[112,1024]{1,0:T(8,128)(2,1)S(1)}, bf16[112,1024]{1,0:T(8,128)(2,1)S(1)}, u32[]{:S(2)}, u32[]{:S(2)}) collective-permute-start(bf16[112,1024]{1,0:T(8,128)(2,1)S(1)} %collective-permute-done.8), channel_id=1, source_target_pairs={{0,15},{1,0},{2,1},{3,2},{4,3},{5,4},{6,5},{7,6},{8,7},{9,8},{10,9... | collective-permute-start | bytes 688136 | tf_op jit(solution)/shard_map/ppermute | solution.py:31
  42.4 0.7 bitcast_dynamic-update-slice_fusion.11
  43.1 0.9 collective-permute-done.2
  43.9 1.9 %collective-permute-start.3 = (bf16[112,1024]{1,0:T(8,128)(2,1)S(1)}, bf16[112,1024]{1,0:T(8,128)(2,1)S(1)}, u32[]{:S(2)}, u32[]{:S(2)}) collective-permute-start(bf16[112,1024]{1,0:T(8,128)(2,1)S(1)} %collective-permute-done.2), channel_id=1, source_target_pairs={{0,1},{1,2},{2,3},{3,4},{4,5},{5,6},{6,7},{7,8},{8,9},{9,10},{10,1... | collective-permute-start | bytes 688136 | tf_op jit(solution)/shard_map/ppermute | solution.py:30
  45.9 0.0 collective-permute-done.9
  45.9 5.6 %collective-permute-start.10 = (bf16[112,1024]{1,0:T(8,128)(2,1)S(1)}, bf16[112,1024]{1,0:T(8,128)(2,1)S(1)}, u32[]{:S(2)}, u32[]{:S(2)}) collective-permute-start(bf16[112,1024]{1,0:T(8,128)(2,1)S(1)} %collective-permute-done.9), channel_id=1, source_target_pairs={{0,15},{1,0},{2,1},{3,2},{4,3},{5,4},{6,5},{7,6},{8,7},{9,8},{10,9... | collective-permute-start | bytes 688136 | tf_op jit(solution)/shard_map/ppermute | solution.py:31
  51.5 0.7 bitcast_dynamic-update-slice_fusion.10
  52.2 0.8 collective-permute-done.3
  53.0 1.9 %collective-permute-start.4 = (bf16[112,1024]{1,0:T(8,128)(2,1)S(1)}, bf16[112,1024]{1,0:T(8,128)(2,1)S(1)}, u32[]{:S(2)}, u32[]{:S(2)}) collective-permute-start(bf16[112,1024]{1,0:T(8,128)(2,1)S(1)} %collective-permute-done.3), channel_id=1, source_target_pairs={{0,1},{1,2},{2,3},{3,4},{4,5},{5,6},{6,7},{7,8},{8,9},{9,10},{10,1... | collective-permute-start | bytes 688136 | tf_op jit(solution)/shard_map/ppermute | solution.py:30
  55.0 0.0 collective-permute-done.10
  55.0 5.6 %collective-permute-start.11 = (bf16[112,1024]{1,0:T(8,128)(2,1)S(1)}, bf16[112,1024]{1,0:T(8,128)(2,1)S(1)}, u32[]{:S(2)}, u32[]{:S(2)}) collective-permute-start(bf16[112,1024]{1,0:T(8,128)(2,1)S(1)} %collective-permute-done.10), channel_id=1, source_target_pairs={{0,15},{1,0},{2,1},{3,2},{4,3},{5,4},{6,5},{7,6},{8,7},{9,8},{10,9... | collective-permute-start | bytes 688136 | tf_op jit(solution)/shard_map/ppermute | solution.py:31
  60.6 0.7 bitcast_dynamic-update-slice_fusion.9
  61.3 0.8 collective-permute-done.4
  62.2 1.9 %collective-permute-start.5 = (bf16[112,1024]{1,0:T(8,128)(2,1)S(1)}, bf16[112,1024]{1,0:T(8,128)(2,1)S(1)}, u32[]{:S(2)}, u32[]{:S(2)}) collective-permute-start(bf16[112,1024]{1,0:T(8,128)(2,1)S(1)} %collective-permute-done.4), channel_id=1, source_target_pairs={{0,1},{1,2},{2,3},{3,4},{4,5},{5,6},{6,7},{7,8},{8,9},{9,10},{10,1... | collective-permute-start | bytes 688136 | tf_op jit(solution)/shard_map/ppermute | solution.py:30
  64.1 0.7 collective-permute-done.11
  64.8 5.6 %collective-permute-start.12 = (bf16[112,1024]{1,0:T(8,128)(2,1)S(1)}, bf16[112,1024]{1,0:T(8,128)(2,1)S(1)}, u32[]{:S(2)}, u32[]{:S(2)}) collective-permute-start(bf16[112,1024]{1,0:T(8,128)(2,1)S(1)} %collective-permute-done.11), channel_id=1, source_target_pairs={{0,15},{1,0},{2,1},{3,2},{4,3},{5,4},{6,5},{7,6},{8,7},{9,8},{10,9... | collective-permute-start | bytes 688136 | tf_op jit(solution)/shard_map/ppermute | solution.py:31
  70.4 0.7 bitcast_dynamic-update-slice_fusion.8
  71.1 4.7 %collective-permute-done.12 = bf16[112,1024]{1,0:T(8,128)(2,1)S(1)} collective-permute-done((bf16[112,1024]{1,0:T(8,128)(2,1)S(1)}, bf16[112,1024]{1,0:T(8,128)(2,1)S(1)}, u32[]{:S(2)}, u32[]{:S(2)}) %collective-permute-start.12) | collective-permute-done | bytes 229408 | tf_op jit(solution)/shard_map/ppermute | solution.py:31
  75.8 5.6 %collective-permute-start.15 = (bf16[112,1024]{1,0:T(8,128)(2,1)S(1)}, bf16[112,1024]{1,0:T(8,128)(2,1)S(1)}, u32[]{:S(2)}, u32[]{:S(2)}) collective-permute-start(bf16[112,1024]{1,0:T(8,128)(2,1)S(1)} %collective-permute-done.12), channel_id=1, source_target_pairs={{0,15},{1,0},{2,1},{3,2},{4,3},{5,4},{6,5},{7,6},{8,7},{9,8},{10,9... | collective-permute-start | bytes 688136 | tf_op jit(solution)/shard_map/ppermute | solution.py:31
  81.4 0.0 collective-permute-done.5
  81.4 1.9 %collective-permute-start.14 = (bf16[112,1024]{1,0:T(8,128)(2,1)S(1)}, bf16[112,1024]{1,0:T(8,128)(2,1)S(1)}, u32[]{:S(2)}, u32[]{:S(2)}) collective-permute-start(bf16[112,1024]{1,0:T(8,128)(2,1)S(1)} %collective-permute-done.5), channel_id=1, source_target_pairs={{0,1},{1,2},{2,3},{3,4},{4,5},{5,6},{6,7},{7,8},{8,9},{9,10},{10,1... | collective-permute-start | bytes 688136 | tf_op jit(solution)/shard_map/ppermute | solution.py:30
  83.3 0.7 bitcast_dynamic-update-slice_fusion.7
  84.0 0.0 collective-permute-done.6
  84.0 0.7 bitcast_dynamic-update-slice_fusion.6
  84.7 0.7 bitcast_dynamic-update-slice_fusion.5
  85.4 0.7 bitcast_dynamic-update-slice_fusion.4
  86.1 0.7 bitcast_dynamic-update-slice_fusion.3
  86.9 0.7 bitcast_dynamic-update-slice_fusion.2
  87.6 0.7 bitcast_dynamic-update-slice_fusion.1
  88.3 0.7 bitcast_dynamic-update-slice_fusion
  89.0 2.7 %fusion.15 = f32[112,1024]{1,0:T(8,128)S(1)} fusion(bf16[112,1792]{1,0:T(8,128)(2,1)S(1)} %collective-permute-done.13, bf16[1792,1024]{1,0:T(8,128)(2,1)} %bitcast.15), kind=kOutput, calls=%fused_computation.51 | convolution fusion | flops 411041792 | bytes 4530176 | tf_op jit(solution)/shard_map/dot_general | solution.py:162
  91.7 2.7 %broadcast_select_fusion.3 = (f32[112,1024]{1,0:T(8,128)S(1)}, f32[112,1024]{1,0:T(8,128)S(1)}) fusion(f32[112,1024]{1,0:T(8,128)S(1)} %fusion.15, pred[]{:T(512)S(6)} %eq.23, bf16[1792,1024]{1,0:T(8,128)(2,1)} %bitcast.15, bf16[112,3584]{1,0:T(8,128)(2,1)S(1)} %copy-done, s32[]{:T(128)S(6)} %select_n.218), kind=kOutput, calls=%fused_computation.26 | convolution fusion | flops 411271168 | bytes 5447685 | tf_op jit(solution)/shard_map/dot_general | solution.py:162
  94.4 0.3 fusion.8
  94.7 0.3 fusion.14
  95.0 10.6 %all-gather = bf16[448,1024]{1,0:T(8,128)(2,1)S(1)} all-gather(bf16[224,1024]{1,0:T(8,128)(2,1)S(1)} %get-tuple-element.19), channel_id=2, replica_groups={{0,16},{1,17},{2,18},{3,19},{4,20},{5,21},{6,22},{7,23},{8,24},{9,25},{..., dimensions={0}, use_global_device_ids=true | all-gather | bytes 1376256 | tf_op jit(solution)/shard_map/all_gather | solution.py:170
  105.6 0.2 fusion.1.plane_ref
  105.8 0.4 unique_blocks.1
  106.3 20.5 %all_to_all.5 = bf16[4,288,256]{2,1,0:T(8,128)(2,1)S(1)} all-to-all(bf16[4,288,256]{2,1,0:T(8,128)(2,1)S(1)} %bitcast.58), channel_id=1, replica_groups={{0,1,2,3},{4,5,6,7},{8,9,10,11},{12,13,14,15},{16,17,18,19},{20,21,22,2..., dimensions={0} | all-to-all | bytes 1179648 | tf_op jit(solution)/shard_map/all_to_all | solution.py:175
  126.7 0.1 reduce_sum.24
  126.8 21.4 %all-gather.1 = bf16[1152,256]{1,0:T(8,128)(2,1)S(1)} all-gather(bf16[288,256]{1,0:T(8,128)(2,1)S(1)} %reduce_sum.24), channel_id=3, replica_groups={{0,4,8,12},{1,5,9,13},{2,6,10,14},{3,7,11,15},{16,20,24,28},{17,21,25,2..., dimensions={0}, use_global_device_ids=true | all-gather | bytes 737280 | tf_op jit(solution)/shard_map/all_gather | solution.py:179
  148.3 0.1 reduce_sum.25
  148.4 5.6 %all-gather.2 = bf16[384,256]{1,0:T(8,128)(2,1)S(1)} all-gather(bf16[192,256]{1,0:T(8,128)(2,1)S(1)} %slice.59), channel_id=4, replica_groups={{0,16},{1,17},{2,18},{3,19},{4,20},{5,21},{6,22},{7,23},{8,24},{9,25},{..., dimensions={0}, use_global_device_ids=true | all-gather | bytes 294912 | tf_op jit(solution)/shard_map/all_gather | solution.py:184
  154.0 21.2 %all-gather.3 = bf16[1920,256]{1,0:T(8,128)(2,1)S(1)} all-gather(bf16[480,256]{1,0:T(8,128)(2,1)S(1)} %pad_maximum_fusion.1), channel_id=5, replica_groups={{0,1,2,3},{4,5,6,7},{8,9,10,11},{12,13,14,15},{16,17,18,19},{20,21,22,2..., dimensions={0}, use_global_device_ids=true | all-gather | bytes 1228800 | tf_op jit(solution)/shard_map/all_gather | solution.py:188
  175.2 6.3 %all-gather.4 = bf16[8,96,256]{2,1,0:T(8,128)(2,1)S(1)} all-gather(bf16[4,96,256]{2,1,0:T(8,128)(2,1)S(1)} %slice.64), channel_id=6, replica_groups={{0,16},{1,17},{2,18},{3,19},{4,20},{5,21},{6,22},{7,23},{8,24},{9,25},{..., dimensions={0}, use_global_device_ids=true | all-gather | bytes 589824 | tf_op jit(solution)/shard_map/all_gather | solution.py:184
  181.6 0.2 broadcast_select_fusion
  181.8 1.8 finish.1
  (14 shorter events, 0.2 us)
Async XLA Ops:
  0.0 24.7 %copy-start.1 = (bf16[112,1024]{1,0:T(8,128)(2,1)S(1)}, bf16[112,1024]{1,0:T(8,128)(2,1)}, u32[]{:S(2)}) copy-start(bf16[112,1024]{1,0:T(8,128)(2,1)} %param.3) | copy-start | bytes 688132
  0.0 25.4 %copy-start = (bf16[112,3584]{1,0:T(8,128)(2,1)S(1)}, bf16[112,3584]{1,0:T(8,128)(2,1)}, u32[]{:S(2)}) copy-start(bf16[112,3584]{1,0:T(8,128)(2,1)} %param.2) | copy-start | bytes 2408452
  0.0 25.5 %collective-permute-start = (bf16[112,1024]{1,0:T(8,128)(2,1)}, bf16[112,1024]{1,0:T(8,128)(2,1)S(1)}, u32[]{:S(2)}, u32[]{:S(2)}) collective-permute-start(bf16[112,1024]{1,0:T(8,128)(2,1)} %param.3), channel_id=1, source_target_pairs={{0,1},{1,2},{2,3},{3,4},{4,5},{5,6},{6,7},{7,8},{8,9},{9,10},{10,1... | collective-permute-start | bytes 688136 | tf_op jit(solution)/shard_map/ppermute | solution.py:27
  4.0 80.1 %collective-permute-start.6 = (bf16[112,1024]{1,0:T(8,128)(2,1)}, bf16[112,1024]{1,0:T(8,128)(2,1)S(1)}, u32[]{:S(2)}, u32[]{:S(2)}) collective-permute-start(bf16[112,1024]{1,0:T(8,128)(2,1)} %param.3), channel_id=1, source_target_pairs={{0,15},{1,0},{2,1},{3,2},{4,3},{5,4},{6,5},{7,6},{8,7},{9,8},{10,9... | collective-permute-start | bytes 688136 | tf_op jit(solution)/shard_map/ppermute | solution.py:27
  13.5 15.0 %collective-permute-start.7 = (bf16[112,1024]{1,0:T(8,128)(2,1)}, bf16[112,1024]{1,0:T(8,128)(2,1)S(1)}, u32[]{:S(2)}, u32[]{:S(2)}) collective-permute-start(bf16[112,1024]{1,0:T(8,128)(2,1)} %param.3), channel_id=1, source_target_pairs={{0,14},{1,15},{2,0},{3,1},{4,2},{5,3},{6,4},{7,5},{8,6},{9,7},{10,... | collective-permute-start | bytes 688136 | tf_op jit(solution)/shard_map/ppermute | solution.py:28
  18.9 15.1 %collective-permute-start.13 = (bf16[112,1792]{1,0:T(8,128)(2,1)S(1)}, bf16[112,1792]{1,0:T(8,128)(2,1)S(1)}, u32[]{:S(2)}, u32[]{:S(2)}) collective-permute-start(bf16[112,1792]{1,0:T(8,128)(2,1)S(1)} %constant_dynamic-slice_fusion.1), channel_id=1, source_target_pairs={{0,16},{1,17},{2,18},{3,19},{4,20},{5,21},{6,22},{7,23},{8,24},{9,... | collective-permute-start | bytes 1204232 | tf_op jit(solution)/shard_map/ppermute | solution.py:148
  25.5 9.3 %collective-permute-start.1 = (bf16[112,1024]{1,0:T(8,128)(2,1)S(1)}, bf16[112,1024]{1,0:T(8,128)(2,1)S(1)}, u32[]{:S(2)}, u32[]{:S(2)}) collective-permute-start(bf16[112,1024]{1,0:T(8,128)(2,1)S(1)} %collective-permute-done), channel_id=1, source_target_pairs={{0,1},{1,2},{2,3},{3,4},{4,5},{5,6},{6,7},{7,8},{8,9},{9,10},{10,1... | collective-permute-start | bytes 688136 | tf_op jit(solution)/shard_map/ppermute | solution.py:30
  28.5 8.3 %collective-permute-start.8 = (bf16[112,1024]{1,0:T(8,128)(2,1)S(1)}, bf16[112,1024]{1,0:T(8,128)(2,1)S(1)}, u32[]{:S(2)}, u32[]{:S(2)}) collective-permute-start(bf16[112,1024]{1,0:T(8,128)(2,1)S(1)} %collective-permute-done.7), channel_id=1, source_target_pairs={{0,15},{1,0},{2,1},{3,2},{4,3},{5,4},{6,5},{7,6},{8,7},{9,8},{10,9... | collective-permute-start | bytes 688136 | tf_op jit(solution)/shard_map/ppermute | solution.py:31
  34.8 9.1 %collective-permute-start.2 = (bf16[112,1024]{1,0:T(8,128)(2,1)S(1)}, bf16[112,1024]{1,0:T(8,128)(2,1)S(1)}, u32[]{:S(2)}, u32[]{:S(2)}) collective-permute-start(bf16[112,1024]{1,0:T(8,128)(2,1)S(1)} %collective-permute-done.1), channel_id=1, source_target_pairs={{0,1},{1,2},{2,3},{3,4},{4,5},{5,6},{6,7},{7,8},{8,9},{9,10},{10,1... | collective-permute-start | bytes 688136 | tf_op jit(solution)/shard_map/ppermute | solution.py:30
  36.8 9.1 %collective-permute-start.9 = (bf16[112,1024]{1,0:T(8,128)(2,1)S(1)}, bf16[112,1024]{1,0:T(8,128)(2,1)S(1)}, u32[]{:S(2)}, u32[]{:S(2)}) collective-permute-start(bf16[112,1024]{1,0:T(8,128)(2,1)S(1)} %collective-permute-done.8), channel_id=1, source_target_pairs={{0,15},{1,0},{2,1},{3,2},{4,3},{5,4},{6,5},{7,6},{8,7},{9,8},{10,9... | collective-permute-start | bytes 688136 | tf_op jit(solution)/shard_map/ppermute | solution.py:31
  43.9 9.1 %collective-permute-start.3 = (bf16[112,1024]{1,0:T(8,128)(2,1)S(1)}, bf16[112,1024]{1,0:T(8,128)(2,1)S(1)}, u32[]{:S(2)}, u32[]{:S(2)}) collective-permute-start(bf16[112,1024]{1,0:T(8,128)(2,1)S(1)} %collective-permute-done.2), channel_id=1, source_target_pairs={{0,1},{1,2},{2,3},{3,4},{4,5},{5,6},{6,7},{7,8},{8,9},{9,10},{10,1... | collective-permute-start | bytes 688136 | tf_op jit(solution)/shard_map/ppermute | solution.py:30
  45.9 9.1 %collective-permute-start.10 = (bf16[112,1024]{1,0:T(8,128)(2,1)S(1)}, bf16[112,1024]{1,0:T(8,128)(2,1)S(1)}, u32[]{:S(2)}, u32[]{:S(2)}) collective-permute-start(bf16[112,1024]{1,0:T(8,128)(2,1)S(1)} %collective-permute-done.9), channel_id=1, source_target_pairs={{0,15},{1,0},{2,1},{3,2},{4,3},{5,4},{6,5},{7,6},{8,7},{9,8},{10,9... | collective-permute-start | bytes 688136 | tf_op jit(solution)/shard_map/ppermute | solution.py:31
  53.0 9.1 %collective-permute-start.4 = (bf16[112,1024]{1,0:T(8,128)(2,1)S(1)}, bf16[112,1024]{1,0:T(8,128)(2,1)S(1)}, u32[]{:S(2)}, u32[]{:S(2)}) collective-permute-start(bf16[112,1024]{1,0:T(8,128)(2,1)S(1)} %collective-permute-done.3), channel_id=1, source_target_pairs={{0,1},{1,2},{2,3},{3,4},{4,5},{5,6},{6,7},{7,8},{8,9},{9,10},{10,1... | collective-permute-start | bytes 688136 | tf_op jit(solution)/shard_map/ppermute | solution.py:30
  55.0 9.8 %collective-permute-start.11 = (bf16[112,1024]{1,0:T(8,128)(2,1)S(1)}, bf16[112,1024]{1,0:T(8,128)(2,1)S(1)}, u32[]{:S(2)}, u32[]{:S(2)}) collective-permute-start(bf16[112,1024]{1,0:T(8,128)(2,1)S(1)} %collective-permute-done.10), channel_id=1, source_target_pairs={{0,15},{1,0},{2,1},{3,2},{4,3},{5,4},{6,5},{7,6},{8,7},{9,8},{10,9... | collective-permute-start | bytes 688136 | tf_op jit(solution)/shard_map/ppermute | solution.py:31
  62.2 19.2 %collective-permute-start.5 = (bf16[112,1024]{1,0:T(8,128)(2,1)S(1)}, bf16[112,1024]{1,0:T(8,128)(2,1)S(1)}, u32[]{:S(2)}, u32[]{:S(2)}) collective-permute-start(bf16[112,1024]{1,0:T(8,128)(2,1)S(1)} %collective-permute-done.4), channel_id=1, source_target_pairs={{0,1},{1,2},{2,3},{3,4},{4,5},{5,6},{6,7},{7,8},{8,9},{9,10},{10,1... | collective-permute-start | bytes 688136 | tf_op jit(solution)/shard_map/ppermute | solution.py:30
  64.8 11.0 %collective-permute-start.12 = (bf16[112,1024]{1,0:T(8,128)(2,1)S(1)}, bf16[112,1024]{1,0:T(8,128)(2,1)S(1)}, u32[]{:S(2)}, u32[]{:S(2)}) collective-permute-start(bf16[112,1024]{1,0:T(8,128)(2,1)S(1)} %collective-permute-done.11), channel_id=1, source_target_pairs={{0,15},{1,0},{2,1},{3,2},{4,3},{5,4},{6,5},{7,6},{8,7},{9,8},{10,9... | collective-permute-start | bytes 688136 | tf_op jit(solution)/shard_map/ppermute | solution.py:31
  75.8 18.6 %collective-permute-start.15 = (bf16[112,1024]{1,0:T(8,128)(2,1)S(1)}, bf16[112,1024]{1,0:T(8,128)(2,1)S(1)}, u32[]{:S(2)}, u32[]{:S(2)}) collective-permute-start(bf16[112,1024]{1,0:T(8,128)(2,1)S(1)} %collective-permute-done.12), channel_id=1, source_target_pairs={{0,15},{1,0},{2,1},{3,2},{4,3},{5,4},{6,5},{7,6},{8,7},{9,8},{10,9... | collective-permute-start | bytes 688136 | tf_op jit(solution)/shard_map/ppermute | solution.py:31
  81.4 13.3 %collective-permute-start.14 = (bf16[112,1024]{1,0:T(8,128)(2,1)S(1)}, bf16[112,1024]{1,0:T(8,128)(2,1)S(1)}, u32[]{:S(2)}, u32[]{:S(2)}) collective-permute-start(bf16[112,1024]{1,0:T(8,128)(2,1)S(1)} %collective-permute-done.5), channel_id=1, source_target_pairs={{0,1},{1,2},{2,3},{3,4},{4,5},{5,6},{6,7},{7,8},{8,9},{9,10},{10,1... | collective-permute-start | bytes 688136 | tf_op jit(solution)/shard_map/ppermute | solution.py:30
